TPU v7x, 512 devices: a whole 4x4x16 slice. The times are simulated.
512 devices in a mesh: section: 16 (over z), seq: 32 (over y, x, core).
Axes of the slice: x: 4, y: 4, z: 16, core: 2. Of those that a mesh axis runs over, the one named last changes fastest.
Arguments:
- in_flight: bfloat16 [16, 2, 64, 4096], P('section', None, 'seq'), may hold values from -64 to 64
- entering: bfloat16 [3, 2, 64, 4096], P(None, None, 'seq'), may hold values from -64 to 64
- patch_frames: int32 [4], replicated, may hold values from 1 to 2, 6 in all
- norm_gain: bfloat16 [16, 4096], P('section'), may hold values from 0.5 to 1.5
- qkv_weight: bfloat16 [16, 4096, 3, 4096], P('section', None, None, 'seq'), may hold values from -0.15625 to 0.15625
- out_weight: bfloat16 [16, 4096, 4096], P('section', None, 'seq'), may hold values from -0.1875 to 0.1875
- stale_kv: bfloat16 [16, 4, 2, 64, 2, 4096], P('section', None, None, None, None, 'seq'), may hold values from -256 to 256
Outputs:
- hidden_out: bfloat16 [16, 4, 2, 64, 4096], P('section', None, None, 'seq')
Inputs may be any that keep to these rules, and one draw needn't show every extreme that they name: `patch_frames`: the frames of the patches sum to 6 and the largest is exactly 2; frame slots past a patch's count in in_flight, entering and stale_kv are ignored.
All inputs are finite; a program needn't handle non-finite values.
Results may differ from a plain program's by a relative error of at most 0.039.
Values may be sent and summed in bfloat16 or wider, within the bound.
No kernel may reach another device: no remote copies, remote signals or barrier semaphores. Data moves between devices by JAX's collectives and lax.ppermute only.
A program may use at most 64 MiB of HBM per device.

v0:
```python
import math

import jax
import jax.numpy as jnp
from jax import lax
from jax.sharding import PartitionSpec as P

HDIM = 128


def from_behind(value, axis, steps):
    count = lax.axis_size(axis)
    initial, last = (max(0, -steps), min(count, count - steps))
    return lax.ppermute(value, axis, [(source, source + steps) for source in range(initial, last)])


def attend(projected, patch_slot, buffer, key_live):
    frames, all_tokens, three, own_width = projected.shape
    heads_here = own_width // HDIM
    queries = projected[:, :, 0, :].reshape(frames * all_tokens, heads_here, HDIM)
    new_slot = projected[:, :, 1:3, :]
    anchor = jnp.zeros((), jnp.int32)
    buffer = lax.dynamic_update_slice(
        buffer, new_slot[None], (patch_slot, anchor, anchor, anchor, anchor)
    )
    keys_all = buffer[:, :, :, 0, :].reshape(-1, heads_here, HDIM)
    values_all = buffer[:, :, :, 1, :].reshape(-1, heads_here, HDIM)
    scores = jnp.einsum(
        "qhd,khd->hqk", queries, keys_all, preferred_element_type=jnp.float32
    ) / math.sqrt(HDIM)
    scores = jnp.where(key_live[None, None, :], scores, -jnp.inf)
    row_max = jnp.max(scores, axis=2, keepdims=True)
    exponent = jnp.exp(scores - row_max)
    row_total = jnp.sum(exponent, axis=2, keepdims=True)
    weights_low = exponent.astype(jnp.bfloat16)
    attended = jnp.einsum(
        "hqk,khd->qhd", weights_low, values_all, preferred_element_type=jnp.float32
    )
    attended = (attended / jnp.transpose(row_total, (1, 0, 2))).astype(jnp.bfloat16)
    return (attended.reshape(frames, all_tokens, own_width), buffer)


def mix_heads(attended, out_cols):
    total = jnp.einsum(
        "ftd,de->fte",
        lax.all_gather(attended, "seq", axis=2, tiled=True),
        out_cols,
        preferred_element_type=jnp.float32,
    )
    return total.astype(jnp.bfloat16)


def pass_on(value):
    return from_behind(value, "section", 1)


def on_device(in_flight, entering, patch_frames, norm_gain, qkv_weight, out_weight, stale_kv):
    section_index = lax.axis_index("section")
    patches = stale_kv.shape[1]
    frames = stale_kv.shape[2]
    all_tokens = stale_kv.shape[3]
    local_tokens = in_flight.shape[2]
    model_width = in_flight.shape[3]
    frame_ids = jnp.arange(frames, dtype=jnp.int32)
    live_table = frame_ids[None, :] < patch_frames[:, None]
    key_live = jnp.broadcast_to(live_table[:, :, None], (patches, frames, all_tokens)).reshape(-1)
    weights_in = qkv_weight[0]
    out_cols = out_weight[0]
    buffer = stale_kv[0]
    gain_row = norm_gain[0]
    anchor = jnp.zeros((), jnp.int32)
    outputs = jnp.zeros((patches, frames, local_tokens, model_width), jnp.bfloat16)
    received = None
    gain_wide = gain_row.astype(jnp.float32)
    for tick_index in range(patches):
        patch_slot = jnp.mod(tick_index - section_index, patches)
        live_rows = live_table[patch_slot]
        if tick_index == 0:
            arrived = in_flight[0]
        else:
            arrived = jnp.where(section_index == 0, entering[tick_index - 1], received)
        hidden = jnp.where(live_rows[:, None, None], arrived, jnp.zeros_like(arrived))
        widened = hidden.astype(jnp.float32)
        mean_square = jnp.mean(widened * widened, axis=-1, keepdims=True)
        normed = (widened * lax.rsqrt(mean_square + 1e-06) * gain_wide).astype(jnp.bfloat16)
        projected = jnp.einsum(
            "ftd,dce->ftce",
            lax.all_gather(normed, "seq", axis=1, tiled=True),
            weights_in,
            preferred_element_type=jnp.float32,
        ).astype(jnp.bfloat16)
        attended, buffer = attend(projected, patch_slot, buffer, key_live)
        branch_own = mix_heads(attended, out_cols)
        branch = lax.all_to_all(branch_own, "seq", split_axis=1, concat_axis=2, tiled=True)
        result = jnp.where(
            live_rows[:, None, None], widened + branch.astype(jnp.float32), 0.0
        ).astype(jnp.bfloat16)
        outputs = lax.dynamic_update_slice(
            outputs, result[None], (patch_slot, anchor, anchor, anchor)
        )
        if tick_index + 1 < patches:
            received = pass_on(result)
    return outputs[None]


def solution(mesh):
    in_specs = (
        P("section", None, "seq", None),
        P(None, None, "seq", None),
        P(),
        P("section", None),
        P("section", None, None, "seq"),
        P("section", None, "seq"),
        P("section", None, None, None, None, "seq"),
    )
    out_specs = P("section", None, None, "seq", None)
    return jax.shard_map(
        on_device, mesh=mesh, in_specs=in_specs, out_specs=out_specs, check_vma=False
    )
```

profile of v0, /device:TPU:1, one launch (start us, length us, event | category | flops | bytes accessed | tf_op | source)
XLA Modules:
  0.0 590.2 jit_solution(11270576672401567618)
XLA Ops:
  6.5 0.9 iota_compare_fusion
  8.0 1.0 fusion.56
  9.0 0.7 convert_element_type.232
  10.5 1.0 copy.101
  11.7 62.8 %all-gather.9.cloned.1.call-done = bf16[2,64,4096]{2,0,1:T(2,128)(2,1)} async-done(((bf16[2,2,4096]{2,0,1:T(2,128)(2,1)}), bf16[2,64,4096]{2,0,1:T(2,128)(2,1)}) %all-gather.9.cloned.1.call-update) | async-done | bytes 1048592 | tf_op jit(solution)/shard_map/all_gather | solution.py:88
  74.5 2.3 fusion.12
  77.3 0.9 fusion.25
  78.3 57.8 %all-gather.11.cloned.1.call-done = bf16[2,64,4096]{2,1,0:T(8,128)(2,1)} async-done(((bf16[2,64,128]{2,1,0:T(8,128)(2,1)}), bf16[2,64,4096]{2,1,0:T(8,128)(2,1)}) %all-gather.11.cloned.1.call-update) | async-done | bytes 1048592 | tf_op jit(solution)/shard_map/all_gather | solution.py:46
  136.1 2.0 convolution_convert_fusion.3
  138.1 12.3 %all_to_all.16 = bf16[2,64,128]{2,0,1:T(2,128)(2,1)S(1)} all-to-all(bf16[2,64,128]{2,0,1:T(2,128)(2,1)S(1)} %copy.29), channel_id=1, replica_groups=mesh['section'=16,'seq'=32] {'seq'}, dimensions={1} | all-to-all | bytes 65536 | tf_op jit(solution)/shard_map/all_to_all | solution.py:94
  151.0 0.9 reshape.261
  151.9 1.3 fusion.60
  153.2 3.2 collective-permute-start
  156.4 1.5 fusion.85
  157.9 0.8 fusion.61
  158.7 0.7 fusion.63
  159.5 58.7 %all-gather.13.cloned.1.call-done = bf16[2,64,4096]{2,0,1:T(2,128)(2,1)} async-done(((bf16[2,2,4096]{2,0,1:T(2,128)(2,1)}), bf16[2,64,4096]{2,0,1:T(2,128)(2,1)}) %all-gather.13.cloned.1.call-update) | async-done | bytes 1048592 | tf_op jit(solution)/shard_map/all_gather | solution.py:88
  218.2 2.3 fusion.15
  221.1 0.9 fusion.27
  222.0 57.8 %all-gather.15.cloned.1.call-done = bf16[2,64,4096]{2,1,0:T(8,128)(2,1)} async-done(((bf16[2,64,128]{2,1,0:T(8,128)(2,1)}), bf16[2,64,4096]{2,1,0:T(8,128)(2,1)}) %all-gather.15.cloned.1.call-update) | async-done | bytes 1048592 | tf_op jit(solution)/shard_map/all_gather | solution.py:46
  279.8 2.0 convolution_convert_fusion.2
  281.8 12.3 %all_to_all.17 = bf16[2,64,128]{2,0,1:T(2,128)(2,1)S(1)} all-to-all(bf16[2,64,128]{2,0,1:T(2,128)(2,1)S(1)} %copy.35), channel_id=1, replica_groups=mesh['section'=16,'seq'=32] {'seq'}, dimensions={1} | all-to-all | bytes 65536 | tf_op jit(solution)/shard_map/all_to_all | solution.py:94
  294.8 0.9 reshape.262
  296.4 3.2 collective-permute-start.1
  299.6 1.0 collective-permute-done.1
  300.6 1.0 fusion.66
  301.5 0.7 fusion.68
  302.3 59.0 %all-gather.17.cloned.1.call-done = bf16[2,64,4096]{2,0,1:T(2,128)(2,1)} async-done(((bf16[2,2,4096]{2,0,1:T(2,128)(2,1)}), bf16[2,64,4096]{2,0,1:T(2,128)(2,1)}) %all-gather.17.cloned.1.call-update) | async-done | bytes 1048592 | tf_op jit(solution)/shard_map/all_gather | solution.py:88
  361.3 2.3 fusion.18
  364.2 0.9 fusion.29
  365.1 57.8 %all-gather.19.cloned.1.call-done = bf16[2,64,4096]{2,1,0:T(8,128)(2,1)} async-done(((bf16[2,64,128]{2,1,0:T(8,128)(2,1)}), bf16[2,64,4096]{2,1,0:T(8,128)(2,1)}) %all-gather.19.cloned.1.call-update) | async-done | bytes 1048592 | tf_op jit(solution)/shard_map/all_gather | solution.py:46
  422.9 2.0 convolution_convert_fusion.1
  424.9 12.3 %all_to_all.18 = bf16[2,64,128]{2,0,1:T(2,128)(2,1)S(1)} all-to-all(bf16[2,64,128]{2,0,1:T(2,128)(2,1)S(1)} %copy.41), channel_id=1, replica_groups=mesh['section'=16,'seq'=32] {'seq'}, dimensions={1} | all-to-all | bytes 65536 | tf_op jit(solution)/shard_map/all_to_all | solution.py:94
  437.9 0.9 reshape.263
  438.7 0.8 fusion.70
  439.5 3.2 collective-permute-start.2
  442.7 1.0 collective-permute-done.2
  443.7 1.0 fusion.71
  445.5 59.0 %all-gather.21.cloned.1.call-done = bf16[2,64,4096]{2,0,1:T(2,128)(2,1)} async-done(((bf16[2,2,4096]{2,0,1:T(2,128)(2,1)}), bf16[2,64,4096]{2,0,1:T(2,128)(2,1)}) %all-gather.21.cloned.1.call-update) | async-done | bytes 1048592 | tf_op jit(solution)/shard_map/all_gather | solution.py:88
  504.4 2.3 fusion.21
  506.9 0.9 fusion.89
  508.0 0.9 fusion.31
  509.2 57.5 %all-gather.23.cloned.1.call-done = bf16[2,64,4096]{2,1,0:T(8,128)(2,1)} async-done(((bf16[2,64,128]{2,1,0:T(8,128)(2,1)}), bf16[2,64,4096]{2,1,0:T(8,128)(2,1)}) %all-gather.23.cloned.1.call-update) | async-done | bytes 1048592 | tf_op jit(solution)/shard_map/all_gather | solution.py:46
  566.7 2.0 convolution_convert_fusion
  569.3 5.3 all-to-all-start.3
  574.6 0.8 copy_dynamic-update-slice_fusion.5
  575.4 6.4 %all-to-all-done.3 = bf16[2,64,128]{2,0,1:T(2,128)(2,1)S(1)} async-done(((bf16[2,64,128]{2,0,1:T(2,128)(2,1)}), bf16[2,64,128]{2,0,1:T(2,128)(2,1)S(1)}, u32[]{:S(2)}, u32[]{:S(2)}) %all-to-all-start.3) | async-done | bytes 32800 | tf_op jit(solution)/shard_map/all_to_all | solution.py:94
  581.9 0.8 fusion.76
  (83 shorter events, 8.8 us)
Async XLA Ops:
  6.5 67.9 %copy-start = (bf16[1,4096,3,128]{3,1,2,0:T(8,128)(2,1)S(1)}, bf16[1,4096,3,128]{3,1,2,0:T(8,128)(2,1)}, u32[]{:S(2)}) copy-start(bf16[1,4096,3,128]{3,1,2,0:T(8,128)(2,1)} %param.11) | copy-start | bytes 9437188
  6.5 67.9 %all-gather.9.cloned.1.call-start = ((), (), s32[]{:S(2)}) async-start(), calls=%async_computation.4 | async-start | bytes 1081344 | tf_op jit(solution)/shard_map/all_gather | solution.py:88
  8.0 66.4 %copy-start.9 = (pred[2]{0:T(512)(128)(4,1)}, pred[2]{0:T(512)(128)(4,1)S(1)}, u32[]{:S(2)}) copy-start(pred[2]{0:T(512)(128)(4,1)S(1)} %get-tuple-element.27) | copy-start | bytes 10
  10.5 125.6 %all-gather.11.cloned.1.call-start = ((), (), s32[]{:S(2)}) async-start(), calls=%async_computation.5 | async-start | bytes 1081344 | tf_op jit(solution)/shard_map/all_gather | solution.py:46
  11.7 65.5 %copy-start.6 = (pred[512]{0:T(512)(128)(4,1)}, pred[512]{0:T(512)(128)(4,1)S(1)}, u32[]{:S(2)}) copy-start(pred[512]{0:T(512)(128)(4,1)S(1)} %broadcast_in_dim.137) | copy-start | bytes 1540
  78.2 140.0 %all-gather.13.cloned.1.call-start = ((), (), s32[]{:S(2)}) async-start(), calls=%async_computation.6 | async-start | bytes 1081344 | tf_op jit(solution)/shard_map/all_gather | solution.py:88
  153.2 4.7 collective-permute-start
  158.7 61.9 %copy-start.7 = (pred[512]{0:T(512)(128)(4,1)S(1)}, pred[512]{0:T(512)(128)(4,1)}, u32[]{:S(2)}) copy-start(pred[512]{0:T(512)(128)(4,1)} %copy-done.6) | copy-start | bytes 1540
  159.5 120.4 %all-gather.15.cloned.1.call-start = ((), (), s32[]{:S(2)}) async-start(), calls=%async_computation.7 | async-start | bytes 1081344 | tf_op jit(solution)/shard_map/all_gather | solution.py:46
  222.0 139.3 %all-gather.17.cloned.1.call-start = ((), (), s32[]{:S(2)}) async-start(), calls=%async_computation.8 | async-start | bytes 1081344 | tf_op jit(solution)/shard_map/all_gather | solution.py:88
  296.4 4.2 copy-start.3
  296.4 4.2 collective-permute-start.1
  301.5 62.2 %copy-start.8 = (pred[512]{0:T(512)(128)(4,1)S(1)}, pred[512]{0:T(512)(128)(4,1)}, u32[]{:S(2)}) copy-start(pred[512]{0:T(512)(128)(4,1)} %copy-done.6) | copy-start | bytes 1540
  302.3 120.6 %all-gather.19.cloned.1.call-start = ((), (), s32[]{:S(2)}) async-start(), calls=%async_computation.9 | async-start | bytes 1081344 | tf_op jit(solution)/shard_map/all_gather | solution.py:46
  365.1 139.4 %all-gather.21.cloned.1.call-start = ((), (), s32[]{:S(2)}) async-start(), calls=%async_computation.10 | async-start | bytes 1081344 | tf_op jit(solution)/shard_map/all_gather | solution.py:88
  439.5 4.2 copy-start.5
  439.5 4.2 collective-permute-start.2
  445.4 121.3 %all-gather.23.cloned.1.call-start = ((), (), s32[]{:S(2)}) async-start(), calls=%async_computation.11 | async-start | bytes 1081344 | tf_op jit(solution)/shard_map/all_gather | solution.py:46
  504.4 4.6 copy-start.2
  504.4 4.6 copy-start.10
  504.4 4.7 copy-start.4
  569.3 12.5 %all-to-all-start.3 = ((bf16[2,64,128]{2,0,1:T(2,128)(2,1)}), bf16[2,64,128]{2,0,1:T(2,128)(2,1)S(1)}, u32[]{:S(2)}, u32[]{:S(2)}) async-start(bf16[2,64,128]{2,0,1:T(2,128)(2,1)} %copy.47), calls=%async_computation.3 | async-start | bytes 65536 | tf_op jit(solution)/shard_map/all_to_all | solution.py:94
  575.4 7.3 %copy-start.1 = (bf16[1,4,2,2,4096]{4,3,2,1,0:T(2,128)(2,1)}, bf16[1,4,2,2,4096]{4,3,2,1,0:T(2,128)(2,1)S(1)}, u32[]{:S(2)}) copy-start(bf16[1,4,2,2,4096]{4,3,2,1,0:T(2,128)(2,1)S(1)} %copy_dynamic-update-slice_fusion.5) | copy-start | bytes 393220
Sparse Core Ops, SparseCore 0:
  10.6 63.8 all-gather.8
  78.3 57.6 all-gather.10
  159.6 58.5 all-gather.12
  222.1 57.6 all-gather.14
  302.4 58.8 all-gather.16
  365.2 57.6 all-gather.18
  445.5 58.8 all-gather.20
  509.0 57.6 all-gather.22
where the time goes:
time: 591 us; the launch traced here: 590 us
  waiting for transfers between devices  479 us (81%)
  blocking collectives  36.9 us (6%)
  matrix products  22.4 us (4%)
  starting transfers between devices  15.1 us (3%)
  between operations  13.9 us (2%)
  other arithmetic  12.7 us (2%)
  local copies, waits for them, and re-layouts  10.4 us (2%)
    all_gather x4, waiting for transfers between devices, on_device(): lax.all_gather(normed, 'seq', axis=1, tiled=True)  239 us
    all_gather x4, waiting for transfers between devices, mix_heads(): lax.all_gather(attended, 'seq', axis=2, tiled=True)  231 us
    all_to_all x3, blocking collectives, on_device(): lax.all_to_all(branch_own, 'seq', split_axis=1, concat_axis=2, tiled=True)  36.9 us
  transfers between devices with their start and end apart: 12, of which 11 were waited for; matrix products, arithmetic and copies ran while one was open for 1% of the time, Pallas kernels for 0%

commit v1 on v0

v1 whole, which is shorter than its diff:
```python
import functools
import math

import jax
import jax.numpy as jnp
from jax import lax
from jax.experimental import pallas as pl
from jax.experimental.pallas import tpu as pltpu
from jax.sharding import PartitionSpec as P

HDIM = 128
CORES = 2
SPARE = 16
VMEM_LIMIT = 12 * 1024 * 1024


def call(body, name, out_shape, scalars, arrays, scratch=()):
    in_vmem = pl.BlockSpec(memory_space=pltpu.VMEM)
    in_smem = pl.BlockSpec(memory_space=pltpu.SMEM)
    return pl.pallas_call(
        body,
        out_shape=out_shape,
        in_specs=[in_smem] * len(scalars) + [in_vmem] * len(arrays),
        out_specs=jax.tree.map(lambda _: in_vmem, out_shape),
        scratch_shapes=list(scratch),
        compiler_params=pltpu.CompilerParams(vmem_limit_bytes=VMEM_LIMIT),
        name=name,
    )(*scalars, *arrays)


def shape(*dims):
    return jax.ShapeDtypeStruct(dims, jnp.bfloat16)


def join_weights(w_ref, out_ref):
    kinds, _, width = w_ref.shape
    for kind in range(kinds):
        out_ref[:, kind * width:(kind + 1) * width] = w_ref[kind]


def pack_first(mine_ref, later_ref, out_ref):
    rows = mine_ref.shape[0]
    for target in range(out_ref.shape[0]):
        out_ref[target, :rows] = mine_ref[...]
        out_ref[target, rows:] = later_ref[target]


def unpack_first(local, came_ref, hidden_ref, fresh_ref, wide_ref):
    group, rows, _ = came_ref.shape
    chips, frames, halves = hidden_ref.shape[:3]
    blocks = chips * halves
    for source in range(group):
        wide_ref[source * rows:(source + 1) * rows] = came_ref[source].astype(jnp.float32)

    def over_sources(row):
        return wide_ref[pl.ds(row, group, stride=rows), :].astype(jnp.bfloat16)

    for frame in range(frames):
        for t in range(local):
            for block in range(blocks):
                hidden_ref[block // halves, frame, block % halves, t * group:(t + 1) * group] = over_sources(
                    (frame * local + t) * blocks + block
                )
    for tick in range(fresh_ref.shape[0]):
        for t in range(local):
            for half in range(halves):
                fresh_ref[tick, half, t * group:(t + 1) * group] = over_sources(
                    frames * local * blocks + (tick * local + t) * halves + half
                )


def layer_front(info_ref, x_ref, gain_ref, w_ref, k_ref, v_ref, out_ref, k_out, v_out, xn_ref):
    chips, frames, halves, tokens, width = x_ref.shape
    slots = k_ref.shape[0]
    rows = frames * tokens
    slot = info_ref[slots]
    count = info_ref[slot]
    for frame in range(frames):
        squares = jnp.zeros((tokens, width), jnp.float32)
        for chip in range(chips):
            for half in range(halves):
                wide = x_ref[chip, frame, half].astype(jnp.float32)
                squares = squares + wide * wide
        mean_square = jnp.sum(squares, axis=1, keepdims=True) / (chips * halves * width)
        scale = jnp.where(frame < count, lax.rsqrt(mean_square + 1e-06), 0.0)
        for chip in range(chips):
            for half in range(halves):
                first = (chip * halves + half) * width
                wide = x_ref[chip, frame, half].astype(jnp.float32)
                normed = wide * scale * gain_ref[:, first:first + width].astype(jnp.float32)
                xn_ref[frame * tokens:(frame + 1) * tokens, first:first + width] = normed.astype(jnp.bfloat16)
    projected = jnp.dot(xn_ref[...], w_ref[...], preferred_element_type=jnp.float32).astype(jnp.bfloat16)
    queries = projected[:, :width]
    k_out[...] = k_ref[...]
    v_out[...] = v_ref[...]
    k_out[slot] = projected[:, width:2 * width]
    v_out[slot] = projected[:, 2 * width:]
    keys = k_out[...].reshape(slots * rows, width)
    values = v_out[...].reshape(slots * rows, width)
    scores = lax.dot_general(
        queries, keys, (((1,), (1,)), ((), ())), preferred_element_type=jnp.float32
    ) / math.sqrt(HDIM)
    key_ids = lax.broadcasted_iota(jnp.int32, (1, slots * rows), 1)
    key_slot = key_ids // rows
    limit = jnp.zeros_like(key_ids)
    for patch in range(slots):
        limit = jnp.where(key_slot == patch, info_ref[patch] * tokens, limit)
    scores = jnp.where(key_ids - key_slot * rows < limit, scores, -jnp.inf)
    exponent = jnp.exp(scores - jnp.max(scores, axis=1, keepdims=True))
    row_total = jnp.sum(exponent, axis=1, keepdims=True)
    attended = jnp.dot(exponent.astype(jnp.bfloat16), values, preferred_element_type=jnp.float32)
    attended = (attended / row_total).astype(jnp.bfloat16)
    for chip in range(chips):
        for frame in range(frames):
            out_ref[chip, frame] = attended[frame * tokens:(frame + 1) * tokens]


def layer_back(info_ref, a_ref, w_own_ref, w_other_ref, x_ref, out_ref, wide_ref):
    blocks, tokens, width = a_ref.shape
    slots = info_ref.shape[0] - 2
    me = info_ref[slots + 1]
    chip = lax.div(me, CORES)
    core = me - chip * CORES
    live = core < info_ref[info_ref[slots]]
    for block in range(blocks):
        wide_ref[:, block * width:(block + 1) * width] = a_ref[block]
    for half, w_ref in ((core, w_own_ref), (1 - core, w_other_ref)):
        branch = jnp.dot(wide_ref[...], w_ref[...], preferred_element_type=jnp.float32).astype(jnp.bfloat16)
        total = x_ref[chip, core, half].astype(jnp.float32) + branch.astype(jnp.float32)
        out_ref[half] = jnp.where(live, total, 0.0).astype(jnp.bfloat16)


def pack_last(*refs):
    *result_refs, out_ref, wide_ref = refs
    group, parts, _ = out_ref.shape
    each = parts // len(result_refs) * group
    for tick, ref in enumerate(result_refs):
        halves, tokens, width = ref.shape
        wide_ref[tick * each:(tick + 1) * each] = ref[...].astype(jnp.float32).reshape(halves * tokens, width)
    for target in range(group):
        out_ref[target] = wide_ref[pl.ds(target, parts, stride=group), :].astype(jnp.bfloat16)


def unpack_last(local, slots_ref, came_ref, out_ref, wide_ref, turn_ref):
    group, parts, _ = came_ref.shape
    patches = slots_ref.shape[0]
    chips = group // CORES
    for source in range(group):
        wide_ref[source * parts:(source + 1) * parts] = came_ref[source].astype(jnp.float32)
    for tick in range(patches):
        slot = slots_ref[tick]
        for frame in range(CORES):
            for t in range(local):
                for half in range(CORES):
                    part = (tick * CORES + half) * local + t
                    turn_ref[pl.ds(half, chips, stride=CORES), :] = wide_ref[
                        pl.ds(frame * parts + part, chips, stride=CORES * parts), :
                    ]
                out_ref[(slot * CORES + frame) * local + t] = turn_ref[...].astype(jnp.bfloat16)


def swap(value):
    return lax.all_to_all(value, "seq", split_axis=0, concat_axis=0, tiled=True)


def on_device(in_flight, entering, patch_frames, norm_gain, qkv_weight, out_weight, stale_kv):
    section = lax.axis_index("section")
    sections = lax.axis_size("section")
    me = lax.axis_index("seq")
    group = lax.axis_size("seq")
    patches, frames, tokens = stale_kv.shape[1:4]
    local = in_flight.shape[2]
    ticks = patches
    chips = group // CORES
    halves = CORES
    owned = frames * local * group
    hidden_dims = (chips, frames, halves, tokens, HDIM)
    w_own = out_weight[0]
    w_other = lax.ppermute(w_own, "seq", [(device, device ^ 1) for device in range(group)])
    keys = stale_kv[0, :, :, :, 0, :].reshape(patches, frames * tokens, HDIM)
    values = stale_kv[0, :, :, :, 1, :].reshape(patches, frames * tokens, HDIM)
    weights = call(
        join_weights, "join", shape(qkv_weight.shape[1], 3 * HDIM), (), (jnp.transpose(qkv_weight[0], (1, 0, 2)),)
    )

    mine = in_flight.reshape(owned, HDIM)
    later = entering.reshape(ticks - 1, frames, local, chips, halves, HDIM)
    later = jnp.transpose(later, (3, 1, 0, 2, 4, 5)).reshape(group, -1, HDIM)
    later = jnp.pad(later, ((0, 0), (0, SPARE - later.shape[1]), (0, 0)))
    came = swap(call(pack_first, "pack_first", shape(group, owned + SPARE, HDIM), (), (mine, later)))
    gathered, fresh = call(
        functools.partial(unpack_first, local),
        "unpack_first",
        (shape(*hidden_dims), shape(ticks - 1, halves, tokens, HDIM)),
        (),
        (came,),
        [pltpu.VMEM((group * (owned + SPARE), HDIM), jnp.float32)],
    )

    slots = jnp.mod(jnp.arange(ticks, dtype=jnp.int32) - section, patches).astype(jnp.int32)
    results = []
    for tick in range(ticks):
        info = jnp.concatenate([patch_frames, slots[tick:tick + 1], me.astype(jnp.int32).reshape(1)])
        if tick:
            arrived = lax.ppermute(
                results[-1], "section", [(source, source + 1) for source in range(sections - 1)]
            )
            arrived = jnp.where(section == 0, fresh[tick - 1], arrived)
            gathered = swap(jnp.broadcast_to(arrived[None], (group,) + arrived.shape)).reshape(hidden_dims)
        attended, keys, values = call(
            layer_front,
            "front",
            (shape(chips, frames, tokens, HDIM), shape(*keys.shape), shape(*values.shape)),
            (info,),
            (gathered, norm_gain, weights, keys, values),
            [pltpu.VMEM((frames * tokens, group * HDIM), jnp.bfloat16)],
        )
        attended = swap(attended.reshape(group, tokens, HDIM))
        results.append(
            call(
                layer_back,
                "back",
                shape(halves, tokens, HDIM),
                (info,),
                (attended, w_own, w_other, gathered),
                [pltpu.VMEM((tokens, group * HDIM), jnp.bfloat16)],
            )
        )

    parts = ticks * halves * local
    sent = call(
        pack_last,
        "pack_last",
        shape(group, parts, HDIM),
        (),
        tuple(results),
        [pltpu.VMEM((ticks * halves * tokens, HDIM), jnp.float32)],
    )
    outputs = call(
        functools.partial(unpack_last, local),
        "unpack_last",
        shape(patches * frames * local, group, HDIM),
        (slots,),
        (swap(sent),),
        [pltpu.VMEM((group * parts, HDIM), jnp.float32), pltpu.VMEM((group, HDIM), jnp.float32)],
    )
    return outputs.reshape(1, patches, frames, local, group * HDIM)


def solution(mesh):
    in_specs = (
        P("section", None, "seq", None),
        P(None, None, "seq", None),
        P(),
        P("section", None),
        P("section", None, None, "seq"),
        P("section", None, "seq"),
        P("section", None, None, None, None, "seq"),
    )
    out_specs = P("section", None, None, "seq", None)
    return jax.shard_map(
        on_device, mesh=mesh, in_specs=in_specs, out_specs=out_specs, check_vma=False
    )
```

time: 591 us -> 218 us (0.37)
  the two profiles are of different devices: /device:TPU:1 before, /device:TPU:385 now
where the time goes in v1:
time: 218 us; the launch traced here: 217 us
  blocking collectives  101 us (46%)
  waiting for transfers between devices  47.1 us (22%)
  starting transfers between devices  28.3 us (13%)
  Pallas kernels  21.5 us (10%)
  local copies, waits for them, and re-layouts  13.5 us (6%)
  other arithmetic  5.96 us (3%)
    all_to_all x6, blocking collectives, swap(): return lax.all_to_all(value, 'seq', split_axis=0, concat_axis=0, tiled=True)  101 us
    all_to_all x3, waiting for transfers between devices, swap(): return lax.all_to_all(value, 'seq', split_axis=0, concat_axis=0, tiled=True)  35.9 us
    pallas_call x13, Pallas kernels, call(): pl.pallas_call(body, out_shape=out_shape, in_specs=[in_smem] * len(scalar...  21.5 us
    all_to_all x3, starting transfers between devices, swap(): return lax.all_to_all(value, 'seq', split_axis=0, concat_axis=0, tiled=True)  19.6 us
    ppermute x3, waiting for transfers between devices, on_device(): lax.ppermute(results[-1], 'section', [(source, source + 1) for source in...  11.2 us
    unnamed x40, local copies, waits for them, and re-layouts  8 us
    ppermute x3, starting transfers between devices, on_device(): lax.ppermute(results[-1], 'section', [(source, source + 1) for source in...  6.48 us
    concatenate x2, other arithmetic, on_device(): jnp.concatenate([patch_frames, slots[tick:tick + 1], me.astype(jnp.int32)...  4.41 us
  transfers between devices with their start and end apart: 7, of which 6 were waited for; matrix products, arithmetic and copies ran while one was open for 3% of the time, Pallas kernels for 2%

profile of v1, /device:TPU:385, one launch (start us, length us, event | category | flops | bytes accessed | tf_op | source)
XLA Modules:
  0.0 217.2 jit_solution(602829577667062697)
XLA Ops:
  0.0 0.8 reshape.43.mine_ref
  0.8 1.0 reshape.44
  2.0 1.2 pack_first.1
  3.2 7.8 %all-to-all-start = ((bf16[32,144,128]{2,1,0:T(8,128)(2,1)}), bf16[32,144,128]{2,1,0:T(8,128)(2,1)}, u32[]{:S(2)}, u32[]{:S(2)}) async-start(bf16[32,144,128]{2,1,0:T(8,128)(2,1)} %pack_first.1), calls=%async_computation | async-start | bytes 2359296 | tf_op jit(solution)/shard_map/all_to_all | solution.py:163
  11.0 2.2 %collective-permute-start = (bf16[4096,128]{1,0:T(8,128)(2,1)}, bf16[4096,128]{1,0:T(8,128)(2,1)}, u32[]{:S(2)}, u32[]{:S(2)}) collective-permute-start(bf16[4096,128]{1,0:T(8,128)(2,1)} %bitcast.8.w_own_ref), channel_id=1, source_target_pairs={{0,1},{1,0},{2,3},{3,2},{4,5},{5,4},{6,7},{7,6},{8,9},{9,8},{10,11... | collective-permute-start | bytes 3145736 | tf_op jit(solution)/shard_map/ppermute | solution.py:179
  13.8 1.9 copy-done.2
  16.2 0.7 fusion.2
  16.9 0.6 copy-done.9
  17.5 1.2 add_add_fusion.info_ref
  18.7 10.1 %all-to-all-done.came_ref = bf16[32,144,128]{2,1,0:T(8,128)(2,1)} async-done(((bf16[32,144,128]{2,1,0:T(8,128)(2,1)}), bf16[32,144,128]{2,1,0:T(8,128)(2,1)}, u32[]{:S(2)}, u32[]{:S(2)}) %all-to-all-start) | async-done | bytes 1179680 | tf_op jit(solution)/shard_map/all_to_all | solution.py:163
  28.7 2.0 unpack_first.1
  30.8 0.6 copy-done.11
  31.4 1.8 front.4
  33.2 1.0 copy-done
  34.2 0.8 copy-done.3
  35.0 0.7 copy-done.5
  35.6 5.9 %all-to-all-start.1 = ((bf16[32,64,128]{2,1,0:T(8,128)(2,1)}), bf16[32,64,128]{2,1,0:T(8,128)(2,1)}, u32[]{:S(2)}, u32[]{:S(2)}) async-start(bf16[32,64,128]{2,1,0:T(8,128)(2,1)} %bitcast.30), calls=%async_computation.1 | async-start | bytes 1048576 | tf_op jit(solution)/shard_map/all_to_all | solution.py:163
  41.6 11.7 %all-to-all-done.1.a_ref = bf16[32,64,128]{2,1,0:T(8,128)(2,1)} async-done(((bf16[32,64,128]{2,1,0:T(8,128)(2,1)}), bf16[32,64,128]{2,1,0:T(8,128)(2,1)}, u32[]{:S(2)}, u32[]{:S(2)}) %all-to-all-start.1) | async-done | bytes 524320 | tf_op jit(solution)/shard_map/all_to_all | solution.py:163
  53.3 1.2 copy-done.1
  54.5 0.6 copy-done.12
  55.1 2.2 %back.4.refs_0_ = bf16[2,64,128]{2,1,0:T(8,128)(2,1)S(1)} custom-call(s32[6]{0:T(128)S(1)} %copy-done.12, bf16[32,64,128]{2,1,0:T(8,128)(2,1)} %all-to-all-done.1.a_ref, bf16[4096,128]{1,0:T(8,128)(2,1)} %bitcast.8.w_own_ref, bf16[4096,128]{1,0:T(8,128)(2,1)} %collective-permute-done.w_other_ref, bf16[16,2,2,64,128]{4,3,2,1,0:T(8,128)(2,1)S(1)} %copy-done.1), custom_call_target="tpu_custom_call" | custom-call | tf_op jit(solution)/shard_map/back/pallas_call | solution.py:20
  57.3 2.6 %collective-permute-start.1 = (bf16[2,64,128]{2,1,0:T(8,128)(2,1)S(1)}, bf16[2,64,128]{2,1,0:T(8,128)(2,1)}, u32[]{:S(2)}, u32[]{:S(2)}) collective-permute-start(bf16[2,64,128]{2,1,0:T(8,128)(2,1)S(1)} %back.4.refs_0_), channel_id=1, source_target_pairs={{0,32},{32,64},{64,96},{96,128},{128,160},{160,192},{192,224},{224... | collective-permute-start | bytes 98312 | tf_op jit(solution)/shard_map/ppermute | solution.py:205
  59.9 3.3 %collective-permute-done.1 = bf16[2,64,128]{2,1,0:T(8,128)(2,1)} collective-permute-done((bf16[2,64,128]{2,1,0:T(8,128)(2,1)S(1)}, bf16[2,64,128]{2,1,0:T(8,128)(2,1)}, u32[]{:S(2)}, u32[]{:S(2)}) %collective-permute-start.1) | collective-permute-done | bytes 32800 | tf_op jit(solution)/shard_map/ppermute | solution.py:205
  63.3 0.8 bitcast_select_fusion.2
  64.0 1.2 broadcast_in_dim.6
  65.2 5.8 %all-to-all-start.2 = ((bf16[32,2,64,128]{3,2,1,0:T(8,128)(2,1)}), bf16[32,2,64,128]{3,2,1,0:T(8,128)(2,1)}, u32[]{:S(2)}, u32[]{:S(2)}) async-start(bf16[32,2,64,128]{3,2,1,0:T(8,128)(2,1)} %broadcast_in_dim.6), calls=%async_computation.2 | async-start | bytes 2097152 | tf_op jit(solution)/shard_map/all_to_all | solution.py:163
  71.1 3.2 %add_add_fusion.3 = (s32[6]{0:T(128)}, s32[6]{0:T(128)}, s32[6]{0:T(128)}) fusion(s32[1]{0:T(128)} %get-tuple-element.34, s32[1]{0:T(128)} %bitcast, s32[4]{0:T(128)} %param.9, s32[1]{0:T(128)} %get-tuple-element.36, s32[1]{0:T(128)} %get-tuple-element.35), kind=kLoop, calls=%fused_computation.10 | loop fusion | flops 36 | bytes 104 | tf_op jit(solution)/shard_map/concatenate | solution.py:203
  74.3 14.1 %all-to-all-done.2 = bf16[32,2,64,128]{3,2,1,0:T(8,128)(2,1)} async-done(((bf16[32,2,64,128]{3,2,1,0:T(8,128)(2,1)}), bf16[32,2,64,128]{3,2,1,0:T(8,128)(2,1)}, u32[]{:S(2)}, u32[]{:S(2)}) %all-to-all-start.2) | async-done | bytes 1048608 | tf_op jit(solution)/shard_map/all_to_all | solution.py:163
  88.4 0.7 copy-done.15
  89.1 2.5 %front.5 = (bf16[16,2,64,128]{3,2,1,0:T(8,128)(2,1)S(1)}, bf16[4,128,128]{2,1,0:T(8,128)(2,1)S(1)}, bf16[4,128,128]{2,1,0:T(8,128)(2,1)S(1)}) custom-call(s32[6]{0:T(128)S(1)} %copy-done.15, bf16[16,2,2,64,128]{4,3,2,1,0:T(8,128)(2,1)} %bitcast.10.x_ref, bf16[1,4096]{1,0:T(2,128)(2,1)S(1)} %copy-done.4, bf16[4096,384]{1,0:T(8,128)(2,1)S(1)} %join.1.w_ref, ...), custom_call_target="tpu_custom_call" | custom-call | tf_op jit(solution)/shard_map/front/pallas_call | solution.py:20
  91.6 15.0 %all_to_all.45.a_ref = bf16[32,64,128]{2,1,0:T(8,128)(2,1)S(1)} all-to-all(bf16[32,64,128]{2,1,0:T(8,128)(2,1)S(1)} %bitcast.32), channel_id=1, replica_groups=mesh['section'=16,'seq'=32] {'seq'}, dimensions={0} | all-to-all | bytes 1048576 | tf_op jit(solution)/shard_map/all_to_all | solution.py:163
  106.6 2.4 %back.5.refs_1_ = bf16[2,64,128]{2,1,0:T(8,128)(2,1)S(1)} custom-call(s32[6]{0:T(128)S(1)} %copy-done.16, bf16[32,64,128]{2,1,0:T(8,128)(2,1)S(1)} %all_to_all.45.a_ref, bf16[4096,128]{1,0:T(8,128)(2,1)} %bitcast.8.w_own_ref, bf16[4096,128]{1,0:T(8,128)(2,1)} %collective-permute-done.w_other_ref, bf16[16,2,2,64,128]{4,3,2,1,0:T(8,128)(2,1)} %bitcast.10.x_ref), custom_call_target="tpu_custom_call" | custom-call | tf_op jit(solution)/shard_map/back/pallas_call | solution.py:20
  109.0 1.9 collective-permute-start.2
  110.9 3.9 %collective-permute-done.2 = bf16[2,64,128]{2,1,0:T(8,128)(2,1)S(1)} collective-permute-done((bf16[2,64,128]{2,1,0:T(8,128)(2,1)S(1)}, bf16[2,64,128]{2,1,0:T(8,128)(2,1)S(1)}, u32[]{:S(2)}, u32[]{:S(2)}) %collective-permute-start.2) | collective-permute-done | bytes 32800 | tf_op jit(solution)/shard_map/ppermute | solution.py:205
  115.1 22.0 %all_to_all.46 = bf16[32,2,64,128]{3,2,1,0:T(8,128)(2,1)S(1)} all-to-all(bf16[32,2,64,128]{3,2,1,0:T(8,128)(2,1)S(1)} %broadcast_in_dim.7), channel_id=1, replica_groups=mesh['section'=16,'seq'=32] {'seq'}, dimensions={0} | all-to-all | bytes 2097152 | tf_op jit(solution)/shard_map/all_to_all | solution.py:163
  137.1 1.8 front.6
  138.9 15.1 %all_to_all.47.a_ref = bf16[32,64,128]{2,1,0:T(8,128)(2,1)S(1)} all-to-all(bf16[32,64,128]{2,1,0:T(8,128)(2,1)S(1)} %bitcast.33), channel_id=1, replica_groups=mesh['section'=16,'seq'=32] {'seq'}, dimensions={0} | all-to-all | bytes 1048576 | tf_op jit(solution)/shard_map/all_to_all | solution.py:163
  154.0 2.1 back.6.refs_2_
  156.1 1.9 collective-permute-start.3
  158.0 3.9 %collective-permute-done.3 = bf16[2,64,128]{2,1,0:T(8,128)(2,1)S(1)} collective-permute-done((bf16[2,64,128]{2,1,0:T(8,128)(2,1)S(1)}, bf16[2,64,128]{2,1,0:T(8,128)(2,1)S(1)}, u32[]{:S(2)}, u32[]{:S(2)}) %collective-permute-start.3) | collective-permute-done | bytes 32800 | tf_op jit(solution)/shard_map/ppermute | solution.py:205
  161.9 0.8 bitcast_select_fusion
  163.0 22.0 %all_to_all.48 = bf16[32,2,64,128]{3,2,1,0:T(8,128)(2,1)S(1)} all-to-all(bf16[32,2,64,128]{3,2,1,0:T(8,128)(2,1)S(1)} %broadcast_in_dim.8), channel_id=1, replica_groups=mesh['section'=16,'seq'=32] {'seq'}, dimensions={0} | all-to-all | bytes 2097152 | tf_op jit(solution)/shard_map/all_to_all | solution.py:163
  185.0 2.1 front.7
  187.0 15.2 %all_to_all.49.a_ref = bf16[32,64,128]{2,1,0:T(8,128)(2,1)S(1)} all-to-all(bf16[32,64,128]{2,1,0:T(8,128)(2,1)S(1)} %bitcast.31), channel_id=1, replica_groups=mesh['section'=16,'seq'=32] {'seq'}, dimensions={0} | all-to-all | bytes 1048576 | tf_op jit(solution)/shard_map/all_to_all | solution.py:163
  202.2 2.1 back.7.refs_3_
  204.4 11.3 %all_to_all.50.came_ref = bf16[32,16,128]{2,1,0:T(8,128)(2,1)S(1)} all-to-all(bf16[32,16,128]{2,1,0:T(8,128)(2,1)S(1)} %pack_last.1), channel_id=1, replica_groups=mesh['section'=16,'seq'=32] {'seq'}, dimensions={0} | all-to-all | bytes 262144 | tf_op jit(solution)/shard_map/all_to_all | solution.py:163
  215.7 0.8 unpack_last.1
  216.5 0.7 reshape.53
  (42 shorter events, 2.0 us)
Async XLA Ops:
  0.0 13.2 %copy-start.17 = (bf16[1,4,2,64,2,128]{5,4,3,2,1,0:T(2,128)(2,1)S(1)}, bf16[1,4,2,64,2,128]{5,4,3,2,1,0:T(2,128)(2,1)}, u32[]{:S(2)}) copy-start(bf16[1,4,2,64,2,128]{5,4,3,2,1,0:T(2,128)(2,1)} %param.13) | copy-start | bytes 786436
  3.2 25.6 %all-to-all-start = ((bf16[32,144,128]{2,1,0:T(8,128)(2,1)}), bf16[32,144,128]{2,1,0:T(8,128)(2,1)}, u32[]{:S(2)}, u32[]{:S(2)}) async-start(bf16[32,144,128]{2,1,0:T(8,128)(2,1)} %pack_first.1), calls=%async_computation | async-start | bytes 2359296 | tf_op jit(solution)/shard_map/all_to_all | solution.py:163
  11.0 30.6 %collective-permute-start = (bf16[4096,128]{1,0:T(8,128)(2,1)}, bf16[4096,128]{1,0:T(8,128)(2,1)}, u32[]{:S(2)}, u32[]{:S(2)}) collective-permute-start(bf16[4096,128]{1,0:T(8,128)(2,1)} %bitcast.8.w_own_ref), channel_id=1, source_target_pairs={{0,1},{1,0},{2,3},{3,2},{4,5},{5,4},{6,7},{7,6},{8,9},{9,8},{10,11... | collective-permute-start | bytes 3145736 | tf_op jit(solution)/shard_map/ppermute | solution.py:179
  13.8 1.9 copy-start.2
  15.7 1.8 copy-start.18
  15.7 15.1 %copy-start.4 = (bf16[1,4096]{1,0:T(2,128)(2,1)S(1)}, bf16[1,4096]{1,0:T(2,128)(2,1)}, u32[]{:S(2)}) copy-start(bf16[1,4096]{1,0:T(2,128)(2,1)} %gain_ref.7) | copy-start | bytes 24580
  16.9 0.6 copy-start.9
  30.8 4.8 %copy-start.7 = (bf16[3,2,64,128]{3,2,1,0:T(8,128)(2,1)}, bf16[3,2,64,128]{3,2,1,0:T(8,128)(2,1)S(1)}, u32[]{:S(2)}) copy-start(bf16[3,2,64,128]{3,2,1,0:T(8,128)(2,1)S(1)} %get-tuple-element.19) | copy-start | bytes 294916
  30.8 0.6 copy-start.11
  33.2 1.0 copy-start
  34.2 0.8 copy-start.3
  35.0 0.7 copy-start.5
  35.6 27.6 %copy-start.8 = (bf16[3,2,64,128]{3,2,1,0:T(8,128)(2,1)S(1)}, bf16[3,2,64,128]{3,2,1,0:T(8,128)(2,1)}, u32[]{:S(2)}) copy-start(bf16[3,2,64,128]{3,2,1,0:T(8,128)(2,1)} %copy-done.7) | copy-start | bytes 294916
  35.6 52.8 %copy-start.6 = (bf16[4,128,128]{2,1,0:T(8,128)(2,1)S(1)}, bf16[4,128,128]{2,1,0:T(8,128)(2,1)}, u32[]{:S(2)}) copy-start(bf16[4,128,128]{2,1,0:T(8,128)(2,1)} %copy-done.5) | copy-start | bytes 393220
  35.6 17.6 %all-to-all-start.1 = ((bf16[32,64,128]{2,1,0:T(8,128)(2,1)}), bf16[32,64,128]{2,1,0:T(8,128)(2,1)}, u32[]{:S(2)}, u32[]{:S(2)}) async-start(bf16[32,64,128]{2,1,0:T(8,128)(2,1)} %bitcast.30), calls=%async_computation.1 | async-start | bytes 1048576 | tf_op jit(solution)/shard_map/all_to_all | solution.py:163
  53.3 1.2 copy-start.1
  54.5 0.6 copy-start.12
  57.3 6.0 %collective-permute-start.1 = (bf16[2,64,128]{2,1,0:T(8,128)(2,1)S(1)}, bf16[2,64,128]{2,1,0:T(8,128)(2,1)}, u32[]{:S(2)}, u32[]{:S(2)}) collective-permute-start(bf16[2,64,128]{2,1,0:T(8,128)(2,1)S(1)} %back.4.refs_0_), channel_id=1, source_target_pairs={{0,32},{32,64},{64,96},{96,128},{128,160},{160,192},{192,224},{224... | collective-permute-start | bytes 98312 | tf_op jit(solution)/shard_map/ppermute | solution.py:205
  65.2 23.2 %all-to-all-start.2 = ((bf16[32,2,64,128]{3,2,1,0:T(8,128)(2,1)}), bf16[32,2,64,128]{3,2,1,0:T(8,128)(2,1)}, u32[]{:S(2)}, u32[]{:S(2)}) async-start(bf16[32,2,64,128]{3,2,1,0:T(8,128)(2,1)} %broadcast_in_dim.6), calls=%async_computation.2 | async-start | bytes 2097152 | tf_op jit(solution)/shard_map/all_to_all | solution.py:163
  88.4 18.2 %copy-start.16 = (s32[6]{0:T(128)S(1)}, s32[6]{0:T(128)}, u32[]{:S(2)}) copy-start(s32[6]{0:T(128)} %get-tuple-element.32.info_ref) | copy-start | bytes 76
  88.4 0.7 copy-start.15
  106.6 30.5 %copy-start.14 = (s32[6]{0:T(128)S(1)}, s32[6]{0:T(128)}, u32[]{:S(2)}) copy-start(s32[6]{0:T(128)} %get-tuple-element.33.info_ref) | copy-start | bytes 76
  109.0 5.9 %collective-permute-start.2 = (bf16[2,64,128]{2,1,0:T(8,128)(2,1)S(1)}, bf16[2,64,128]{2,1,0:T(8,128)(2,1)S(1)}, u32[]{:S(2)}, u32[]{:S(2)}) collective-permute-start(bf16[2,64,128]{2,1,0:T(8,128)(2,1)S(1)} %back.5.refs_1_), channel_id=1, source_target_pairs={{0,32},{32,64},{64,96},{96,128},{128,160},{160,192},{192,224},{224... | collective-permute-start | bytes 98312 | tf_op jit(solution)/shard_map/ppermute | solution.py:205
  154.0 31.0 %copy-start.13 = (s32[6]{0:T(128)S(1)}, s32[6]{0:T(128)}, u32[]{:S(2)}) copy-start(s32[6]{0:T(128)} %get-tuple-element.31.info_ref) | copy-start | bytes 76
  156.1 5.9 %collective-permute-start.3 = (bf16[2,64,128]{2,1,0:T(8,128)(2,1)S(1)}, bf16[2,64,128]{2,1,0:T(8,128)(2,1)S(1)}, u32[]{:S(2)}, u32[]{:S(2)}) collective-permute-start(bf16[2,64,128]{2,1,0:T(8,128)(2,1)S(1)} %back.6.refs_2_), channel_id=1, source_target_pairs={{0,32},{32,64},{64,96},{96,128},{128,160},{160,192},{192,224},{224... | collective-permute-start | bytes 98312 | tf_op jit(solution)/shard_map/ppermute | solution.py:205
  187.0 28.7 %copy-start.10 = (s32[4]{0:T(128)S(1)}, s32[4]{0:T(128)}, u32[]{:S(2)}) copy-start(s32[4]{0:T(128)} %copy-done.9) | copy-start | bytes 52

commit v2 on v1

v2 whole, which is shorter than its diff:
```python
import functools
import math

import jax
import jax.numpy as jnp
from jax import lax
from jax.experimental import pallas as pl
from jax.experimental.pallas import tpu as pltpu
from jax.sharding import PartitionSpec as P

HDIM = 128
CORES = 2
MOST_SECTIONS = 1024
SPARE = 16
VMEM_LIMIT = 12 * 1024 * 1024


def call(body, name, out_shape, scalars, arrays, scratch=(), anywhere=()):
    in_vmem = pl.BlockSpec(memory_space=pltpu.VMEM)
    in_smem = pl.BlockSpec(memory_space=pltpu.SMEM)
    return pl.pallas_call(
        body,
        out_shape=out_shape,
        in_specs=[in_smem] * len(scalars)
        + [pl.BlockSpec(memory_space=pl.ANY) if place in anywhere else in_vmem for place in range(len(arrays))],
        out_specs=jax.tree.map(lambda _: in_vmem, out_shape),
        scratch_shapes=list(scratch),
        compiler_params=pltpu.CompilerParams(vmem_limit_bytes=VMEM_LIMIT),
        name=name,
    )(*scalars, *arrays)


def shape(*dims):
    return jax.ShapeDtypeStruct(dims, jnp.bfloat16)


def pack_first(mine_ref, later_ref, out_ref, rows_ref, spare_ref):
    _, frames, local, width = mine_ref.shape
    group = out_ref.shape[0]
    blocks = width // HDIM
    each = local * blocks
    for frame in range(frames):
        wide = mine_ref[0, frame].astype(jnp.float32)
        for block in range(blocks):
            rows_ref[pl.ds(frame * each + block, local, stride=blocks), :] = wide[:, block * HDIM:(block + 1) * HDIM]
    spare_ref[...] = jnp.zeros_like(spare_ref)
    for tick in range(later_ref.shape[0]):
        for frame in range(frames):
            wide = later_ref[tick, frame].astype(jnp.float32)
            for block in range(blocks):
                chip, half = divmod(block, CORES)
                row = (chip * CORES + frame) * SPARE + tick * local * CORES + half
                spare_ref[pl.ds(row, local, stride=CORES), :] = wide[:, block * HDIM:(block + 1) * HDIM]
    for target in range(group):
        frame = target % CORES
        out_ref[target, :each] = rows_ref[frame * each:(frame + 1) * each].astype(jnp.bfloat16)
        out_ref[target, each:] = spare_ref[target * SPARE:(target + 1) * SPARE].astype(jnp.bfloat16)


def side_by_side(core, wide, own_ref, other_ref, out_ref, sem_ref, first):
    copies = []
    for index, (ref, place) in enumerate(((own_ref, core), (other_ref, 1 - core))):
        columns = pl.ds(pl.multiple_of(place * wide + first, HDIM), HDIM)
        copies.append(pltpu.make_async_copy(ref, out_ref.at[:, columns], sem_ref.at[index]))
    return copies


def unpack_first(local, info_ref, came_ref, own_ref, other_ref, hidden_ref, fresh_ref, wkv_ref, wq_ref, wide_ref, sem_ref):
    group, rows, _ = came_ref.shape
    chips, halves = hidden_ref.shape[:2]
    blocks = chips * halves
    core = lax.rem(info_ref[info_ref.shape[0] - 1], CORES)
    copies = []
    for kind, (out_ref, wide, first) in enumerate(((wq_ref, HDIM, 0), (wkv_ref, 2 * HDIM, 0), (wkv_ref, 2 * HDIM, HDIM))):
        copies += side_by_side(core, wide, own_ref.at[kind], other_ref.at[kind], out_ref, sem_ref.at[kind], first)
    for copy in copies:
        copy.start()
    for source in range(group):
        wide_ref[source * rows:(source + 1) * rows] = came_ref[source].astype(jnp.float32)

    def over_sources(row):
        return wide_ref[pl.ds(row, group, stride=rows), :].astype(jnp.bfloat16)

    for t in range(local):
        for block in range(blocks):
            hidden_ref[block // halves, block % halves, t * group:(t + 1) * group] = over_sources(t * blocks + block)
    for tick in range(fresh_ref.shape[0]):
        for t in range(local):
            for half in range(halves):
                fresh_ref[tick, half, t * group:(t + 1) * group] = over_sources(
                    local * blocks + (tick * local + t) * halves + half
                )
    for copy in copies:
        copy.wait()


def join_out(info_ref, own_ref, other_ref, after_ref, out_ref, sem_ref):
    core = lax.rem(info_ref[info_ref.shape[0] - 1], CORES)
    copies = side_by_side(core, HDIM, own_ref, other_ref, out_ref, sem_ref, 0)
    for copy in copies:
        copy.start()
    for copy in copies:
        copy.wait()


def slot_of(info_ref, tick):
    slots = info_ref.shape[0] - 2
    return lax.rem(tick + slots * MOST_SECTIONS - info_ref[slots], slots)


def core_live(info_ref, tick):
    core = lax.rem(info_ref[info_ref.shape[0] - 1], CORES)
    return core < info_ref[slot_of(info_ref, tick)]


def layer_keys(tick, info_ref, x_ref, gain_ref, w_ref, *refs):
    *stale_ref, xn_ref, new_ref = refs
    chips, halves, tokens, width = x_ref.shape
    squares = jnp.zeros((tokens, width), jnp.float32)
    for chip in range(chips):
        for half in range(halves):
            wide = x_ref[chip, half].astype(jnp.float32)
            squares = squares + wide * wide
    mean_square = jnp.sum(squares, axis=1, keepdims=True) / (chips * halves * width)
    scale = jnp.where(core_live(info_ref, tick), lax.rsqrt(mean_square + 1e-06), 0.0)
    for chip in range(chips):
        for half in range(halves):
            first = (chip * halves + half) * width
            wide = x_ref[chip, half].astype(jnp.float32)
            normed = wide * scale * gain_ref[:, first:first + width].astype(jnp.float32)
            xn_ref[:, first:first + width] = normed.astype(jnp.bfloat16)
    new_ref[:tokens] = jnp.dot(xn_ref[...], w_ref[...], preferred_element_type=jnp.float32).astype(jnp.bfloat16)
    for ref in stale_ref:
        rows, both = ref.shape
        for part in range(CORES):
            new_ref[tokens:, part * both:(part + 1) * both] = ref[part * rows // CORES:(part + 1) * rows // CORES]


def layer_queries(xn_ref, w_ref, out_ref):
    out_ref[...] = jnp.dot(xn_ref[...], w_ref[...], preferred_element_type=jnp.float32).astype(jnp.bfloat16)


def layer_attend(tick, info_ref, q_ref, own_ref, other_ref, *refs):
    *kv_ref, out_ref, kv_out = refs
    chips, halves, tokens, width = out_ref.shape
    slots, frames = kv_out.shape[:2]
    rows = frames * tokens
    slot = slot_of(info_ref, tick)
    core = lax.rem(info_ref[slots + 1], CORES)
    for ref in kv_ref:
        kv_out[...] = ref[...]
    if not kv_ref:
        both = 2 * width
        dims = (slots // CORES, frames, tokens, both)
        for mine in range(CORES):

            @pl.when(core == mine)
            def _():
                for half, ref in enumerate((own_ref, other_ref) if mine == 0 else (other_ref, own_ref)):
                    for part in range(CORES):
                        kv_out[part * dims[0]:(part + 1) * dims[0], :, :, half * both:(half + 1) * both] = ref[
                            tokens:, part * both:(part + 1) * both
                        ].reshape(dims)

    kv_out[slot, core] = own_ref[:tokens]
    kv_out[slot, 1 - core] = other_ref[:tokens]
    key_ids = lax.broadcasted_iota(jnp.int32, (1, slots * rows), 1)
    key_slot = key_ids // rows
    limit = jnp.zeros_like(key_ids)
    for patch in range(slots):
        limit = jnp.where(key_slot == patch, info_ref[patch] * tokens, limit)
    key_live = key_ids - key_slot * rows < limit
    for half in range(halves):
        queries = q_ref[:, half * width:(half + 1) * width]
        keys = kv_out[:, :, :, 2 * half * width:(2 * half + 1) * width].reshape(slots * rows, width)
        values = kv_out[:, :, :, (2 * half + 1) * width:(2 * half + 2) * width].reshape(slots * rows, width)
        scores = lax.dot_general(
            queries, keys, (((1,), (1,)), ((), ())), preferred_element_type=jnp.float32
        ) / math.sqrt(HDIM)
        scores = jnp.where(key_live, scores, -jnp.inf)
        exponent = jnp.exp(scores - jnp.max(scores, axis=1, keepdims=True))
        row_total = jnp.sum(exponent, axis=1, keepdims=True)
        attended = jnp.dot(exponent.astype(jnp.bfloat16), values, preferred_element_type=jnp.float32)
        attended = (attended / row_total).astype(jnp.bfloat16)
        for chip in range(chips):
            out_ref[chip, half] = attended


def layer_back(tick, info_ref, a_ref, w_ref, x_ref, out_ref, wide_ref):
    chips, halves, tokens, width = a_ref.shape
    chip = lax.div(info_ref[info_ref.shape[0] - 1], CORES)
    live = core_live(info_ref, tick)
    for source in range(chips):
        for half in range(halves):
            first = (source * halves + half) * width
            wide_ref[:, first:first + width] = a_ref[source, half]
    branch = jnp.dot(wide_ref[...], w_ref[...], preferred_element_type=jnp.float32).astype(jnp.bfloat16)
    for half in range(halves):
        total = x_ref[chip, half].astype(jnp.float32) + branch[:, half * width:(half + 1) * width].astype(jnp.float32)
        out_ref[half] = jnp.where(live, total, 0.0).astype(jnp.bfloat16)


def pack_last(*refs):
    *result_refs, out_ref, wide_ref = refs
    group, parts, _ = out_ref.shape
    ticks = len(result_refs)
    for tick, ref in enumerate(result_refs):
        halves, tokens, _ = ref.shape
        for half in range(halves):
            first = (half * ticks + tick) * tokens
            wide_ref[first:first + tokens] = ref[half].astype(jnp.float32)
    for target in range(group):
        out_ref[target] = wide_ref[pl.ds(target, parts, stride=group), :].astype(jnp.bfloat16)


def unpack_last(info_ref, came_ref, out_ref, turn_ref):
    group, parts, width = came_ref.shape
    patches, frames, local, _ = out_ref.shape
    each = parts // CORES
    for source in range(group):
        chip, frame = divmod(source, CORES)
        wide = came_ref[source].astype(jnp.float32)
        for half in range(CORES):
            first = (chip * CORES + half) * width
            turn_ref[frame * each:(frame + 1) * each, first:first + width] = wide[half * each:(half + 1) * each]
    for tick in range(patches):
        slot = slot_of(info_ref, tick)
        for frame in range(frames):
            row = frame * each + tick * local
            out_ref[slot, frame] = turn_ref[row:row + local].astype(jnp.bfloat16)


def swap(value, groups=None):
    return lax.all_to_all(value, "seq", split_axis=0, concat_axis=0, tiled=True, axis_index_groups=groups)


def on_device(in_flight, entering, patch_frames, norm_gain, qkv_weight, out_weight, stale_kv):
    section = lax.axis_index("section")
    sections = lax.axis_size("section")
    me = lax.axis_index("seq")
    group = lax.axis_size("seq")
    patches, frames, tokens = stale_kv.shape[1:4]
    local = in_flight.shape[2]
    width = in_flight.shape[3]
    ticks = patches
    chips = group // CORES
    halves = CORES
    owned = local * group
    same_core = [[CORES * chip + core for chip in range(chips)] for core in range(CORES)]
    partner = [(device, device ^ 1) for device in range(group)]
    info = jnp.concatenate([patch_frames, jnp.stack([section, me]).astype(jnp.int32)])

    w_in = jnp.transpose(qkv_weight[0], (1, 0, 2))
    w_in_other = lax.ppermute(w_in, "seq", partner)
    sent = call(
        pack_first,
        "pack_first",
        shape(group, owned + SPARE, HDIM),
        (),
        (in_flight, entering),
        [pltpu.VMEM((frames * owned, HDIM), jnp.float32), pltpu.VMEM((group * SPARE, HDIM), jnp.float32)],
    )
    sent, w_out_own = lax.optimization_barrier((sent, out_weight[0]))
    came = swap(sent)
    w_out_other = lax.ppermute(w_out_own, "seq", partner)
    stale = stale_kv[0].reshape(patches * frames * tokens, 2 * HDIM)
    gathered, fresh, w_kv, w_q = call(
        functools.partial(unpack_first, local),
        "unpack_first",
        (
            shape(chips, halves, tokens, HDIM),
            shape(ticks - 1, halves, tokens, HDIM),
            shape(width, 2 * halves * HDIM),
            shape(width, halves * HDIM),
        ),
        (info,),
        (came, w_in, w_in_other),
        [pltpu.VMEM((group * (owned + SPARE), HDIM), jnp.float32), pltpu.SemaphoreType.DMA((3, CORES))],
        anywhere=(1, 2),
    )
    w_out = call(
        join_out,
        "join_out",
        shape(width, halves * HDIM),
        (info,),
        (out_weight[0], w_out_other, fresh),
        [pltpu.SemaphoreType.DMA((CORES,))],
        anywhere=(0, 1, 2),
    )

    new_rows = tokens + patches * frames * tokens // CORES
    results = []
    for tick in range(ticks):
        if tick:
            arrived = lax.ppermute(
                results[-1], "section", [(source, source + 1) for source in range(sections - 1)]
            )
            arrived = jnp.where(section == 0, fresh[tick - 1], arrived)
            gathered = swap(jnp.broadcast_to(arrived[None], (chips,) + arrived.shape), same_core)
        normed, own = call(
            functools.partial(layer_keys, tick),
            "keys",
            (shape(tokens, width), shape(tokens if tick else new_rows, 2 * halves * HDIM)),
            (info,),
            (gathered, norm_gain, w_kv) + (() if tick else (stale,)),
        )
        other = lax.ppermute(own, "seq", partner)
        queries = call(layer_queries, "queries", shape(tokens, halves * HDIM), (), (normed, w_q))
        attended, kv = call(
            functools.partial(layer_attend, tick),
            "attend",
            (shape(chips, halves, tokens, HDIM), shape(patches, frames, tokens, 2 * halves * HDIM)),
            (info,),
            (queries, own, other) + ((kv,) if tick else ()),
        )
        results.append(
            call(
                functools.partial(layer_back, tick),
                "back",
                shape(halves, tokens, HDIM),
                (info,),
                (swap(attended, same_core), w_out, gathered),
                [pltpu.VMEM((tokens, width), jnp.bfloat16)],
            )
        )

    parts = ticks * halves * local
    sent = call(
        pack_last,
        "pack_last",
        shape(group, parts, HDIM),
        (),
        tuple(results),
        [pltpu.VMEM((ticks * halves * tokens, HDIM), jnp.float32)],
    )
    outputs = call(
        unpack_last,
        "unpack_last",
        shape(patches, frames, local, width),
        (info,),
        (swap(sent),),
        [pltpu.VMEM((parts, width), jnp.float32)],
    )
    return outputs[None]


def solution(mesh):
    in_specs = (
        P("section", None, "seq", None),
        P(None, None, "seq", None),
        P(),
        P("section", None),
        P("section", None, None, "seq"),
        P("section", None, "seq"),
        P("section", None, None, None, None, "seq"),
    )
    out_specs = P("section", None, None, "seq", None)
    return jax.shard_map(
        on_device, mesh=mesh, in_specs=in_specs, out_specs=out_specs, check_vma=False
    )
```

time: 218 us -> 197 us (0.904)
  waiting for transfers between devices: 47.1 us -> 29.7 us
  starting transfers between devices: 28.3 us -> 40.4 us
  blocking collectives: 101 us -> 90.2 us
  other arithmetic: 5.96 us -> 0.76 us
  local copies, waits for them, and re-layouts: 13.5 us -> 9.98 us
  Pallas kernels: 21.5 us -> 24.3 us
    ppermute x1 -> x6, starting transfers between devices: 2.21 us -> 23.1 us  [the longest x4 18.3 us: on_device(): other = lax.ppermute(own, 'seq', partner)]
    all_to_all x3 -> x2, waiting for transfers between devices: 35.9 us -> 16.8 us  [swap(): lax.all_to_all(value, 'seq', split_axis=0, concat_axis=0, tiled=True, axi...]
    all_to_all x6 -> x7, blocking collectives: 101 us -> 90.2 us  [swap(): lax.all_to_all(value, 'seq', split_axis=0, concat_axis=0, tiled=True, axi...]
    all_to_all x3 -> x2, starting transfers between devices: 19.6 us -> 10.8 us  [swap(): lax.all_to_all(value, 'seq', split_axis=0, concat_axis=0, tiled=True, axi...]
    concatenate x2 -> x1, other arithmetic: 4.41 us -> 0.73 us  [on_device(): jnp.concatenate([patch_frames, jnp.stack([section, me]).astype(jnp.int32)])]
    pallas_call x13 -> x21, Pallas kernels: 21.5 us -> 24.3 us  [call(): pl.pallas_call(body, out_shape=out_shape, in_specs=[in_smem] * len(scalar...]
    reshape x5 -> x0, local copies, waits for them, and re-layouts: 2.65 us -> none  [the longest x2 1.08 us: on_device(): later = entering.reshape(ticks - 1, frames, local, chips, halves, HDIM)]
    unnamed x40 -> x31, local copies, waits for them, and re-layouts: 8 us -> 9.65 us
  transfers between devices with their start and end apart: 7 -> 11, of which waited for: 6 -> 9; matrix products, arithmetic and copies ran while one was open for 3% -> 1% of each run, Pallas kernels for 2% -> 5%
where the time goes in v2:
time: 197 us; the launch traced here: 196 us
  blocking collectives  90.2 us (46%)
  starting transfers between devices  40.4 us (21%)
  waiting for transfers between devices  29.7 us (15%)
  Pallas kernels  24.3 us (12%)
  local copies, waits for them, and re-layouts  9.98 us (5%)
    all_to_all x7, blocking collectives, swap(): lax.all_to_all(value, 'seq', split_axis=0, concat_axis=0, tiled=True, axi...  90.2 us
    pallas_call x21, Pallas kernels, call(): pl.pallas_call(body, out_shape=out_shape, in_specs=[in_smem] * len(scalar...  24.3 us
    ppermute x4, starting transfers between devices, on_device(): other = lax.ppermute(own, 'seq', partner)  18.3 us
    all_to_all x2, waiting for transfers between devices, swap(): lax.all_to_all(value, 'seq', split_axis=0, concat_axis=0, tiled=True, axi...  16.8 us
    ppermute x3, waiting for transfers between devices, on_device(): lax.ppermute(results[-1], 'section', [(source, source + 1) for source in...  11.1 us
    all_to_all x2, starting transfers between devices, swap(): lax.all_to_all(value, 'seq', split_axis=0, concat_axis=0, tiled=True, axi...  10.8 us
    unnamed x31, local copies, waits for them, and re-layouts  9.65 us
    ppermute x3, starting transfers between devices, on_device(): lax.ppermute(results[-1], 'section', [(source, source + 1) for source in...  6.49 us
  transfers between devices with their start and end apart: 11, of which 9 were waited for; matrix products, arithmetic and copies ran while one was open for 1% of the time, Pallas kernels for 5%

profile of v2, /device:TPU:385, one launch (start us, length us, event | category | flops | bytes accessed | tf_op | source)
XLA Modules:
  0.0 195.7 jit_solution(3932931513737016167)
XLA Ops:
  0.0 2.6 %collective-permute-start = (bf16[3,4096,128]{2,1,0:T(8,128)(2,1)}, bf16[3,4096,128]{2,1,0:T(8,128)(2,1)S(1)}, u32[]{:S(2)}, u32[]{:S(2)}) collective-permute-start(bf16[3,4096,128]{2,1,0:T(8,128)(2,1)} %bitcast.18), channel_id=1, source_target_pairs={{0,1},{1,0},{2,3},{3,2},{4,5},{5,4},{6,7},{7,6},{8,9},{9,8},{10,11... | collective-permute-start | bytes 9437192 | tf_op jit(solution)/shard_map/ppermute | solution.py:254
  2.6 0.9 copy-done.13
  3.5 0.8 copy-done.14
  4.4 0.9 copy-done.6
  5.3 7.2 %all-to-all-start = ((bf16[32,80,128]{2,1,0:T(8,128)(2,1)}), bf16[32,80,128]{2,1,0:T(8,128)(2,1)}, u32[]{:S(2)}, u32[]{:S(2)}) async-start(bf16[32,80,128]{2,1,0:T(8,128)(2,1)} %copy-done.6), calls=%async_computation | async-start | bytes 1310720 | tf_op jit(solution)/shard_map/all_to_all | solution.py:234
  12.5 2.2 %collective-permute-start.2 = (bf16[4096,128]{1,0:T(8,128)(2,1)}, bf16[4096,128]{1,0:T(8,128)(2,1)}, u32[]{:S(2)}, u32[]{:S(2)}) collective-permute-start(bf16[4096,128]{1,0:T(8,128)(2,1)} %bitcast.20), channel_id=1, source_target_pairs={{0,1},{1,0},{2,3},{3,2},{4,5},{5,4},{6,7},{7,6},{8,9},{9,8},{10,11... | collective-permute-start | bytes 3145736 | tf_op jit(solution)/shard_map/ppermute | solution.py:265
  14.7 1.0 copy.10
  15.7 0.7 pad_add_fusion.info_ref
  16.5 9.0 %all-to-all-done.came_ref = bf16[32,80,128]{2,1,0:T(8,128)(2,1)} async-done(((bf16[32,80,128]{2,1,0:T(8,128)(2,1)}), bf16[32,80,128]{2,1,0:T(8,128)(2,1)}, u32[]{:S(2)}, u32[]{:S(2)}) %all-to-all-start) | async-done | bytes 655392 | tf_op jit(solution)/shard_map/all_to_all | solution.py:234
  25.5 1.9 copy-done.5
  27.4 2.7 %unpack_first.1 = (bf16[16,2,64,128]{3,2,1,0:T(8,128)(2,1)S(1)}, bf16[3,2,64,128]{3,2,1,0:T(8,128)(2,1)S(1)}, bf16[4096,512]{1,0:T(8,128)(2,1)S(1)}, bf16[4096,256]{1,0:T(8,128)(2,1)S(1)}) custom-call(s32[6]{0:T(128)S(1)} %pad_add_fusion.info_ref, bf16[32,80,128]{2,1,0:T(8,128)(2,1)} %all-to-all-done.came_ref, bf16[3,4096,128]{2,1,0:T(8,128)(2,1)S(1)} %bitcast.19, ...), custom_call_target="tpu_custom_call" | custom-call | tf_op jit(solution)/shard_map/unpack_first/pallas_call | solution.py:21
  30.1 1.5 keys.4
  31.6 2.5 %collective-permute-start.1 = (bf16[320,512]{1,0:T(8,128)(2,1)S(1)}, bf16[320,512]{1,0:T(8,128)(2,1)S(1)}, u32[]{:S(2)}, u32[]{:S(2)}) collective-permute-start(bf16[320,512]{1,0:T(8,128)(2,1)S(1)} %get-tuple-element.31.own_ref), channel_id=1, source_target_pairs={{0,1},{1,0},{2,3},{3,2},{4,5},{5,4},{6,7},{7,6},{8,9},{9,8},{10,11... | collective-permute-start | bytes 983048 | tf_op jit(solution)/shard_map/ppermute | solution.py:307
  34.6 0.7 collective-permute-done.1.other_ref
  35.3 2.1 %attend.4 = (bf16[16,2,64,128]{3,2,1,0:T(8,128)(2,1)}, bf16[4,2,64,512]{3,2,1,0:T(8,128)(2,1)S(1)}) custom-call(s32[6]{0:T(128)S(1)} %pad_add_fusion.info_ref, bf16[64,256]{1,0:T(8,128)(2,1)S(1)} %queries.4.q_ref, bf16[320,512]{1,0:T(8,128)(2,1)S(1)} %get-tuple-element.31.own_ref, bf16[320,512]{1,0:T(8,128)(2,1)S(1)} %collective-permute-done.1.other_ref), custom_call_target="tpu_custom_call" | custom-call | tf_op jit(solution)/shard_map/attend/pallas_call | solution.py:21
  37.4 0.8 copy-done.10
  38.2 3.6 %all-to-all-start.1 = ((bf16[16,2,64,128]{3,2,1,0:T(8,128)(2,1)}), bf16[16,2,64,128]{3,2,1,0:T(8,128)(2,1)S(1)}, u32[]{:S(2)}, u32[]{:S(2)}) async-start(bf16[16,2,64,128]{3,2,1,0:T(8,128)(2,1)} %get-tuple-element.32), calls=%async_computation.1 | async-start | bytes 1048576 | tf_op jit(solution)/shard_map/all_to_all | solution.py:234
  41.8 1.2 copy-done.9
  43.0 2.0 %join_out.1.w_ref = bf16[4096,256]{1,0:T(8,128)(2,1)S(1)} custom-call(s32[6]{0:T(128)S(1)} %pad_add_fusion.info_ref, bf16[4096,128]{1,0:T(8,128)(2,1)S(1)} %bitcast.21, bf16[4096,128]{1,0:T(8,128)(2,1)} %collective-permute-done.2.other_ref, bf16[3,2,64,128]{3,2,1,0:T(8,128)(2,1)S(1)} %get-tuple-element.34.after_ref), custom_call_target="tpu_custom_call" | custom-call | tf_op jit(solution)/shard_map/join_out/pallas_call | solution.py:21
  45.0 7.7 %all-to-all-done.1.a_ref = bf16[16,2,64,128]{3,2,1,0:T(8,128)(2,1)S(1)} async-done(((bf16[16,2,64,128]{3,2,1,0:T(8,128)(2,1)}), bf16[16,2,64,128]{3,2,1,0:T(8,128)(2,1)S(1)}, u32[]{:S(2)}, u32[]{:S(2)}) %all-to-all-start.1) | async-done | bytes 524320 | tf_op jit(solution)/shard_map/all_to_all | solution.py:234
  52.8 1.1 back.4.refs_0_
  53.8 2.6 %collective-permute-start.3 = (bf16[2,64,128]{2,1,0:T(8,128)(2,1)S(1)}, bf16[2,64,128]{2,1,0:T(8,128)(2,1)S(1)}, u32[]{:S(2)}, u32[]{:S(2)}) collective-permute-start(bf16[2,64,128]{2,1,0:T(8,128)(2,1)S(1)} %back.4.refs_0_), channel_id=1, source_target_pairs={{0,32},{32,64},{64,96},{96,128},{128,160},{160,192},{192,224},{224... | collective-permute-start | bytes 98312 | tf_op jit(solution)/shard_map/ppermute | solution.py:295
  56.5 3.2 %collective-permute-done.3 = bf16[2,64,128]{2,1,0:T(8,128)(2,1)S(1)} collective-permute-done((bf16[2,64,128]{2,1,0:T(8,128)(2,1)S(1)}, bf16[2,64,128]{2,1,0:T(8,128)(2,1)S(1)}, u32[]{:S(2)}, u32[]{:S(2)}) %collective-permute-start.3) | collective-permute-done | bytes 32800 | tf_op jit(solution)/shard_map/ppermute | solution.py:295
  59.8 12.3 %all_to_all.45.x_ref = bf16[16,2,64,128]{3,2,1,0:T(8,128)(2,1)S(1)} all-to-all(bf16[16,2,64,128]{3,2,1,0:T(8,128)(2,1)S(1)} %broadcast_in_dim.8), channel_id=1, replica_groups={{0,2,4,6,8,10,12,14,16,18,20,22,24,26,28,30},{1,3,5,7,9,11,13,15,17,19,..., dimensions={0} | all-to-all | bytes 1048576 | tf_op jit(solution)/shard_map/all_to_all | solution.py:234
  72.2 2.2 %copy-done.1 = bf16[4096,512]{1,0:T(8,128)(2,1)S(1)} copy-done((bf16[4096,512]{1,0:T(8,128)(2,1)S(1)}, bf16[4096,512]{1,0:T(8,128)(2,1)}, u32[]{:S(2)}) %copy-start.1) | copy-done | bytes 4194328
  74.4 1.5 keys.5
  75.9 5.1 %collective-permute-start.4 = (bf16[64,512]{1,0:T(8,128)(2,1)S(1)}, bf16[64,512]{1,0:T(8,128)(2,1)S(1)}, u32[]{:S(2)}, u32[]{:S(2)}) collective-permute-start(bf16[64,512]{1,0:T(8,128)(2,1)S(1)} %get-tuple-element.36.own_ref), channel_id=1, source_target_pairs={{0,1},{1,0},{2,3},{3,2},{4,5},{5,4},{6,7},{7,6},{8,9},{9,8},{10,11... | collective-permute-start | bytes 196616 | tf_op jit(solution)/shard_map/ppermute | solution.py:307
  81.9 1.2 attend.5
  83.1 13.6 %all_to_all.46.a_ref = bf16[16,2,64,128]{3,2,1,0:T(8,128)(2,1)S(1)} all-to-all(bf16[16,2,64,128]{3,2,1,0:T(8,128)(2,1)S(1)} %get-tuple-element.38), channel_id=1, replica_groups={{0,2,4,6,8,10,12,14,16,18,20,22,24,26,28,30},{1,3,5,7,9,11,13,15,17,19,..., dimensions={0} | all-to-all | bytes 1048576 | tf_op jit(solution)/shard_map/all_to_all | solution.py:234
  96.7 1.1 back.5.refs_1_
  97.8 1.9 collective-permute-start.5
  99.7 3.9 %collective-permute-done.5 = bf16[2,64,128]{2,1,0:T(8,128)(2,1)S(1)} collective-permute-done((bf16[2,64,128]{2,1,0:T(8,128)(2,1)S(1)}, bf16[2,64,128]{2,1,0:T(8,128)(2,1)S(1)}, u32[]{:S(2)}, u32[]{:S(2)}) %collective-permute-start.5) | collective-permute-done | bytes 32800 | tf_op jit(solution)/shard_map/ppermute | solution.py:295
  103.8 12.5 %all_to_all.47.x_ref = bf16[16,2,64,128]{3,2,1,0:T(8,128)(2,1)S(1)} all-to-all(bf16[16,2,64,128]{3,2,1,0:T(8,128)(2,1)S(1)} %broadcast_in_dim.9), channel_id=1, replica_groups={{0,2,4,6,8,10,12,14,16,18,20,22,24,26,28,30},{1,3,5,7,9,11,13,15,17,19,..., dimensions={0} | all-to-all | bytes 1048576 | tf_op jit(solution)/shard_map/all_to_all | solution.py:234
  116.3 1.5 keys.6
  117.8 5.4 %collective-permute-start.6 = (bf16[64,512]{1,0:T(8,128)(2,1)S(1)}, bf16[64,512]{1,0:T(8,128)(2,1)S(1)}, u32[]{:S(2)}, u32[]{:S(2)}) collective-permute-start(bf16[64,512]{1,0:T(8,128)(2,1)S(1)} %get-tuple-element.40.own_ref), channel_id=1, source_target_pairs={{0,1},{1,0},{2,3},{3,2},{4,5},{5,4},{6,7},{7,6},{8,9},{9,8},{10,11... | collective-permute-start | bytes 196616 | tf_op jit(solution)/shard_map/ppermute | solution.py:307
  124.0 1.2 attend.6
  125.3 13.5 %all_to_all.48.a_ref = bf16[16,2,64,128]{3,2,1,0:T(8,128)(2,1)S(1)} all-to-all(bf16[16,2,64,128]{3,2,1,0:T(8,128)(2,1)S(1)} %get-tuple-element.42), channel_id=1, replica_groups={{0,2,4,6,8,10,12,14,16,18,20,22,24,26,28,30},{1,3,5,7,9,11,13,15,17,19,..., dimensions={0} | all-to-all | bytes 1048576 | tf_op jit(solution)/shard_map/all_to_all | solution.py:234
  138.7 1.1 back.6.refs_2_
  139.8 1.9 collective-permute-start.7
  141.7 3.9 %collective-permute-done.7 = bf16[2,64,128]{2,1,0:T(8,128)(2,1)S(1)} collective-permute-done((bf16[2,64,128]{2,1,0:T(8,128)(2,1)S(1)}, bf16[2,64,128]{2,1,0:T(8,128)(2,1)S(1)}, u32[]{:S(2)}, u32[]{:S(2)}) %collective-permute-start.7) | collective-permute-done | bytes 32800 | tf_op jit(solution)/shard_map/ppermute | solution.py:295
  145.8 12.5 %all_to_all.49.x_ref = bf16[16,2,64,128]{3,2,1,0:T(8,128)(2,1)S(1)} all-to-all(bf16[16,2,64,128]{3,2,1,0:T(8,128)(2,1)S(1)} %broadcast_in_dim.10), channel_id=1, replica_groups={{0,2,4,6,8,10,12,14,16,18,20,22,24,26,28,30},{1,3,5,7,9,11,13,15,17,19,..., dimensions={0} | all-to-all | bytes 1048576 | tf_op jit(solution)/shard_map/all_to_all | solution.py:234
  158.3 1.5 keys.7
  159.8 5.4 %collective-permute-start.8 = (bf16[64,512]{1,0:T(8,128)(2,1)S(1)}, bf16[64,512]{1,0:T(8,128)(2,1)S(1)}, u32[]{:S(2)}, u32[]{:S(2)}) collective-permute-start(bf16[64,512]{1,0:T(8,128)(2,1)S(1)} %get-tuple-element.44.own_ref), channel_id=1, source_target_pairs={{0,1},{1,0},{2,3},{3,2},{4,5},{5,4},{6,7},{7,6},{8,9},{9,8},{10,11... | collective-permute-start | bytes 196616 | tf_op jit(solution)/shard_map/ppermute | solution.py:307
  166.0 1.4 attend.7
  167.4 13.4 %all_to_all.50.a_ref = bf16[16,2,64,128]{3,2,1,0:T(8,128)(2,1)S(1)} all-to-all(bf16[16,2,64,128]{3,2,1,0:T(8,128)(2,1)S(1)} %get-tuple-element.46), channel_id=1, replica_groups={{0,2,4,6,8,10,12,14,16,18,20,22,24,26,28,30},{1,3,5,7,9,11,13,15,17,19,..., dimensions={0} | all-to-all | bytes 1048576 | tf_op jit(solution)/shard_map/all_to_all | solution.py:234
  180.8 1.1 back.7.refs_3_
  182.1 12.4 %all_to_all.51.came_ref = bf16[32,16,128]{2,1,0:T(8,128)(2,1)S(1)} all-to-all(bf16[32,16,128]{2,1,0:T(8,128)(2,1)S(1)} %pack_last.1), channel_id=1, replica_groups=mesh['section'=16,'seq'=32] {'seq'}, dimensions={0} | all-to-all | bytes 262144 | tf_op jit(solution)/shard_map/all_to_all | solution.py:234
  194.5 1.3 unpack_last.1
  (40 shorter events, 3.8 us)
Async XLA Ops:
  0.0 25.5 %collective-permute-start = (bf16[3,4096,128]{2,1,0:T(8,128)(2,1)}, bf16[3,4096,128]{2,1,0:T(8,128)(2,1)S(1)}, u32[]{:S(2)}, u32[]{:S(2)}) collective-permute-start(bf16[3,4096,128]{2,1,0:T(8,128)(2,1)} %bitcast.18), channel_id=1, source_target_pairs={{0,1},{1,0},{2,3},{3,2},{4,5},{5,4},{6,7},{7,6},{8,9},{9,8},{10,11... | collective-permute-start | bytes 9437192 | tf_op jit(solution)/shard_map/ppermute | solution.py:254
  2.6 0.9 copy-start.13
  3.5 0.8 copy-start.14
  4.4 0.9 copy-start.6
  5.3 20.2 %all-to-all-start = ((bf16[32,80,128]{2,1,0:T(8,128)(2,1)}), bf16[32,80,128]{2,1,0:T(8,128)(2,1)}, u32[]{:S(2)}, u32[]{:S(2)}) async-start(bf16[32,80,128]{2,1,0:T(8,128)(2,1)} %copy-done.6), calls=%async_computation | async-start | bytes 1310720 | tf_op jit(solution)/shard_map/all_to_all | solution.py:234
  12.5 29.3 %collective-permute-start.2 = (bf16[4096,128]{1,0:T(8,128)(2,1)}, bf16[4096,128]{1,0:T(8,128)(2,1)}, u32[]{:S(2)}, u32[]{:S(2)}) collective-permute-start(bf16[4096,128]{1,0:T(8,128)(2,1)} %bitcast.20), channel_id=1, source_target_pairs={{0,1},{1,0},{2,3},{3,2},{4,5},{5,4},{6,7},{7,6},{8,9},{9,8},{10,11... | collective-permute-start | bytes 3145736 | tf_op jit(solution)/shard_map/ppermute | solution.py:265
  25.5 1.9 copy-start.5
  27.4 2.7 %copy-start.12 = (bf16[1,4096]{1,0:T(2,128)(2,1)S(1)}, bf16[1,4096]{1,0:T(2,128)(2,1)}, u32[]{:S(2)}) copy-start(bf16[1,4096]{1,0:T(2,128)(2,1)} %gain_ref.7) | copy-start | bytes 24580
  30.1 4.5 %copy-start = (bf16[4096,512]{1,0:T(8,128)(2,1)}, bf16[4096,512]{1,0:T(8,128)(2,1)S(1)}, u32[]{:S(2)}) copy-start(bf16[4096,512]{1,0:T(8,128)(2,1)S(1)} %get-tuple-element.28.w_ref) | copy-start | bytes 12582916
  30.1 4.5 %copy-start.3 = (bf16[4096,256]{1,0:T(8,128)(2,1)}, bf16[4096,256]{1,0:T(8,128)(2,1)S(1)}, u32[]{:S(2)}) copy-start(bf16[4096,256]{1,0:T(8,128)(2,1)S(1)} %get-tuple-element.30.w_ref) | copy-start | bytes 6291460
  30.1 4.5 %copy-start.7 = (bf16[16,2,64,128]{3,2,1,0:T(8,128)(2,1)}, bf16[16,2,64,128]{3,2,1,0:T(8,128)(2,1)S(1)}, u32[]{:S(2)}) copy-start(bf16[16,2,64,128]{3,2,1,0:T(8,128)(2,1)S(1)} %get-tuple-element.27.x_ref) | copy-start | bytes 1572868
  31.6 3.7 %collective-permute-start.1 = (bf16[320,512]{1,0:T(8,128)(2,1)S(1)}, bf16[320,512]{1,0:T(8,128)(2,1)S(1)}, u32[]{:S(2)}, u32[]{:S(2)}) collective-permute-start(bf16[320,512]{1,0:T(8,128)(2,1)S(1)} %get-tuple-element.31.own_ref), channel_id=1, source_target_pairs={{0,1},{1,0},{2,3},{3,2},{4,5},{5,4},{6,7},{7,6},{8,9},{9,8},{10,11... | collective-permute-start | bytes 983048 | tf_op jit(solution)/shard_map/ppermute | solution.py:307
  35.3 17.5 %copy-start.8 = (bf16[16,2,64,128]{3,2,1,0:T(8,128)(2,1)S(1)}, bf16[16,2,64,128]{3,2,1,0:T(8,128)(2,1)}, u32[]{:S(2)}) copy-start(bf16[16,2,64,128]{3,2,1,0:T(8,128)(2,1)} %copy-done.7) | copy-start | bytes 1572868
  37.4 0.8 copy-start.10
  38.2 14.5 %all-to-all-start.1 = ((bf16[16,2,64,128]{3,2,1,0:T(8,128)(2,1)}), bf16[16,2,64,128]{3,2,1,0:T(8,128)(2,1)S(1)}, u32[]{:S(2)}, u32[]{:S(2)}) async-start(bf16[16,2,64,128]{3,2,1,0:T(8,128)(2,1)} %get-tuple-element.32), calls=%async_computation.1 | async-start | bytes 1048576 | tf_op jit(solution)/shard_map/all_to_all | solution.py:234
  41.8 1.2 copy-start.9
  53.8 5.9 %collective-permute-start.3 = (bf16[2,64,128]{2,1,0:T(8,128)(2,1)S(1)}, bf16[2,64,128]{2,1,0:T(8,128)(2,1)S(1)}, u32[]{:S(2)}, u32[]{:S(2)}) collective-permute-start(bf16[2,64,128]{2,1,0:T(8,128)(2,1)S(1)} %back.4.refs_0_), channel_id=1, source_target_pairs={{0,32},{32,64},{64,96},{96,128},{128,160},{160,192},{192,224},{224... | collective-permute-start | bytes 98312 | tf_op jit(solution)/shard_map/ppermute | solution.py:295
  72.2 2.2 %copy-start.1 = (bf16[4096,512]{1,0:T(8,128)(2,1)S(1)}, bf16[4096,512]{1,0:T(8,128)(2,1)}, u32[]{:S(2)}) copy-start(bf16[4096,512]{1,0:T(8,128)(2,1)} %copy-done) | copy-start | bytes 12582916
  74.4 6.6 %copy-start.4 = (bf16[4096,256]{1,0:T(8,128)(2,1)S(1)}, bf16[4096,256]{1,0:T(8,128)(2,1)}, u32[]{:S(2)}) copy-start(bf16[4096,256]{1,0:T(8,128)(2,1)} %copy-done.3) | copy-start | bytes 6291460
  74.4 7.5 %copy-start.11 = (bf16[4,2,64,512]{3,2,1,0:T(8,128)(2,1)S(1)}, bf16[4,2,64,512]{3,2,1,0:T(8,128)(2,1)}, u32[]{:S(2)}) copy-start(bf16[4,2,64,512]{3,2,1,0:T(8,128)(2,1)} %copy-done.10) | copy-start | bytes 1572868
  75.9 6.0 %collective-permute-start.4 = (bf16[64,512]{1,0:T(8,128)(2,1)S(1)}, bf16[64,512]{1,0:T(8,128)(2,1)S(1)}, u32[]{:S(2)}, u32[]{:S(2)}) collective-permute-start(bf16[64,512]{1,0:T(8,128)(2,1)S(1)} %get-tuple-element.36.own_ref), channel_id=1, source_target_pairs={{0,1},{1,0},{2,3},{3,2},{4,5},{5,4},{6,7},{7,6},{8,9},{9,8},{10,11... | collective-permute-start | bytes 196616 | tf_op jit(solution)/shard_map/ppermute | solution.py:307
  81.9 34.4 %copy-start.2 = (bf16[4096,512]{1,0:T(8,128)(2,1)S(1)}, bf16[4096,512]{1,0:T(8,128)(2,1)}, u32[]{:S(2)}) copy-start(bf16[4096,512]{1,0:T(8,128)(2,1)} %copy-done) | copy-start | bytes 12582916
  97.8 5.9 %collective-permute-start.5 = (bf16[2,64,128]{2,1,0:T(8,128)(2,1)S(1)}, bf16[2,64,128]{2,1,0:T(8,128)(2,1)S(1)}, u32[]{:S(2)}, u32[]{:S(2)}) collective-permute-start(bf16[2,64,128]{2,1,0:T(8,128)(2,1)S(1)} %back.5.refs_1_), channel_id=1, source_target_pairs={{0,32},{32,64},{64,96},{96,128},{128,160},{160,192},{192,224},{224... | collective-permute-start | bytes 98312 | tf_op jit(solution)/shard_map/ppermute | solution.py:295
  117.8 6.3 %collective-permute-start.6 = (bf16[64,512]{1,0:T(8,128)(2,1)S(1)}, bf16[64,512]{1,0:T(8,128)(2,1)S(1)}, u32[]{:S(2)}, u32[]{:S(2)}) collective-permute-start(bf16[64,512]{1,0:T(8,128)(2,1)S(1)} %get-tuple-element.40.own_ref), channel_id=1, source_target_pairs={{0,1},{1,0},{2,3},{3,2},{4,5},{5,4},{6,7},{7,6},{8,9},{9,8},{10,11... | collective-permute-start | bytes 196616 | tf_op jit(solution)/shard_map/ppermute | solution.py:307
  139.8 5.9 %collective-permute-start.7 = (bf16[2,64,128]{2,1,0:T(8,128)(2,1)S(1)}, bf16[2,64,128]{2,1,0:T(8,128)(2,1)S(1)}, u32[]{:S(2)}, u32[]{:S(2)}) collective-permute-start(bf16[2,64,128]{2,1,0:T(8,128)(2,1)S(1)} %back.6.refs_2_), channel_id=1, source_target_pairs={{0,32},{32,64},{64,96},{96,128},{128,160},{160,192},{192,224},{224... | collective-permute-start | bytes 98312 | tf_op jit(solution)/shard_map/ppermute | solution.py:295
  159.8 6.3 %collective-permute-start.8 = (bf16[64,512]{1,0:T(8,128)(2,1)S(1)}, bf16[64,512]{1,0:T(8,128)(2,1)S(1)}, u32[]{:S(2)}, u32[]{:S(2)}) collective-permute-start(bf16[64,512]{1,0:T(8,128)(2,1)S(1)} %get-tuple-element.44.own_ref), channel_id=1, source_target_pairs={{0,1},{1,0},{2,3},{3,2},{4,5},{5,4},{6,7},{7,6},{8,9},{9,8},{10,11... | collective-permute-start | bytes 196616 | tf_op jit(solution)/shard_map/ppermute | solution.py:307

commit v3 on v2

--- a/solution.py
+++ b/solution.py
@@ -15,15 +15,19 @@
 VMEM_LIMIT = 12 * 1024 * 1024
 
 
-def call(body, name, out_shape, scalars, arrays, scratch=(), anywhere=()):
+def call(body, name, out_shape, scalars, arrays, scratch=(), in_hbm=(), anywhere=(), out_specs=None):
+    arrays = [
+        pltpu.with_memory_space_constraint(array, pltpu.HBM) if place in in_hbm else array
+        for place, array in enumerate(arrays)
+    ]
     in_vmem = pl.BlockSpec(memory_space=pltpu.VMEM)
     in_smem = pl.BlockSpec(memory_space=pltpu.SMEM)
     return pl.pallas_call(
         body,
         out_shape=out_shape,
         in_specs=[in_smem] * len(scalars)
-        + [pl.BlockSpec(memory_space=pl.ANY) if place in anywhere else in_vmem for place in range(len(arrays))],
-        out_specs=jax.tree.map(lambda _: in_vmem, out_shape),
+        + [pl.BlockSpec(memory_space=pl.ANY) if place in (*in_hbm, *anywhere) else in_vmem for place in range(len(arrays))],
+        out_specs=jax.tree.map(lambda _: in_vmem, out_shape) if out_specs is None else out_specs,
         scratch_shapes=list(scratch),
         compiler_params=pltpu.CompilerParams(vmem_limit_bytes=VMEM_LIMIT),
         name=name,
@@ -34,8 +38,21 @@
     return jax.ShapeDtypeStruct(dims, jnp.bfloat16)
 
 
-def pack_first(mine_ref, later_ref, out_ref, rows_ref, spare_ref):
+def kept(*dims):
+    return pltpu.VMEM(dims, jnp.bfloat16)
+
+
+def pack_first(mine_any, later_any, out_ref, mine_ref, later_ref, rows_ref, spare_ref, sem_ref):
     _, frames, local, width = mine_ref.shape
+    copies = [
+        pltpu.make_async_copy(mine_any, mine_ref, sem_ref.at[0]),
+        pltpu.make_async_copy(later_any, later_ref, sem_ref.at[1]),
+    ]
+    for copy in copies:
+        copy.start()
+    spare_ref[...] = jnp.zeros_like(spare_ref)
+    for copy in copies:
+        copy.wait()
     group = out_ref.shape[0]
     blocks = width // HDIM
     each = local * blocks
@@ -43,7 +60,6 @@
         wide = mine_ref[0, frame].astype(jnp.float32)
         for block in range(blocks):
             rows_ref[pl.ds(frame * each + block, local, stride=blocks), :] = wide[:, block * HDIM:(block + 1) * HDIM]
-    spare_ref[...] = jnp.zeros_like(spare_ref)
     for tick in range(later_ref.shape[0]):
         for frame in range(frames):
             wide = later_ref[tick, frame].astype(jnp.float32)
@@ -65,16 +81,22 @@
     return copies
 
 
-def unpack_first(local, info_ref, came_ref, own_ref, other_ref, hidden_ref, fresh_ref, wkv_ref, wq_ref, wide_ref, sem_ref):
+def unpack_first(
+    local, info_ref, came_any, own_ref, other_ref,
+    hidden_ref, fresh_ref, wkv_ref, wq_ref, came_ref, wide_ref, came_sem, sem_ref,
+):
     group, rows, _ = came_ref.shape
     chips, halves = hidden_ref.shape[:2]
     blocks = chips * halves
     core = lax.rem(info_ref[info_ref.shape[0] - 1], CORES)
+    first_copy = pltpu.make_async_copy(came_any, came_ref, came_sem.at[0])
+    first_copy.start()
     copies = []
     for kind, (out_ref, wide, first) in enumerate(((wq_ref, HDIM, 0), (wkv_ref, 2 * HDIM, 0), (wkv_ref, 2 * HDIM, HDIM))):
         copies += side_by_side(core, wide, own_ref.at[kind], other_ref.at[kind], out_ref, sem_ref.at[kind], first)
     for copy in copies:
         copy.start()
+    first_copy.wait()
     for source in range(group):
         wide_ref[source * rows:(source + 1) * rows] = came_ref[source].astype(jnp.float32)
 
@@ -90,15 +112,6 @@
                 fresh_ref[tick, half, t * group:(t + 1) * group] = over_sources(
                     local * blocks + (tick * local + t) * halves + half
                 )
-    for copy in copies:
-        copy.wait()
-
-
-def join_out(info_ref, own_ref, other_ref, after_ref, out_ref, sem_ref):
-    core = lax.rem(info_ref[info_ref.shape[0] - 1], CORES)
-    copies = side_by_side(core, HDIM, own_ref, other_ref, out_ref, sem_ref, 0)
-    for copy in copies:
-        copy.start()
     for copy in copies:
         copy.wait()
 
@@ -140,48 +153,119 @@
     out_ref[...] = jnp.dot(xn_ref[...], w_ref[...], preferred_element_type=jnp.float32).astype(jnp.bfloat16)
 
 
-def layer_attend(tick, info_ref, q_ref, own_ref, other_ref, *refs):
-    *kv_ref, out_ref, kv_out = refs
+def live_keys(info_ref, slots, rows, tokens):
+    key_ids = lax.broadcasted_iota(jnp.int32, (1, slots * rows), 1)
+    key_slot = key_ids // rows
+    limit = jnp.zeros_like(key_ids)
+    for patch in range(slots):
+        limit = jnp.where(key_slot == patch, info_ref[patch] * tokens, limit)
+    return key_ids, key_ids - key_slot * rows < limit
+
+
+def softmax_part(queries, keys, values, live):
+    scores = lax.dot_general(
+        queries, keys, (((1,), (1,)), ((), ())), preferred_element_type=jnp.float32
+    ) / math.sqrt(HDIM)
+    scores = jnp.where(live, scores, -jnp.inf)
+    top = jnp.max(scores, axis=1, keepdims=True)
+    exponent = jnp.exp(scores - top)
+    total = jnp.sum(exponent, axis=1, keepdims=True)
+    return top, total, jnp.dot(exponent.astype(jnp.bfloat16), values, preferred_element_type=jnp.float32)
+
+
+def head_columns(half, width):
+    return slice(2 * half * width, (2 * half + 1) * width), slice((2 * half + 1) * width, (2 * half + 2) * width)
+
+
+def layer_attend_first(
+    tick, info_ref, q_ref, own_ref, other_ref, w_own_ref, w_other_ref, out_ref, kv_out, w_out_ref, sem_ref
+):
     chips, halves, tokens, width = out_ref.shape
     slots, frames = kv_out.shape[:2]
     rows = frames * tokens
     slot = slot_of(info_ref, tick)
     core = lax.rem(info_ref[slots + 1], CORES)
-    for ref in kv_ref:
-        kv_out[...] = ref[...]
-    if not kv_ref:
-        both = 2 * width
-        dims = (slots // CORES, frames, tokens, both)
-        for mine in range(CORES):
-
-            @pl.when(core == mine)
-            def _():
-                for half, ref in enumerate((own_ref, other_ref) if mine == 0 else (other_ref, own_ref)):
-                    for part in range(CORES):
-                        kv_out[part * dims[0]:(part + 1) * dims[0], :, :, half * both:(half + 1) * both] = ref[
-                            tokens:, part * both:(part + 1) * both
-                        ].reshape(dims)
+    copies = side_by_side(core, width, w_own_ref, w_other_ref, w_out_ref, sem_ref, 0)
+    for copy in copies:
+        copy.start()
+    both = 2 * width
+    dims = (slots // CORES, frames, tokens, both)
+    for mine in range(CORES):
+
+        @pl.when(core == mine)
+        def _():
+            for half, ref in enumerate((own_ref, other_ref) if mine == 0 else (other_ref, own_ref)):
+                for part in range(CORES):
+                    kv_out[part * dims[0]:(part + 1) * dims[0], :, :, half * both:(half + 1) * both] = ref[
+                        tokens:, part * both:(part + 1) * both
+                    ].reshape(dims)
 
     kv_out[slot, core] = own_ref[:tokens]
     kv_out[slot, 1 - core] = other_ref[:tokens]
-    key_ids = lax.broadcasted_iota(jnp.int32, (1, slots * rows), 1)
-    key_slot = key_ids // rows
-    limit = jnp.zeros_like(key_ids)
-    for patch in range(slots):
-        limit = jnp.where(key_slot == patch, info_ref[patch] * tokens, limit)
-    key_live = key_ids - key_slot * rows < limit
+    _, live = live_keys(info_ref, slots, rows, tokens)
     for half in range(halves):
-        queries = q_ref[:, half * width:(half + 1) * width]
-        keys = kv_out[:, :, :, 2 * half * width:(2 * half + 1) * width].reshape(slots * rows, width)
-        values = kv_out[:, :, :, (2 * half + 1) * width:(2 * half + 2) * width].reshape(slots * rows, width)
+        key_columns, value_columns = head_columns(half, width)
+        _, total, attended = softmax_part(
+            q_ref[:, half * width:(half + 1) * width],
+            kv_out[:, :, :, key_columns].reshape(slots * rows, width),
+            kv_out[:, :, :, value_columns].reshape(slots * rows, width),
+            live,
+        )
+        attended = (attended / total).astype(jnp.bfloat16)
+        for chip in range(chips):
+            out_ref[chip, half] = attended
+    for copy in copies:
+        copy.wait()
+
+
+def layer_attend_most(tick, info_ref, xn_ref, w_ref, own_ref, kv_ref, *refs):
+    *late_ref, q_ref, kv_out, acc_ref, top_ref, total_ref = refs
+    slots, frames, tokens, _ = kv_out.shape
+    rows = frames * tokens
+    width = HDIM
+    slot = slot_of(info_ref, tick)
+    core = lax.rem(info_ref[slots + 1], CORES)
+    q_ref[...] = jnp.dot(xn_ref[...], w_ref[...], preferred_element_type=jnp.float32).astype(jnp.bfloat16)
+    kv_out[...] = kv_ref[...]
+    for ref in late_ref:
+        kv_out[slot_of(info_ref, tick - 1), 1 - core] = ref[...]
+    kv_out[slot, core] = own_ref[...]
+    key_ids, live = live_keys(info_ref, slots, rows, tokens)
+    missing = slot * rows + (1 - core) * tokens
+    live = live & ((key_ids < missing) | (key_ids >= missing + tokens))
+    for half in range(acc_ref.shape[0]):
+        key_columns, value_columns = head_columns(half, width)
+        top, total, acc = softmax_part(
+            q_ref[:, half * width:(half + 1) * width],
+            kv_out[:, :, :, key_columns].reshape(slots * rows, width),
+            kv_out[:, :, :, value_columns].reshape(slots * rows, width),
+            live,
+        )
+        acc_ref[half] = acc
+        top_ref[half] = jnp.broadcast_to(top, (tokens, width))
+        total_ref[half] = jnp.broadcast_to(total, (tokens, width))
+
+
+def layer_attend_rest(tick, info_ref, q_ref, other_ref, acc_ref, top_ref, total_ref, out_ref):
+    chips, halves, tokens, width = out_ref.shape
+    core = lax.rem(info_ref[info_ref.shape[0] - 1], CORES)
+    live = 1 - core < info_ref[slot_of(info_ref, tick)]
+    for half in range(halves):
+        key_columns, value_columns = head_columns(half, width)
         scores = lax.dot_general(
-            queries, keys, (((1,), (1,)), ((), ())), preferred_element_type=jnp.float32
+            q_ref[:, half * width:(half + 1) * width], other_ref[:, key_columns], (((1,), (1,)), ((), ())),
+            preferred_element_type=jnp.float32,
         ) / math.sqrt(HDIM)
-        scores = jnp.where(key_live, scores, -jnp.inf)
-        exponent = jnp.exp(scores - jnp.max(scores, axis=1, keepdims=True))
-        row_total = jnp.sum(exponent, axis=1, keepdims=True)
-        attended = jnp.dot(exponent.astype(jnp.bfloat16), values, preferred_element_type=jnp.float32)
-        attended = (attended / row_total).astype(jnp.bfloat16)
+        scores = jnp.where(live, scores, -jnp.inf)
+        before = top_ref[half]
+        top = jnp.maximum(before, jnp.max(scores, axis=1, keepdims=True))
+        exponent = jnp.exp(scores - top[:, :1])
+        shrink = jnp.exp(before - top)
+        total = total_ref[half] * shrink + jnp.sum(exponent, axis=1, keepdims=True)
+        attended = acc_ref[half] * shrink + jnp.dot(
+            exponent.astype(jnp.bfloat16), other_ref[:, value_columns], preferred_element_type=jnp.float32
+        )
+        attended = (attended / total).astype(jnp.bfloat16)
         for chip in range(chips):
             out_ref[chip, half] = attended
 
@@ -258,7 +342,14 @@
         shape(group, owned + SPARE, HDIM),
         (),
         (in_flight, entering),
-        [pltpu.VMEM((frames * owned, HDIM), jnp.float32), pltpu.VMEM((group * SPARE, HDIM), jnp.float32)],
+        [
+            pltpu.VMEM(in_flight.shape, jnp.bfloat16),
+            pltpu.VMEM(entering.shape, jnp.bfloat16),
+            pltpu.VMEM((frames * owned, HDIM), jnp.float32),
+            pltpu.VMEM((group * SPARE, HDIM), jnp.float32),
+            pltpu.SemaphoreType.DMA((2,)),
+        ],
+        in_hbm=(0, 1),
     )
     sent, w_out_own = lax.optimization_barrier((sent, out_weight[0]))
     came = swap(sent)
@@ -270,24 +361,20 @@
         (
             shape(chips, halves, tokens, HDIM),
             shape(ticks - 1, halves, tokens, HDIM),
-            shape(width, 2 * halves * HDIM),
-            shape(width, halves * HDIM),
+            kept(width, 2 * halves * HDIM),
+            kept(width, halves * HDIM),
         ),
         (info,),
         (came, w_in, w_in_other),
-        [pltpu.VMEM((group * (owned + SPARE), HDIM), jnp.float32), pltpu.SemaphoreType.DMA((3, CORES))],
-        anywhere=(1, 2),
-    )
-    w_out = call(
-        join_out,
-        "join_out",
-        shape(width, halves * HDIM),
-        (info,),
-        (out_weight[0], w_out_other, fresh),
-        [pltpu.SemaphoreType.DMA((CORES,))],
-        anywhere=(0, 1, 2),
-    )
-
+        [
+            pltpu.VMEM(came.shape, jnp.bfloat16),
+            pltpu.VMEM((group * (owned + SPARE), HDIM), jnp.float32),
+            pltpu.SemaphoreType.DMA((1,)),
+            pltpu.SemaphoreType.DMA((3, CORES)),
+        ],
+        in_hbm=(1,),
+        anywhere=(0, 2),
+    )
     new_rows = tokens + patches * frames * tokens // CORES
     results = []
     for tick in range(ticks):
@@ -305,14 +392,38 @@
             (gathered, norm_gain, w_kv) + (() if tick else (stale,)),
         )
         other = lax.ppermute(own, "seq", partner)
-        queries = call(layer_queries, "queries", shape(tokens, halves * HDIM), (), (normed, w_q))
-        attended, kv = call(
-            functools.partial(layer_attend, tick),
-            "attend",
-            (shape(chips, halves, tokens, HDIM), shape(patches, frames, tokens, 2 * halves * HDIM)),
-            (info,),
-            (queries, own, other) + ((kv,) if tick else ()),
-        )
+        kv_dims = (patches, frames, tokens, 2 * halves * HDIM)
+        sent_dims = (chips, halves, tokens, HDIM)
+        if tick == 0:
+            queries = call(layer_queries, "queries", shape(tokens, halves * HDIM), (), (normed, w_q))
+            attended, kv, w_out = call(
+                functools.partial(layer_attend_first, tick),
+                "attend_first",
+                (shape(*sent_dims), shape(*kv_dims), kept(width, halves * HDIM)),
+                (info,),
+                (queries, own, other, out_weight[0], w_out_other),
+                [pltpu.SemaphoreType.DMA((CORES,))],
+                in_hbm=(3,),
+                anywhere=(4,),
+            )
+            late = ()
+        else:
+            per_head = jax.ShapeDtypeStruct((halves, tokens, HDIM), jnp.float32)
+            queries, kv, *part = call(
+                functools.partial(layer_attend_most, tick),
+                "attend_most",
+                (shape(tokens, halves * HDIM), shape(*kv_dims), per_head, per_head, per_head),
+                (info,),
+                (normed, w_q, own, kv) + late,
+            )
+            attended = call(
+                functools.partial(layer_attend_rest, tick),
+                "attend_rest",
+                shape(*sent_dims),
+                (info,),
+                (queries, other, *part),
+            )
+            late = (other,)
         results.append(
             call(
                 functools.partial(layer_back, tick),

time: 197 us -> 203 us (1.030)
  blocking collectives: 90.2 us -> 105 us
  waiting for transfers between devices: 29.7 us -> 23.1 us
  starting transfers between devices: 40.4 us -> 36.5 us
  Pallas kernels: 24.3 us -> 27.6 us
    all_to_all x7 -> x8, blocking collectives: 90.2 us -> 105 us  [swap(): lax.all_to_all(value, 'seq', split_axis=0, concat_axis=0, tiled=True, axi...]
    all_to_all x2 -> x1, waiting for transfers between devices: 16.8 us -> 11.2 us  [swap(): lax.all_to_all(value, 'seq', split_axis=0, concat_axis=0, tiled=True, axi...]
    pallas_call x21 -> x20, Pallas kernels: 24.3 us -> 27.6 us  [call(): pl.pallas_call(body, out_shape=out_shape, in_specs=[in_smem] * len(scalar...]
    all_to_all x2 -> x1, starting transfers between devices: 10.8 us -> 7.64 us  [swap(): lax.all_to_all(value, 'seq', split_axis=0, concat_axis=0, tiled=True, axi...]
    unnamed x31 -> x19, local copies, waits for them, and re-layouts: 9.65 us -> 8.9 us
  transfers between devices with their start and end apart: 11 -> 10, of which waited for: 9 -> 5; matrix products, arithmetic and copies ran while one was open for 1% -> 1% of each run, Pallas kernels for 5% -> 6%
where the time goes in v3:
time: 203 us; the launch traced here: 202 us
  blocking collectives  105 us (52%)
  starting transfers between devices  36.5 us (18%)
  Pallas kernels  27.6 us (14%)
  waiting for transfers between devices  23.1 us (11%)
  local copies, waits for them, and re-layouts  9.23 us (5%)
    all_to_all x8, blocking collectives, swap(): lax.all_to_all(value, 'seq', split_axis=0, concat_axis=0, tiled=True, axi...  105 us
    pallas_call x20, Pallas kernels, call(): pl.pallas_call(body, out_shape=out_shape, in_specs=[in_smem] * len(scalar...  27.6 us
    ppermute x4, starting transfers between devices, on_device(): other = lax.ppermute(own, 'seq', partner)  17.9 us
    all_to_all x1, waiting for transfers between devices, swap(): lax.all_to_all(value, 'seq', split_axis=0, concat_axis=0, tiled=True, axi...  11.2 us
    ppermute x3, waiting for transfers between devices, on_device(): lax.ppermute(results[-1], 'section', [(source, source + 1) for source in...  11.1 us
    unnamed x19, local copies, waits for them, and re-layouts  8.9 us
    all_to_all x1, starting transfers between devices, swap(): lax.all_to_all(value, 'seq', split_axis=0, concat_axis=0, tiled=True, axi...  7.64 us
    ppermute x3, starting transfers between devices, on_device(): lax.ppermute(results[-1], 'section', [(source, source + 1) for source in...  6.48 us
  transfers between devices with their start and end apart: 10, of which 5 were waited for; matrix products, arithmetic and copies ran while one was open for 1% of the time, Pallas kernels for 6%

profile of v3, /device:TPU:385, one launch (start us, length us, event | category | flops | bytes accessed | tf_op | source)
XLA Modules:
  0.0 202.1 jit_solution(16190998207050184875)
XLA Ops:
  0.0 2.6 %collective-permute-start = (bf16[3,4096,128]{2,1,0:T(8,128)(2,1)}, bf16[3,4096,128]{2,1,0:T(8,128)(2,1)S(1)}, u32[]{:S(2)}, u32[]{:S(2)}) collective-permute-start(bf16[3,4096,128]{2,1,0:T(8,128)(2,1)} %bitcast.19), channel_id=1, source_target_pairs={{0,1},{1,0},{2,3},{3,2},{4,5},{5,4},{6,7},{7,6},{8,9},{9,8},{10,11... | collective-permute-start | bytes 9437192 | tf_op jit(solution)/shard_map/ppermute | solution.py:338
  2.6 1.1 pack_first.1
  3.7 0.8 copy-done.7
  4.5 1.9 collective-permute-start.2
  6.4 7.6 %all-to-all-start = ((bf16[32,80,128]{2,1,0:T(8,128)(2,1)}), bf16[32,80,128]{2,1,0:T(8,128)(2,1)}, u32[]{:S(2)}, u32[]{:S(2)}) async-start(bf16[32,80,128]{2,1,0:T(8,128)(2,1)} %copy-done.7), calls=%async_computation | async-start | bytes 1310720 | tf_op jit(solution)/shard_map/all_to_all | solution.py:318
  14.1 1.0 copy.10
  15.1 0.7 pad_add_fusion.info_ref
  15.8 11.2 %all-to-all-done.came_any = bf16[32,80,128]{2,1,0:T(8,128)(2,1)} async-done(((bf16[32,80,128]{2,1,0:T(8,128)(2,1)}), bf16[32,80,128]{2,1,0:T(8,128)(2,1)}, u32[]{:S(2)}, u32[]{:S(2)}) %all-to-all-start) | async-done | bytes 655392 | tf_op jit(solution)/shard_map/all_to_all | solution.py:318
  27.0 1.6 copy-done.5
  28.7 1.9 copy-done.6
  30.6 2.8 %unpack_first.1 = (bf16[16,2,64,128]{3,2,1,0:T(8,128)(2,1)S(1)}, bf16[3,2,64,128]{3,2,1,0:T(8,128)(2,1)S(1)}, bf16[4096,512]{1,0:T(8,128)(2,1)S(1)}, bf16[4096,256]{1,0:T(8,128)(2,1)S(1)}) custom-call(s32[6]{0:T(128)S(1)} %pad_add_fusion.info_ref, bf16[32,80,128]{2,1,0:T(8,128)(2,1)} %all-to-all-done.came_any, bf16[3,4096,128]{2,1,0:T(8,128)(2,1)} %bitcast.20, ...), custom_call_target="tpu_custom_call" | custom-call | tf_op jit(solution)/shard_map/unpack_first/pallas_call | solution.py:25
  33.4 1.5 keys.4
  34.8 2.5 %collective-permute-start.1 = (bf16[320,512]{1,0:T(8,128)(2,1)S(1)}, bf16[320,512]{1,0:T(8,128)(2,1)S(1)}, u32[]{:S(2)}, u32[]{:S(2)}) collective-permute-start(bf16[320,512]{1,0:T(8,128)(2,1)S(1)} %get-tuple-element.41.own_ref), channel_id=1, source_target_pairs={{0,1},{1,0},{2,3},{3,2},{4,5},{5,4},{6,7},{7,6},{8,9},{9,8},{10,11... | collective-permute-start | bytes 983048 | tf_op jit(solution)/shard_map/ppermute | solution.py:394
  37.8 0.7 collective-permute-done.1.other_ref
  38.5 2.1 %attend_first.1 = (bf16[16,2,64,128]{3,2,1,0:T(8,128)(2,1)S(1)}, bf16[4,2,64,512]{3,2,1,0:T(8,128)(2,1)S(1)}, bf16[4096,256]{1,0:T(8,128)(2,1)S(1)}) custom-call(s32[6]{0:T(128)S(1)} %pad_add_fusion.info_ref, bf16[64,256]{1,0:T(8,128)(2,1)S(1)} %queries.1.q_ref, bf16[320,512]{1,0:T(8,128)(2,1)S(1)} %get-tuple-element.41.own_ref, ...), custom_call_target="tpu_custom_call" | custom-call | tf_op jit(solution)/shard_map/attend_first/pallas_call | solution.py:25
  40.7 13.9 %all_to_all.45.a_ref = bf16[16,2,64,128]{3,2,1,0:T(8,128)(2,1)S(1)} all-to-all(bf16[16,2,64,128]{3,2,1,0:T(8,128)(2,1)S(1)} %get-tuple-element.43), channel_id=1, replica_groups={{0,2,4,6,8,10,12,14,16,18,20,22,24,26,28,30},{1,3,5,7,9,11,13,15,17,19,..., dimensions={0} | all-to-all | bytes 1048576 | tf_op jit(solution)/shard_map/all_to_all | solution.py:318
  54.5 1.1 back.4.refs_0_
  55.6 1.3 copy-done.3
  57.0 2.6 %collective-permute-start.3 = (bf16[2,64,128]{2,1,0:T(8,128)(2,1)S(1)}, bf16[2,64,128]{2,1,0:T(8,128)(2,1)S(1)}, u32[]{:S(2)}, u32[]{:S(2)}) collective-permute-start(bf16[2,64,128]{2,1,0:T(8,128)(2,1)S(1)} %back.4.refs_0_), channel_id=1, source_target_pairs={{0,32},{32,64},{64,96},{96,128},{128,160},{160,192},{192,224},{224... | collective-permute-start | bytes 98312 | tf_op jit(solution)/shard_map/ppermute | solution.py:382
  59.6 3.2 %collective-permute-done.3 = bf16[2,64,128]{2,1,0:T(8,128)(2,1)S(1)} collective-permute-done((bf16[2,64,128]{2,1,0:T(8,128)(2,1)S(1)}, bf16[2,64,128]{2,1,0:T(8,128)(2,1)S(1)}, u32[]{:S(2)}, u32[]{:S(2)}) %collective-permute-start.3) | collective-permute-done | bytes 32800 | tf_op jit(solution)/shard_map/ppermute | solution.py:382
  63.0 12.4 %all_to_all.46.x_ref = bf16[16,2,64,128]{3,2,1,0:T(8,128)(2,1)S(1)} all-to-all(bf16[16,2,64,128]{3,2,1,0:T(8,128)(2,1)S(1)} %broadcast_in_dim.8), channel_id=1, replica_groups={{0,2,4,6,8,10,12,14,16,18,20,22,24,26,28,30},{1,3,5,7,9,11,13,15,17,19,..., dimensions={0} | all-to-all | bytes 1048576 | tf_op jit(solution)/shard_map/all_to_all | solution.py:318
  75.3 2.2 %copy-done.1 = bf16[4096,512]{1,0:T(8,128)(2,1)S(1)} copy-done((bf16[4096,512]{1,0:T(8,128)(2,1)S(1)}, bf16[4096,512]{1,0:T(8,128)(2,1)}, u32[]{:S(2)}) %copy-start.1) | copy-done | bytes 4194328
  77.5 1.5 keys.5
  79.0 5.3 %collective-permute-start.4 = (bf16[64,512]{1,0:T(8,128)(2,1)S(1)}, bf16[64,512]{1,0:T(8,128)(2,1)S(1)}, u32[]{:S(2)}, u32[]{:S(2)}) collective-permute-start(bf16[64,512]{1,0:T(8,128)(2,1)S(1)} %get-tuple-element.47.own_ref), channel_id=1, source_target_pairs={{0,1},{1,0},{2,3},{3,2},{4,5},{5,4},{6,7},{7,6},{8,9},{9,8},{10,11... | collective-permute-start | bytes 196616 | tf_op jit(solution)/shard_map/ppermute | solution.py:394
  84.3 1.8 attend_most.3
  86.1 1.3 attend_rest.3
  87.4 14.1 %all_to_all.47.a_ref = bf16[16,2,64,128]{3,2,1,0:T(8,128)(2,1)S(1)} all-to-all(bf16[16,2,64,128]{3,2,1,0:T(8,128)(2,1)S(1)} %attend_rest.3), channel_id=1, replica_groups={{0,2,4,6,8,10,12,14,16,18,20,22,24,26,28,30},{1,3,5,7,9,11,13,15,17,19,..., dimensions={0} | all-to-all | bytes 1048576 | tf_op jit(solution)/shard_map/all_to_all | solution.py:318
  101.4 1.1 back.5.refs_1_
  102.5 1.9 collective-permute-start.5
  104.5 3.9 %collective-permute-done.5 = bf16[2,64,128]{2,1,0:T(8,128)(2,1)S(1)} collective-permute-done((bf16[2,64,128]{2,1,0:T(8,128)(2,1)S(1)}, bf16[2,64,128]{2,1,0:T(8,128)(2,1)S(1)}, u32[]{:S(2)}, u32[]{:S(2)}) %collective-permute-start.5) | collective-permute-done | bytes 32800 | tf_op jit(solution)/shard_map/ppermute | solution.py:382
  108.5 12.4 %all_to_all.48.x_ref = bf16[16,2,64,128]{3,2,1,0:T(8,128)(2,1)S(1)} all-to-all(bf16[16,2,64,128]{3,2,1,0:T(8,128)(2,1)S(1)} %broadcast_in_dim.9), channel_id=1, replica_groups={{0,2,4,6,8,10,12,14,16,18,20,22,24,26,28,30},{1,3,5,7,9,11,13,15,17,19,..., dimensions={0} | all-to-all | bytes 1048576 | tf_op jit(solution)/shard_map/all_to_all | solution.py:318
  120.9 1.5 keys.6
  122.4 5.1 %collective-permute-start.6 = (bf16[64,512]{1,0:T(8,128)(2,1)S(1)}, bf16[64,512]{1,0:T(8,128)(2,1)S(1)}, u32[]{:S(2)}, u32[]{:S(2)}) collective-permute-start(bf16[64,512]{1,0:T(8,128)(2,1)S(1)} %get-tuple-element.54.own_ref), channel_id=1, source_target_pairs={{0,1},{1,0},{2,3},{3,2},{4,5},{5,4},{6,7},{7,6},{8,9},{9,8},{10,11... | collective-permute-start | bytes 196616 | tf_op jit(solution)/shard_map/ppermute | solution.py:394
  127.5 1.8 attend_most.4
  129.3 1.3 attend_rest.4
  130.5 13.8 %all_to_all.49.a_ref = bf16[16,2,64,128]{3,2,1,0:T(8,128)(2,1)S(1)} all-to-all(bf16[16,2,64,128]{3,2,1,0:T(8,128)(2,1)S(1)} %attend_rest.4), channel_id=1, replica_groups={{0,2,4,6,8,10,12,14,16,18,20,22,24,26,28,30},{1,3,5,7,9,11,13,15,17,19,..., dimensions={0} | all-to-all | bytes 1048576 | tf_op jit(solution)/shard_map/all_to_all | solution.py:318
  144.4 1.1 back.6.refs_2_
  145.4 1.9 collective-permute-start.7
  147.4 3.9 %collective-permute-done.7 = bf16[2,64,128]{2,1,0:T(8,128)(2,1)S(1)} collective-permute-done((bf16[2,64,128]{2,1,0:T(8,128)(2,1)S(1)}, bf16[2,64,128]{2,1,0:T(8,128)(2,1)S(1)}, u32[]{:S(2)}, u32[]{:S(2)}) %collective-permute-start.7) | collective-permute-done | bytes 32800 | tf_op jit(solution)/shard_map/ppermute | solution.py:382
  151.4 12.4 %all_to_all.50.x_ref = bf16[16,2,64,128]{3,2,1,0:T(8,128)(2,1)S(1)} all-to-all(bf16[16,2,64,128]{3,2,1,0:T(8,128)(2,1)S(1)} %broadcast_in_dim.10), channel_id=1, replica_groups={{0,2,4,6,8,10,12,14,16,18,20,22,24,26,28,30},{1,3,5,7,9,11,13,15,17,19,..., dimensions={0} | all-to-all | bytes 1048576 | tf_op jit(solution)/shard_map/all_to_all | solution.py:318
  163.8 1.5 keys.7
  165.3 5.1 %collective-permute-start.8 = (bf16[64,512]{1,0:T(8,128)(2,1)S(1)}, bf16[64,512]{1,0:T(8,128)(2,1)S(1)}, u32[]{:S(2)}, u32[]{:S(2)}) collective-permute-start(bf16[64,512]{1,0:T(8,128)(2,1)S(1)} %get-tuple-element.61.own_ref), channel_id=1, source_target_pairs={{0,1},{1,0},{2,3},{3,2},{4,5},{5,4},{6,7},{7,6},{8,9},{9,8},{10,11... | collective-permute-start | bytes 196616 | tf_op jit(solution)/shard_map/ppermute | solution.py:394
  170.4 2.2 %attend_most.5 = (bf16[64,256]{1,0:T(8,128)(2,1)S(1)}, bf16[4,2,64,512]{3,2,1,0:T(8,128)(2,1)}, f32[2,64,128]{2,1,0:T(8,128)S(1)}, f32[2,64,128]{2,1,0:T(8,128)S(1)}, f32[2,64,128]{2,1,0:T(8,128)S(1)}) custom-call(s32[6]{0:T(128)S(1)} %pad_add_fusion.info_ref, bf16[64,4096]{1,0:T(8,128)(2,1)S(1)} %get-tuple-element.60.xn_ref, ...), custom_call_target="tpu_custom_call" | custom-call | tf_op jit(solution)/shard_map/attend_most/pallas_call | solution.py:25
  172.6 1.3 attend_rest.5
  173.8 13.8 %all_to_all.51.a_ref = bf16[16,2,64,128]{3,2,1,0:T(8,128)(2,1)S(1)} all-to-all(bf16[16,2,64,128]{3,2,1,0:T(8,128)(2,1)S(1)} %attend_rest.5), channel_id=1, replica_groups={{0,2,4,6,8,10,12,14,16,18,20,22,24,26,28,30},{1,3,5,7,9,11,13,15,17,19,..., dimensions={0} | all-to-all | bytes 1048576 | tf_op jit(solution)/shard_map/all_to_all | solution.py:318
  187.6 1.1 back.7.refs_3_
  188.9 12.0 %all_to_all.52.came_ref = bf16[32,16,128]{2,1,0:T(8,128)(2,1)S(1)} all-to-all(bf16[32,16,128]{2,1,0:T(8,128)(2,1)S(1)} %pack_last.1), channel_id=1, replica_groups=mesh['section'=16,'seq'=32] {'seq'}, dimensions={0} | all-to-all | bytes 262144 | tf_op jit(solution)/shard_map/all_to_all | solution.py:318
  200.8 1.3 unpack_last.1
  (26 shorter events, 1.0 us)
Async XLA Ops:
  0.0 27.0 %collective-permute-start = (bf16[3,4096,128]{2,1,0:T(8,128)(2,1)}, bf16[3,4096,128]{2,1,0:T(8,128)(2,1)S(1)}, u32[]{:S(2)}, u32[]{:S(2)}) collective-permute-start(bf16[3,4096,128]{2,1,0:T(8,128)(2,1)} %bitcast.19), channel_id=1, source_target_pairs={{0,1},{1,0},{2,3},{3,2},{4,5},{5,4},{6,7},{7,6},{8,9},{9,8},{10,11... | collective-permute-start | bytes 9437192 | tf_op jit(solution)/shard_map/ppermute | solution.py:338
  3.7 0.8 copy-start.7
  4.5 33.3 %collective-permute-start.2 = (bf16[4096,128]{1,0:T(8,128)(2,1)}, bf16[4096,128]{1,0:T(8,128)(2,1)}, u32[]{:S(2)}, u32[]{:S(2)}) collective-permute-start(bf16[4096,128]{1,0:T(8,128)(2,1)} %bitcast.21), channel_id=1, source_target_pairs={{0,1},{1,0},{2,3},{3,2},{4,5},{5,4},{6,7},{7,6},{8,9},{9,8},{10,11... | collective-permute-start | bytes 3145736 | tf_op jit(solution)/shard_map/ppermute | solution.py:356
  6.4 20.6 %all-to-all-start = ((bf16[32,80,128]{2,1,0:T(8,128)(2,1)}), bf16[32,80,128]{2,1,0:T(8,128)(2,1)}, u32[]{:S(2)}, u32[]{:S(2)}) async-start(bf16[32,80,128]{2,1,0:T(8,128)(2,1)} %copy-done.7), calls=%async_computation | async-start | bytes 1310720 | tf_op jit(solution)/shard_map/all_to_all | solution.py:318
  27.0 1.6 copy-start.5
  28.7 1.9 copy-start.6
  30.6 2.8 %copy-start.8 = (bf16[1,4096]{1,0:T(2,128)(2,1)S(1)}, bf16[1,4096]{1,0:T(2,128)(2,1)}, u32[]{:S(2)}) copy-start(bf16[1,4096]{1,0:T(2,128)(2,1)} %gain_ref.7) | copy-start | bytes 24580
  33.3 4.5 %copy-start = (bf16[4096,512]{1,0:T(8,128)(2,1)}, bf16[4096,512]{1,0:T(8,128)(2,1)S(1)}, u32[]{:S(2)}) copy-start(bf16[4096,512]{1,0:T(8,128)(2,1)S(1)} %get-tuple-element.38.w_ref) | copy-start | bytes 12582916
  34.8 3.7 %collective-permute-start.1 = (bf16[320,512]{1,0:T(8,128)(2,1)S(1)}, bf16[320,512]{1,0:T(8,128)(2,1)S(1)}, u32[]{:S(2)}, u32[]{:S(2)}) collective-permute-start(bf16[320,512]{1,0:T(8,128)(2,1)S(1)} %get-tuple-element.41.own_ref), channel_id=1, source_target_pairs={{0,1},{1,0},{2,3},{3,2},{4,5},{5,4},{6,7},{7,6},{8,9},{9,8},{10,11... | collective-permute-start | bytes 983048 | tf_op jit(solution)/shard_map/ppermute | solution.py:394
  55.6 1.4 copy-start.3
  57.0 5.9 %collective-permute-start.3 = (bf16[2,64,128]{2,1,0:T(8,128)(2,1)S(1)}, bf16[2,64,128]{2,1,0:T(8,128)(2,1)S(1)}, u32[]{:S(2)}, u32[]{:S(2)}) collective-permute-start(bf16[2,64,128]{2,1,0:T(8,128)(2,1)S(1)} %back.4.refs_0_), channel_id=1, source_target_pairs={{0,32},{32,64},{64,96},{96,128},{128,160},{160,192},{192,224},{224... | collective-permute-start | bytes 98312 | tf_op jit(solution)/shard_map/ppermute | solution.py:382
  75.3 2.2 %copy-start.1 = (bf16[4096,512]{1,0:T(8,128)(2,1)S(1)}, bf16[4096,512]{1,0:T(8,128)(2,1)}, u32[]{:S(2)}) copy-start(bf16[4096,512]{1,0:T(8,128)(2,1)} %copy-done) | copy-start | bytes 12582916
  79.0 22.4 %copy-start.4 = (bf16[4096,256]{1,0:T(8,128)(2,1)S(1)}, bf16[4096,256]{1,0:T(8,128)(2,1)}, u32[]{:S(2)}) copy-start(bf16[4096,256]{1,0:T(8,128)(2,1)} %copy-done.3) | copy-start | bytes 6291460
  79.0 7.1 %collective-permute-start.4 = (bf16[64,512]{1,0:T(8,128)(2,1)S(1)}, bf16[64,512]{1,0:T(8,128)(2,1)S(1)}, u32[]{:S(2)}, u32[]{:S(2)}) collective-permute-start(bf16[64,512]{1,0:T(8,128)(2,1)S(1)} %get-tuple-element.47.own_ref), channel_id=1, source_target_pairs={{0,1},{1,0},{2,3},{3,2},{4,5},{5,4},{6,7},{7,6},{8,9},{9,8},{10,11... | collective-permute-start | bytes 196616 | tf_op jit(solution)/shard_map/ppermute | solution.py:394
  87.4 33.5 %copy-start.2 = (bf16[4096,512]{1,0:T(8,128)(2,1)S(1)}, bf16[4096,512]{1,0:T(8,128)(2,1)}, u32[]{:S(2)}) copy-start(bf16[4096,512]{1,0:T(8,128)(2,1)} %copy-done) | copy-start | bytes 12582916
  102.5 5.9 %collective-permute-start.5 = (bf16[2,64,128]{2,1,0:T(8,128)(2,1)S(1)}, bf16[2,64,128]{2,1,0:T(8,128)(2,1)S(1)}, u32[]{:S(2)}, u32[]{:S(2)}) collective-permute-start(bf16[2,64,128]{2,1,0:T(8,128)(2,1)S(1)} %back.5.refs_1_), channel_id=1, source_target_pairs={{0,32},{32,64},{64,96},{96,128},{128,160},{160,192},{192,224},{224... | collective-permute-start | bytes 98312 | tf_op jit(solution)/shard_map/ppermute | solution.py:382
  122.4 6.9 %collective-permute-start.6 = (bf16[64,512]{1,0:T(8,128)(2,1)S(1)}, bf16[64,512]{1,0:T(8,128)(2,1)S(1)}, u32[]{:S(2)}, u32[]{:S(2)}) collective-permute-start(bf16[64,512]{1,0:T(8,128)(2,1)S(1)} %get-tuple-element.54.own_ref), channel_id=1, source_target_pairs={{0,1},{1,0},{2,3},{3,2},{4,5},{5,4},{6,7},{7,6},{8,9},{9,8},{10,11... | collective-permute-start | bytes 196616 | tf_op jit(solution)/shard_map/ppermute | solution.py:394
  145.4 5.9 %collective-permute-start.7 = (bf16[2,64,128]{2,1,0:T(8,128)(2,1)S(1)}, bf16[2,64,128]{2,1,0:T(8,128)(2,1)S(1)}, u32[]{:S(2)}, u32[]{:S(2)}) collective-permute-start(bf16[2,64,128]{2,1,0:T(8,128)(2,1)S(1)} %back.6.refs_2_), channel_id=1, source_target_pairs={{0,32},{32,64},{64,96},{96,128},{128,160},{160,192},{192,224},{224... | collective-permute-start | bytes 98312 | tf_op jit(solution)/shard_map/ppermute | solution.py:382
  165.3 7.3 %collective-permute-start.8 = (bf16[64,512]{1,0:T(8,128)(2,1)S(1)}, bf16[64,512]{1,0:T(8,128)(2,1)S(1)}, u32[]{:S(2)}, u32[]{:S(2)}) collective-permute-start(bf16[64,512]{1,0:T(8,128)(2,1)S(1)} %get-tuple-element.61.own_ref), channel_id=1, source_target_pairs={{0,1},{1,0},{2,3},{3,2},{4,5},{5,4},{6,7},{7,6},{8,9},{9,8},{10,11... | collective-permute-start | bytes 196616 | tf_op jit(solution)/shard_map/ppermute | solution.py:394

commit v4 on v2

--- a/solution.py
+++ b/solution.py
@@ -10,19 +10,24 @@
 
 HDIM = 128
 CORES = 2
+WEIGHT_PARTS = 4
 MOST_SECTIONS = 1024
 SPARE = 16
 VMEM_LIMIT = 12 * 1024 * 1024
 
 
-def call(body, name, out_shape, scalars, arrays, scratch=(), anywhere=()):
+def call(body, name, out_shape, scalars, arrays, scratch=(), in_hbm=(), anywhere=()):
+    arrays = [
+        pltpu.with_memory_space_constraint(array, pltpu.HBM) if place in in_hbm else array
+        for place, array in enumerate(arrays)
+    ]
     in_vmem = pl.BlockSpec(memory_space=pltpu.VMEM)
     in_smem = pl.BlockSpec(memory_space=pltpu.SMEM)
     return pl.pallas_call(
         body,
         out_shape=out_shape,
         in_specs=[in_smem] * len(scalars)
-        + [pl.BlockSpec(memory_space=pl.ANY) if place in anywhere else in_vmem for place in range(len(arrays))],
+        + [pl.BlockSpec(memory_space=pl.ANY) if place in (*in_hbm, *anywhere) else in_vmem for place in range(len(arrays))],
         out_specs=jax.tree.map(lambda _: in_vmem, out_shape),
         scratch_shapes=list(scratch),
         compiler_params=pltpu.CompilerParams(vmem_limit_bytes=VMEM_LIMIT),
@@ -34,8 +39,17 @@
     return jax.ShapeDtypeStruct(dims, jnp.bfloat16)
 
 
-def pack_first(mine_ref, later_ref, out_ref, rows_ref, spare_ref):
+def pack_first(mine_any, later_any, ready_any, out_ref, mine_ref, later_ref, rows_ref, spare_ref, sem_ref):
     _, frames, local, width = mine_ref.shape
+    copies = [
+        pltpu.make_async_copy(mine_any, mine_ref, sem_ref.at[0]),
+        pltpu.make_async_copy(later_any, later_ref, sem_ref.at[1]),
+    ]
+    for copy in copies:
+        copy.start()
+    spare_ref[...] = jnp.zeros_like(spare_ref)
+    for copy in copies:
+        copy.wait()
     group = out_ref.shape[0]
     blocks = width // HDIM
     each = local * blocks
@@ -43,7 +57,6 @@
         wide = mine_ref[0, frame].astype(jnp.float32)
         for block in range(blocks):
             rows_ref[pl.ds(frame * each + block, local, stride=blocks), :] = wide[:, block * HDIM:(block + 1) * HDIM]
-    spare_ref[...] = jnp.zeros_like(spare_ref)
     for tick in range(later_ref.shape[0]):
         for frame in range(frames):
             wide = later_ref[tick, frame].astype(jnp.float32)
@@ -65,16 +78,21 @@
     return copies
 
 
-def unpack_first(local, info_ref, came_ref, own_ref, other_ref, hidden_ref, fresh_ref, wkv_ref, wq_ref, wide_ref, sem_ref):
+def unpack_first(
+    local, came_any, own_ref, other_ref, hidden_ref, fresh_ref, wkv_ref, wq_ref, came_ref, wide_ref, came_sem, sem_ref
+):
     group, rows, _ = came_ref.shape
     chips, halves = hidden_ref.shape[:2]
     blocks = chips * halves
-    core = lax.rem(info_ref[info_ref.shape[0] - 1], CORES)
+    core = own_core()
+    first_copy = pltpu.make_async_copy(came_any, came_ref, came_sem.at[0])
+    first_copy.start()
     copies = []
     for kind, (out_ref, wide, first) in enumerate(((wq_ref, HDIM, 0), (wkv_ref, 2 * HDIM, 0), (wkv_ref, 2 * HDIM, HDIM))):
         copies += side_by_side(core, wide, own_ref.at[kind], other_ref.at[kind], out_ref, sem_ref.at[kind], first)
     for copy in copies:
         copy.start()
+    first_copy.wait()
     for source in range(group):
         wide_ref[source * rows:(source + 1) * rows] = came_ref[source].astype(jnp.float32)
 
@@ -94,27 +112,41 @@
         copy.wait()
 
 
-def join_out(info_ref, own_ref, other_ref, after_ref, out_ref, sem_ref):
-    core = lax.rem(info_ref[info_ref.shape[0] - 1], CORES)
-    copies = side_by_side(core, HDIM, own_ref, other_ref, out_ref, sem_ref, 0)
-    for copy in copies:
-        copy.start()
-    for copy in copies:
-        copy.wait()
-
-
-def slot_of(info_ref, tick):
-    slots = info_ref.shape[0] - 2
-    return lax.rem(tick + slots * MOST_SECTIONS - info_ref[slots], slots)
-
-
-def core_live(info_ref, tick):
-    core = lax.rem(info_ref[info_ref.shape[0] - 1], CORES)
-    return core < info_ref[slot_of(info_ref, tick)]
-
-
-def layer_keys(tick, info_ref, x_ref, gain_ref, w_ref, *refs):
-    *stale_ref, xn_ref, new_ref = refs
+def slot_of(frames_ref, tick):
+    slots = frames_ref.shape[0]
+    return lax.rem(tick + slots * MOST_SECTIONS - lax.axis_index("section"), slots)
+
+
+def own_core():
+    return lax.rem(lax.axis_index("seq"), CORES)
+
+
+def core_live(frames_ref, tick):
+    return own_core() < frames_ref[slot_of(frames_ref, tick)]
+
+
+def first_rows(tokens, slot_rows, width):
+    stale = tokens + slot_rows // CORES
+    return stale, stale + width // WEIGHT_PARTS
+
+
+def layer_keys(tick, frames_ref, x_ref, gain_ref, w_ref, *refs):
+    *first_refs, xn_ref, new_ref = refs if tick else refs[:-1]
+    copies = []
+    if tick == 0:
+        stale_ref, out_any = first_refs
+        sem_ref = refs[-1]
+        stale_end, weight_end = first_rows(x_ref.shape[2], stale_ref.shape[0], out_any.shape[0])
+        part_rows = weight_end - stale_end
+        for part in range(WEIGHT_PARTS):
+            copies.append(
+                pltpu.make_async_copy(
+                    out_any.at[part * part_rows:(part + 1) * part_rows],
+                    new_ref.at[stale_end:weight_end, part * HDIM:(part + 1) * HDIM],
+                    sem_ref.at[part],
+                )
+            )
+            copies[-1].start()
     chips, halves, tokens, width = x_ref.shape
     squares = jnp.zeros((tokens, width), jnp.float32)
     for chip in range(chips):
@@ -122,7 +154,7 @@
             wide = x_ref[chip, half].astype(jnp.float32)
             squares = squares + wide * wide
     mean_square = jnp.sum(squares, axis=1, keepdims=True) / (chips * halves * width)
-    scale = jnp.where(core_live(info_ref, tick), lax.rsqrt(mean_square + 1e-06), 0.0)
+    scale = jnp.where(core_live(frames_ref, tick), lax.rsqrt(mean_square + 1e-06), 0.0)
     for chip in range(chips):
         for half in range(halves):
             first = (chip * halves + half) * width
@@ -130,27 +162,40 @@
             normed = wide * scale * gain_ref[:, first:first + width].astype(jnp.float32)
             xn_ref[:, first:first + width] = normed.astype(jnp.bfloat16)
     new_ref[:tokens] = jnp.dot(xn_ref[...], w_ref[...], preferred_element_type=jnp.float32).astype(jnp.bfloat16)
-    for ref in stale_ref:
-        rows, both = ref.shape
+    if tick == 0:
+        rows, both = stale_ref.shape
         for part in range(CORES):
-            new_ref[tokens:, part * both:(part + 1) * both] = ref[part * rows // CORES:(part + 1) * rows // CORES]
+            new_ref[tokens:stale_end, part * both:(part + 1) * both] = stale_ref[
+                part * rows // CORES:(part + 1) * rows // CORES
+            ]
+        for copy in copies:
+            copy.wait()
 
 
 def layer_queries(xn_ref, w_ref, out_ref):
     out_ref[...] = jnp.dot(xn_ref[...], w_ref[...], preferred_element_type=jnp.float32).astype(jnp.bfloat16)
 
 
-def layer_attend(tick, info_ref, q_ref, own_ref, other_ref, *refs):
-    *kv_ref, out_ref, kv_out = refs
+def layer_attend(tick, frames_ref, q_ref, own_ref, other_ref, *refs):
+    *kv_ref, out_ref, kv_out = refs if tick else refs[:2]
     chips, halves, tokens, width = out_ref.shape
     slots, frames = kv_out.shape[:2]
     rows = frames * tokens
-    slot = slot_of(info_ref, tick)
-    core = lax.rem(info_ref[slots + 1], CORES)
+    slot = slot_of(frames_ref, tick)
+    core = own_core()
     for ref in kv_ref:
         kv_out[...] = ref[...]
-    if not kv_ref:
+    copies = []
+    if tick == 0:
+        w_out_ref, sem_ref = refs[2:]
         both = 2 * width
+        stale_end, weight_end = first_rows(tokens, slots * rows, w_out_ref.shape[0])
+        for part in range(WEIGHT_PARTS):
+            source = (slice(stale_end, weight_end), slice(part * width, (part + 1) * width))
+            target = w_out_ref.at[part * (weight_end - stale_end):(part + 1) * (weight_end - stale_end)]
+            copies += side_by_side(core, width, own_ref.at[source], other_ref.at[source], target, sem_ref.at[part], 0)
+        for copy in copies:
+            copy.start()
         dims = (slots // CORES, frames, tokens, both)
         for mine in range(CORES):
 
@@ -159,7 +204,7 @@
                 for half, ref in enumerate((own_ref, other_ref) if mine == 0 else (other_ref, own_ref)):
                     for part in range(CORES):
                         kv_out[part * dims[0]:(part + 1) * dims[0], :, :, half * both:(half + 1) * both] = ref[
-                            tokens:, part * both:(part + 1) * both
+                            tokens:stale_end, part * both:(part + 1) * both
                         ].reshape(dims)
 
     kv_out[slot, core] = own_ref[:tokens]
@@ -168,7 +213,7 @@
     key_slot = key_ids // rows
     limit = jnp.zeros_like(key_ids)
     for patch in range(slots):
-        limit = jnp.where(key_slot == patch, info_ref[patch] * tokens, limit)
+        limit = jnp.where(key_slot == patch, frames_ref[patch] * tokens, limit)
     key_live = key_ids - key_slot * rows < limit
     for half in range(halves):
         queries = q_ref[:, half * width:(half + 1) * width]
@@ -184,12 +229,20 @@
         attended = (attended / row_total).astype(jnp.bfloat16)
         for chip in range(chips):
             out_ref[chip, half] = attended
-
-
-def layer_back(tick, info_ref, a_ref, w_ref, x_ref, out_ref, wide_ref):
+    for copy in copies:
+        copy.wait()
+
+
+def spread(tick, fresh_ref, arrived_ref, out_ref):
+    rows = jnp.where(lax.axis_index("section") == 0, fresh_ref[tick - 1], arrived_ref[...])
+    for chip in range(out_ref.shape[0]):
+        out_ref[chip] = rows
+
+
+def layer_back(tick, frames_ref, a_ref, w_ref, x_ref, out_ref, wide_ref):
     chips, halves, tokens, width = a_ref.shape
-    chip = lax.div(info_ref[info_ref.shape[0] - 1], CORES)
-    live = core_live(info_ref, tick)
+    chip = lax.div(lax.axis_index("seq"), CORES)
+    live = core_live(frames_ref, tick)
     for source in range(chips):
         for half in range(halves):
             first = (source * halves + half) * width
@@ -213,7 +266,7 @@
         out_ref[target] = wide_ref[pl.ds(target, parts, stride=group), :].astype(jnp.bfloat16)
 
 
-def unpack_last(info_ref, came_ref, out_ref, turn_ref):
+def unpack_last(frames_ref, came_ref, out_ref, turn_ref):
     group, parts, width = came_ref.shape
     patches, frames, local, _ = out_ref.shape
     each = parts // CORES
@@ -224,7 +277,7 @@
             first = (chip * CORES + half) * width
             turn_ref[frame * each:(frame + 1) * each, first:first + width] = wide[half * each:(half + 1) * each]
     for tick in range(patches):
-        slot = slot_of(info_ref, tick)
+        slot = slot_of(frames_ref, tick)
         for frame in range(frames):
             row = frame * each + tick * local
             out_ref[slot, frame] = turn_ref[row:row + local].astype(jnp.bfloat16)
@@ -235,9 +288,7 @@
 
 
 def on_device(in_flight, entering, patch_frames, norm_gain, qkv_weight, out_weight, stale_kv):
-    section = lax.axis_index("section")
     sections = lax.axis_size("section")
-    me = lax.axis_index("seq")
     group = lax.axis_size("seq")
     patches, frames, tokens = stale_kv.shape[1:4]
     local = in_flight.shape[2]
@@ -248,22 +299,27 @@
     owned = local * group
     same_core = [[CORES * chip + core for chip in range(chips)] for core in range(CORES)]
     partner = [(device, device ^ 1) for device in range(group)]
-    info = jnp.concatenate([patch_frames, jnp.stack([section, me]).astype(jnp.int32)])
 
     w_in = jnp.transpose(qkv_weight[0], (1, 0, 2))
     w_in_other = lax.ppermute(w_in, "seq", partner)
+    stale = stale_kv[0].reshape(patches * frames * tokens, 2 * HDIM)
     sent = call(
         pack_first,
         "pack_first",
         shape(group, owned + SPARE, HDIM),
         (),
-        (in_flight, entering),
-        [pltpu.VMEM((frames * owned, HDIM), jnp.float32), pltpu.VMEM((group * SPARE, HDIM), jnp.float32)],
-    )
-    sent, w_out_own = lax.optimization_barrier((sent, out_weight[0]))
+        (in_flight, entering, stale),
+        [
+            pltpu.VMEM(in_flight.shape, jnp.bfloat16),
+            pltpu.VMEM(entering.shape, jnp.bfloat16),
+            pltpu.VMEM((frames * owned, HDIM), jnp.float32),
+            pltpu.VMEM((group * SPARE, HDIM), jnp.float32),
+            pltpu.SemaphoreType.DMA((2,)),
+        ],
+        in_hbm=(0, 1),
+        anywhere=(2,),
+    )
     came = swap(sent)
-    w_out_other = lax.ppermute(w_out_own, "seq", partner)
-    stale = stale_kv[0].reshape(patches * frames * tokens, 2 * HDIM)
     gathered, fresh, w_kv, w_q = call(
         functools.partial(unpack_first, local),
         "unpack_first",
@@ -273,52 +329,56 @@
             shape(width, 2 * halves * HDIM),
             shape(width, halves * HDIM),
         ),
-        (info,),
+        (),
         (came, w_in, w_in_other),
-        [pltpu.VMEM((group * (owned + SPARE), HDIM), jnp.float32), pltpu.SemaphoreType.DMA((3, CORES))],
-        anywhere=(1, 2),
-    )
-    w_out = call(
-        join_out,
-        "join_out",
-        shape(width, halves * HDIM),
-        (info,),
-        (out_weight[0], w_out_other, fresh),
-        [pltpu.SemaphoreType.DMA((CORES,))],
-        anywhere=(0, 1, 2),
-    )
-
-    new_rows = tokens + patches * frames * tokens // CORES
+        [
+            pltpu.VMEM(came.shape, jnp.bfloat16),
+            pltpu.VMEM((group * (owned + SPARE), HDIM), jnp.float32),
+            pltpu.SemaphoreType.DMA((1,)),
+            pltpu.SemaphoreType.DMA((3, CORES)),
+        ],
+        in_hbm=(1,),
+        anywhere=(0, 2),
+    )
     results = []
     for tick in range(ticks):
         if tick:
             arrived = lax.ppermute(
                 results[-1], "section", [(source, source + 1) for source in range(sections - 1)]
             )
-            arrived = jnp.where(section == 0, fresh[tick - 1], arrived)
-            gathered = swap(jnp.broadcast_to(arrived[None], (chips,) + arrived.shape), same_core)
+            gathered = call(
+                functools.partial(spread, tick), "spread", shape(chips, halves, tokens, HDIM), (), (fresh, arrived)
+            )
+            gathered = swap(gathered, same_core)
+        new_rows = tokens if tick else first_rows(tokens, stale.shape[0], width)[1]
         normed, own = call(
             functools.partial(layer_keys, tick),
             "keys",
-            (shape(tokens, width), shape(tokens if tick else new_rows, 2 * halves * HDIM)),
-            (info,),
-            (gathered, norm_gain, w_kv) + (() if tick else (stale,)),
+            (shape(tokens, width), shape(new_rows, 2 * halves * HDIM)),
+            (patch_frames,),
+            (gathered, norm_gain, w_kv) + (() if tick else (stale, out_weight[0])),
+            () if tick else [pltpu.SemaphoreType.DMA((WEIGHT_PARTS,))],
+            in_hbm=() if tick else (4,),
         )
         other = lax.ppermute(own, "seq", partner)
         queries = call(layer_queries, "queries", shape(tokens, halves * HDIM), (), (normed, w_q))
-        attended, kv = call(
+        attended, kv, *joined = call(
             functools.partial(layer_attend, tick),
             "attend",
-            (shape(chips, halves, tokens, HDIM), shape(patches, frames, tokens, 2 * halves * HDIM)),
-            (info,),
+            (shape(chips, halves, tokens, HDIM), shape(patches, frames, tokens, 2 * halves * HDIM))
+            + (() if tick else (shape(width, halves * HDIM),)),
+            (patch_frames,),
             (queries, own, other) + ((kv,) if tick else ()),
+            () if tick else [pltpu.SemaphoreType.DMA((WEIGHT_PARTS, CORES))],
         )
+        if tick == 0:
+            (w_out,) = joined
         results.append(
             call(
                 functools.partial(layer_back, tick),
                 "back",
                 shape(halves, tokens, HDIM),
-                (info,),
+                (patch_frames,),
                 (swap(attended, same_core), w_out, gathered),
                 [pltpu.VMEM((tokens, width), jnp.bfloat16)],
             )
@@ -337,7 +397,7 @@
         unpack_last,
         "unpack_last",
         shape(patches, frames, local, width),
-        (info,),
+        (patch_frames,),
         (swap(sent),),
         [pltpu.VMEM((parts, width), jnp.float32)],
     )

time: 197 us -> 191 us (0.970)
  blocking collectives: 90.2 us -> 124 us
  waiting for transfers between devices: 29.7 us -> 14.5 us
  starting transfers between devices: 40.4 us -> 27.3 us
  local copies, waits for them, and re-layouts: 9.98 us -> 0.99 us
    all_to_all x7 -> x9, blocking collectives: 90.2 us -> 124 us  [swap(): lax.all_to_all(value, 'seq', split_axis=0, concat_axis=0, tiled=True, axi...]
    all_to_all x2 -> x0, waiting for transfers between devices: 16.8 us -> none  [swap(): lax.all_to_all(value, 'seq', split_axis=0, concat_axis=0, tiled=True, axi...]
    all_to_all x2 -> x0, starting transfers between devices: 10.8 us -> none  [swap(): lax.all_to_all(value, 'seq', split_axis=0, concat_axis=0, tiled=True, axi...]
    unnamed x31 -> x5, local copies, waits for them, and re-layouts: 9.65 us -> 0.99 us
    ppermute x1 -> x0, starting transfers between devices: 2.21 us -> none  [on_device(): w_out_other = lax.ppermute(w_out_own, 'seq', partner)]
    pallas_call x21 -> x23, Pallas kernels: 24.3 us -> 23.7 us  [call(): pl.pallas_call(body, out_shape=out_shape, in_specs=[in_smem] * len(scalar...]
  transfers between devices with their start and end apart: 11 -> 8, of which waited for: 9 -> 7; matrix products, arithmetic and copies ran while one was open for 1% -> 1% of each run, Pallas kernels for 5% -> 2%
where the time goes in v4:
time: 191 us
  blocking collectives  124 us (65%)
  starting transfers between devices  27.3 us (14%)
  Pallas kernels  23.7 us (12%)
  waiting for transfers between devices  14.5 us (8%)
    all_to_all x9, blocking collectives, swap(): lax.all_to_all(value, 'seq', split_axis=0, concat_axis=0, tiled=True, axi...  124 us
    pallas_call x23, Pallas kernels, call(): pl.pallas_call(body, out_shape=out_shape, in_specs=[in_smem] * len(scalar...  23.7 us
    ppermute x4, starting transfers between devices, on_device(): other = lax.ppermute(own, 'seq', partner)  18.3 us
    ppermute x3, waiting for transfers between devices, on_device(): lax.ppermute(results[-1], 'section', [(source, source + 1) for source in...  11.1 us
    ppermute x3, starting transfers between devices, on_device(): lax.ppermute(results[-1], 'section', [(source, source + 1) for source in...  6.49 us
  transfers between devices with their start and end apart: 8, of which 7 were waited for; matrix products, arithmetic and copies ran while one was open for 1% of the time, Pallas kernels for 2%

profile of v4, /device:TPU:385, one launch (start us, length us, event | category | flops | bytes accessed | tf_op | source)
XLA Modules:
  0.0 190.8 jit_solution(3000245054951378755)
XLA Ops:
  0.0 2.6 %collective-permute-start = (bf16[3,4096,128]{2,1,0:T(8,128)(2,1)}, bf16[3,4096,128]{2,1,0:T(8,128)(2,1)S(1)}, u32[]{:S(2)}, u32[]{:S(2)}) collective-permute-start(bf16[3,4096,128]{2,1,0:T(8,128)(2,1)} %bitcast.12), channel_id=1, source_target_pairs={{0,1},{1,0},{2,3},{3,2},{4,5},{5,4},{6,7},{7,6},{8,9},{9,8},{10,11... | collective-permute-start | bytes 9437192 | tf_op jit(solution)/shard_map/ppermute | solution.py:304
  2.6 1.0 copy.10
  3.6 1.1 pack_first.1
  4.7 19.9 %all_to_all.45.came_any = bf16[32,80,128]{2,1,0:T(8,128)(2,1)S(1)} all-to-all(bf16[32,80,128]{2,1,0:T(8,128)(2,1)S(1)} %pack_first.1), channel_id=1, replica_groups=mesh['section'=16,'seq'=32] {'seq'}, dimensions={0} | all-to-all | bytes 1310720 | tf_op jit(solution)/shard_map/all_to_all | solution.py:287
  24.6 2.2 %unpack_first.1 = (bf16[16,2,64,128]{3,2,1,0:T(8,128)(2,1)S(1)}, bf16[3,2,64,128]{3,2,1,0:T(8,128)(2,1)S(1)}, bf16[4096,512]{1,0:T(8,128)(2,1)S(1)}, bf16[4096,256]{1,0:T(8,128)(2,1)S(1)}) custom-call(bf16[32,80,128]{2,1,0:T(8,128)(2,1)S(1)} %all_to_all.45.came_any, bf16[3,4096,128]{2,1,0:T(8,128)(2,1)} %bitcast.13, ...), custom_call_target="tpu_custom_call" | custom-call | tf_op jit(solution)/shard_map/unpack_first/pallas_call | solution.py:26
  26.8 2.4 %keys.4 = (bf16[64,4096]{1,0:T(8,128)(2,1)S(1)}, bf16[1344,512]{1,0:T(8,128)(2,1)S(1)}) custom-call(s32[4]{0:T(128)S(1)} %copy-done.1, bf16[16,2,64,128]{3,2,1,0:T(8,128)(2,1)S(1)} %get-tuple-element.25.x_ref, bf16[1,4096]{1,0:T(2,128)(2,1)S(1)} %copy-done, bf16[4096,512]{1,0:T(8,128)(2,1)S(1)} %get-tuple-element.26.w_ref, bf16[512,256]{1,0:T(8,128)(2,1)S(1)} %bitcast.11, ...), custom_call_target="tpu_custom_call" | custom-call | tf_op jit(solution)/shard_map/keys/pallas_call | solution.py:26
  29.2 2.5 %collective-permute-start.1 = (bf16[1344,512]{1,0:T(8,128)(2,1)S(1)}, bf16[1344,512]{1,0:T(8,128)(2,1)S(1)}, u32[]{:S(2)}, u32[]{:S(2)}) collective-permute-start(bf16[1344,512]{1,0:T(8,128)(2,1)S(1)} %get-tuple-element.29.own_ref), channel_id=1, source_target_pairs={{0,1},{1,0},{2,3},{3,2},{4,5},{5,4},{6,7},{7,6},{8,9},{9,8},{10,11... | collective-permute-start | bytes 4128776 | tf_op jit(solution)/shard_map/ppermute | solution.py:363
  31.7 0.5 queries.4.q_ref
  32.2 2.2 %collective-permute-done.1.other_ref = bf16[1344,512]{1,0:T(8,128)(2,1)S(1)} collective-permute-done((bf16[1344,512]{1,0:T(8,128)(2,1)S(1)}, bf16[1344,512]{1,0:T(8,128)(2,1)S(1)}, u32[]{:S(2)}, u32[]{:S(2)}) %collective-permute-start.1) | collective-permute-done | bytes 1376288 | tf_op jit(solution)/shard_map/ppermute | solution.py:363
  34.4 1.7 attend.4
  36.1 13.9 %all_to_all.46.a_ref = bf16[16,2,64,128]{3,2,1,0:T(8,128)(2,1)S(1)} all-to-all(bf16[16,2,64,128]{3,2,1,0:T(8,128)(2,1)S(1)} %get-tuple-element.30), channel_id=1, replica_groups={{0,2,4,6,8,10,12,14,16,18,20,22,24,26,28,30},{1,3,5,7,9,11,13,15,17,19,..., dimensions={0} | all-to-all | bytes 1048576 | tf_op jit(solution)/shard_map/all_to_all | solution.py:287
  50.0 1.1 back.4.refs_0_
  51.1 2.6 %collective-permute-start.2 = (bf16[2,64,128]{2,1,0:T(8,128)(2,1)S(1)}, bf16[2,64,128]{2,1,0:T(8,128)(2,1)S(1)}, u32[]{:S(2)}, u32[]{:S(2)}) collective-permute-start(bf16[2,64,128]{2,1,0:T(8,128)(2,1)S(1)} %back.4.refs_0_), channel_id=1, source_target_pairs={{0,32},{32,64},{64,96},{96,128},{128,160},{160,192},{192,224},{224... | collective-permute-start | bytes 98312 | tf_op jit(solution)/shard_map/ppermute | solution.py:346
  53.7 3.2 %collective-permute-done.2.arrived_ref = bf16[2,64,128]{2,1,0:T(8,128)(2,1)S(1)} collective-permute-done((bf16[2,64,128]{2,1,0:T(8,128)(2,1)S(1)}, bf16[2,64,128]{2,1,0:T(8,128)(2,1)S(1)}, u32[]{:S(2)}, u32[]{:S(2)}) %collective-permute-start.2) | collective-permute-done | bytes 32800 | tf_op jit(solution)/shard_map/ppermute | solution.py:346
  56.9 0.1 spread.3
  57.0 12.4 %all_to_all.47.x_ref = bf16[16,2,64,128]{3,2,1,0:T(8,128)(2,1)S(1)} all-to-all(bf16[16,2,64,128]{3,2,1,0:T(8,128)(2,1)S(1)} %spread.3), channel_id=1, replica_groups={{0,2,4,6,8,10,12,14,16,18,20,22,24,26,28,30},{1,3,5,7,9,11,13,15,17,19,..., dimensions={0} | all-to-all | bytes 1048576 | tf_op jit(solution)/shard_map/all_to_all | solution.py:287
  69.4 1.5 keys.5
  71.0 5.1 %collective-permute-start.3 = (bf16[64,512]{1,0:T(8,128)(2,1)S(1)}, bf16[64,512]{1,0:T(8,128)(2,1)S(1)}, u32[]{:S(2)}, u32[]{:S(2)}) collective-permute-start(bf16[64,512]{1,0:T(8,128)(2,1)S(1)} %get-tuple-element.34.own_ref), channel_id=1, source_target_pairs={{0,1},{1,0},{2,3},{3,2},{4,5},{5,4},{6,7},{7,6},{8,9},{9,8},{10,11... | collective-permute-start | bytes 196616 | tf_op jit(solution)/shard_map/ppermute | solution.py:363
  76.1 0.5 queries.5.q_ref
  76.6 0.4 collective-permute-done.3.other_ref
  77.0 1.2 attend.5
  78.2 13.4 %all_to_all.48.a_ref = bf16[16,2,64,128]{3,2,1,0:T(8,128)(2,1)S(1)} all-to-all(bf16[16,2,64,128]{3,2,1,0:T(8,128)(2,1)S(1)} %get-tuple-element.36), channel_id=1, replica_groups={{0,2,4,6,8,10,12,14,16,18,20,22,24,26,28,30},{1,3,5,7,9,11,13,15,17,19,..., dimensions={0} | all-to-all | bytes 1048576 | tf_op jit(solution)/shard_map/all_to_all | solution.py:287
  91.7 1.1 back.5.refs_1_
  92.7 1.9 %collective-permute-start.4 = (bf16[2,64,128]{2,1,0:T(8,128)(2,1)S(1)}, bf16[2,64,128]{2,1,0:T(8,128)(2,1)S(1)}, u32[]{:S(2)}, u32[]{:S(2)}) collective-permute-start(bf16[2,64,128]{2,1,0:T(8,128)(2,1)S(1)} %back.5.refs_1_), channel_id=1, source_target_pairs={{0,32},{32,64},{64,96},{96,128},{128,160},{160,192},{192,224},{224... | collective-permute-start | bytes 98312 | tf_op jit(solution)/shard_map/ppermute | solution.py:346
  94.7 3.9 %collective-permute-done.4.arrived_ref = bf16[2,64,128]{2,1,0:T(8,128)(2,1)S(1)} collective-permute-done((bf16[2,64,128]{2,1,0:T(8,128)(2,1)S(1)}, bf16[2,64,128]{2,1,0:T(8,128)(2,1)S(1)}, u32[]{:S(2)}, u32[]{:S(2)}) %collective-permute-start.4) | collective-permute-done | bytes 32800 | tf_op jit(solution)/shard_map/ppermute | solution.py:346
  98.6 0.1 spread.4
  98.7 12.5 %all_to_all.49.x_ref = bf16[16,2,64,128]{3,2,1,0:T(8,128)(2,1)S(1)} all-to-all(bf16[16,2,64,128]{3,2,1,0:T(8,128)(2,1)S(1)} %spread.4), channel_id=1, replica_groups={{0,2,4,6,8,10,12,14,16,18,20,22,24,26,28,30},{1,3,5,7,9,11,13,15,17,19,..., dimensions={0} | all-to-all | bytes 1048576 | tf_op jit(solution)/shard_map/all_to_all | solution.py:287
  111.2 1.5 keys.6
  112.8 5.3 %collective-permute-start.5 = (bf16[64,512]{1,0:T(8,128)(2,1)S(1)}, bf16[64,512]{1,0:T(8,128)(2,1)S(1)}, u32[]{:S(2)}, u32[]{:S(2)}) collective-permute-start(bf16[64,512]{1,0:T(8,128)(2,1)S(1)} %get-tuple-element.38.own_ref), channel_id=1, source_target_pairs={{0,1},{1,0},{2,3},{3,2},{4,5},{5,4},{6,7},{7,6},{8,9},{9,8},{10,11... | collective-permute-start | bytes 196616 | tf_op jit(solution)/shard_map/ppermute | solution.py:363
  118.1 0.5 queries.6.q_ref
  118.6 0.4 collective-permute-done.5.other_ref
  119.0 1.2 attend.6
  120.2 13.4 %all_to_all.50.a_ref = bf16[16,2,64,128]{3,2,1,0:T(8,128)(2,1)S(1)} all-to-all(bf16[16,2,64,128]{3,2,1,0:T(8,128)(2,1)S(1)} %get-tuple-element.40), channel_id=1, replica_groups={{0,2,4,6,8,10,12,14,16,18,20,22,24,26,28,30},{1,3,5,7,9,11,13,15,17,19,..., dimensions={0} | all-to-all | bytes 1048576 | tf_op jit(solution)/shard_map/all_to_all | solution.py:287
  133.7 1.1 back.6.refs_2_
  134.8 1.9 %collective-permute-start.6 = (bf16[2,64,128]{2,1,0:T(8,128)(2,1)S(1)}, bf16[2,64,128]{2,1,0:T(8,128)(2,1)S(1)}, u32[]{:S(2)}, u32[]{:S(2)}) collective-permute-start(bf16[2,64,128]{2,1,0:T(8,128)(2,1)S(1)} %back.6.refs_2_), channel_id=1, source_target_pairs={{0,32},{32,64},{64,96},{96,128},{128,160},{160,192},{192,224},{224... | collective-permute-start | bytes 98312 | tf_op jit(solution)/shard_map/ppermute | solution.py:346
  136.7 3.9 %collective-permute-done.6.arrived_ref = bf16[2,64,128]{2,1,0:T(8,128)(2,1)S(1)} collective-permute-done((bf16[2,64,128]{2,1,0:T(8,128)(2,1)S(1)}, bf16[2,64,128]{2,1,0:T(8,128)(2,1)S(1)}, u32[]{:S(2)}, u32[]{:S(2)}) %collective-permute-start.6) | collective-permute-done | bytes 32800 | tf_op jit(solution)/shard_map/ppermute | solution.py:346
  140.6 0.1 spread.5
  140.7 12.5 %all_to_all.51.x_ref = bf16[16,2,64,128]{3,2,1,0:T(8,128)(2,1)S(1)} all-to-all(bf16[16,2,64,128]{3,2,1,0:T(8,128)(2,1)S(1)} %spread.5), channel_id=1, replica_groups={{0,2,4,6,8,10,12,14,16,18,20,22,24,26,28,30},{1,3,5,7,9,11,13,15,17,19,..., dimensions={0} | all-to-all | bytes 1048576 | tf_op jit(solution)/shard_map/all_to_all | solution.py:287
  153.3 1.5 keys.7
  154.8 5.3 %collective-permute-start.7 = (bf16[64,512]{1,0:T(8,128)(2,1)S(1)}, bf16[64,512]{1,0:T(8,128)(2,1)S(1)}, u32[]{:S(2)}, u32[]{:S(2)}) collective-permute-start(bf16[64,512]{1,0:T(8,128)(2,1)S(1)} %get-tuple-element.42.own_ref), channel_id=1, source_target_pairs={{0,1},{1,0},{2,3},{3,2},{4,5},{5,4},{6,7},{7,6},{8,9},{9,8},{10,11... | collective-permute-start | bytes 196616 | tf_op jit(solution)/shard_map/ppermute | solution.py:363
  160.1 0.5 queries.7.q_ref
  160.6 0.4 collective-permute-done.7.other_ref
  161.0 1.4 attend.7
  162.4 13.4 %all_to_all.52.a_ref = bf16[16,2,64,128]{3,2,1,0:T(8,128)(2,1)S(1)} all-to-all(bf16[16,2,64,128]{3,2,1,0:T(8,128)(2,1)S(1)} %get-tuple-element.44), channel_id=1, replica_groups={{0,2,4,6,8,10,12,14,16,18,20,22,24,26,28,30},{1,3,5,7,9,11,13,15,17,19,..., dimensions={0} | all-to-all | bytes 1048576 | tf_op jit(solution)/shard_map/all_to_all | solution.py:287
  175.8 1.1 back.7.refs_3_
  176.9 0.2 pack_last.1
  177.1 12.4 %all_to_all.53.came_ref = bf16[32,16,128]{2,1,0:T(8,128)(2,1)S(1)} all-to-all(bf16[32,16,128]{2,1,0:T(8,128)(2,1)S(1)} %pack_last.1), channel_id=1, replica_groups=mesh['section'=16,'seq'=32] {'seq'}, dimensions={0} | all-to-all | bytes 262144 | tf_op jit(solution)/shard_map/all_to_all | solution.py:287
  189.5 1.3 unpack_last.1
  (5 shorter events, 0.0 us)
Async XLA Ops:
  0.0 24.6 %collective-permute-start = (bf16[3,4096,128]{2,1,0:T(8,128)(2,1)}, bf16[3,4096,128]{2,1,0:T(8,128)(2,1)S(1)}, u32[]{:S(2)}, u32[]{:S(2)}) collective-permute-start(bf16[3,4096,128]{2,1,0:T(8,128)(2,1)} %bitcast.12), channel_id=1, source_target_pairs={{0,1},{1,0},{2,3},{3,2},{4,5},{5,4},{6,7},{7,6},{8,9},{9,8},{10,11... | collective-permute-start | bytes 9437192 | tf_op jit(solution)/shard_map/ppermute | solution.py:304
  24.6 2.2 %copy-start = (bf16[1,4096]{1,0:T(2,128)(2,1)S(1)}, bf16[1,4096]{1,0:T(2,128)(2,1)}, u32[]{:S(2)}) copy-start(bf16[1,4096]{1,0:T(2,128)(2,1)} %gain_ref.7) | copy-start | bytes 24580
  24.6 2.2 %copy-start.1 = (s32[4]{0:T(128)S(1)}, s32[4]{0:T(128)}, u32[]{:S(2)}) copy-start(s32[4]{0:T(128)} %frames_ref.25) | copy-start | bytes 52
  29.2 5.2 %collective-permute-start.1 = (bf16[1344,512]{1,0:T(8,128)(2,1)S(1)}, bf16[1344,512]{1,0:T(8,128)(2,1)S(1)}, u32[]{:S(2)}, u32[]{:S(2)}) collective-permute-start(bf16[1344,512]{1,0:T(8,128)(2,1)S(1)} %get-tuple-element.29.own_ref), channel_id=1, source_target_pairs={{0,1},{1,0},{2,3},{3,2},{4,5},{5,4},{6,7},{7,6},{8,9},{9,8},{10,11... | collective-permute-start | bytes 4128776 | tf_op jit(solution)/shard_map/ppermute | solution.py:363
  51.1 5.9 %collective-permute-start.2 = (bf16[2,64,128]{2,1,0:T(8,128)(2,1)S(1)}, bf16[2,64,128]{2,1,0:T(8,128)(2,1)S(1)}, u32[]{:S(2)}, u32[]{:S(2)}) collective-permute-start(bf16[2,64,128]{2,1,0:T(8,128)(2,1)S(1)} %back.4.refs_0_), channel_id=1, source_target_pairs={{0,32},{32,64},{64,96},{96,128},{128,160},{160,192},{192,224},{224... | collective-permute-start | bytes 98312 | tf_op jit(solution)/shard_map/ppermute | solution.py:346
  71.0 6.0 %collective-permute-start.3 = (bf16[64,512]{1,0:T(8,128)(2,1)S(1)}, bf16[64,512]{1,0:T(8,128)(2,1)S(1)}, u32[]{:S(2)}, u32[]{:S(2)}) collective-permute-start(bf16[64,512]{1,0:T(8,128)(2,1)S(1)} %get-tuple-element.34.own_ref), channel_id=1, source_target_pairs={{0,1},{1,0},{2,3},{3,2},{4,5},{5,4},{6,7},{7,6},{8,9},{9,8},{10,11... | collective-permute-start | bytes 196616 | tf_op jit(solution)/shard_map/ppermute | solution.py:363
  92.7 5.9 %collective-permute-start.4 = (bf16[2,64,128]{2,1,0:T(8,128)(2,1)S(1)}, bf16[2,64,128]{2,1,0:T(8,128)(2,1)S(1)}, u32[]{:S(2)}, u32[]{:S(2)}) collective-permute-start(bf16[2,64,128]{2,1,0:T(8,128)(2,1)S(1)} %back.5.refs_1_), channel_id=1, source_target_pairs={{0,32},{32,64},{64,96},{96,128},{128,160},{160,192},{192,224},{224... | collective-permute-start | bytes 98312 | tf_op jit(solution)/shard_map/ppermute | solution.py:346
  112.8 6.2 %collective-permute-start.5 = (bf16[64,512]{1,0:T(8,128)(2,1)S(1)}, bf16[64,512]{1,0:T(8,128)(2,1)S(1)}, u32[]{:S(2)}, u32[]{:S(2)}) collective-permute-start(bf16[64,512]{1,0:T(8,128)(2,1)S(1)} %get-tuple-element.38.own_ref), channel_id=1, source_target_pairs={{0,1},{1,0},{2,3},{3,2},{4,5},{5,4},{6,7},{7,6},{8,9},{9,8},{10,11... | collective-permute-start | bytes 196616 | tf_op jit(solution)/shard_map/ppermute | solution.py:363
  134.8 5.9 %collective-permute-start.6 = (bf16[2,64,128]{2,1,0:T(8,128)(2,1)S(1)}, bf16[2,64,128]{2,1,0:T(8,128)(2,1)S(1)}, u32[]{:S(2)}, u32[]{:S(2)}) collective-permute-start(bf16[2,64,128]{2,1,0:T(8,128)(2,1)S(1)} %back.6.refs_2_), channel_id=1, source_target_pairs={{0,32},{32,64},{64,96},{96,128},{128,160},{160,192},{192,224},{224... | collective-permute-start | bytes 98312 | tf_op jit(solution)/shard_map/ppermute | solution.py:346
  154.8 6.2 %collective-permute-start.7 = (bf16[64,512]{1,0:T(8,128)(2,1)S(1)}, bf16[64,512]{1,0:T(8,128)(2,1)S(1)}, u32[]{:S(2)}, u32[]{:S(2)}) collective-permute-start(bf16[64,512]{1,0:T(8,128)(2,1)S(1)} %get-tuple-element.42.own_ref), channel_id=1, source_target_pairs={{0,1},{1,0},{2,3},{3,2},{4,5},{5,4},{6,7},{7,6},{8,9},{9,8},{10,11... | collective-permute-start | bytes 196616 | tf_op jit(solution)/shard_map/ppermute | solution.py:363

commit v5 on v4

v5 whole, which is shorter than its diff:
```python
import functools
import math

import jax
import jax.numpy as jnp
from jax import lax
from jax.experimental import pallas as pl
from jax.experimental.pallas import tpu as pltpu
from jax.sharding import PartitionSpec as P

HDIM = 128
CORES = 2
WEIGHT_PARTS = 4
MOST_SECTIONS = 1024
SPARE = 32
VMEM_LIMIT = 12 * 1024 * 1024


def call(body, name, out_shape, scalars, arrays, scratch=(), in_hbm=(), anywhere=(), aliases=()):
    arrays = [
        pltpu.with_memory_space_constraint(array, pltpu.HBM) if place in in_hbm else array
        for place, array in enumerate(arrays)
    ]
    in_vmem = pl.BlockSpec(memory_space=pltpu.VMEM)
    in_smem = pl.BlockSpec(memory_space=pltpu.SMEM)
    return pl.pallas_call(
        body,
        out_shape=out_shape,
        in_specs=[in_smem] * len(scalars)
        + [pl.BlockSpec(memory_space=pl.ANY) if place in (*in_hbm, *anywhere) else in_vmem for place in range(len(arrays))],
        out_specs=jax.tree.map(lambda _: in_vmem, out_shape),
        scratch_shapes=list(scratch),
        input_output_aliases=dict(aliases),
        compiler_params=pltpu.CompilerParams(vmem_limit_bytes=VMEM_LIMIT),
        name=name,
    )(*scalars, *arrays)


def shape(*dims):
    return jax.ShapeDtypeStruct(dims, jnp.bfloat16)


def pack_first(mine_any, later_any, ready_any, out_ref, mine_ref, later_ref, rows_ref, spare_ref, sem_ref):
    _, frames, local, width = mine_ref.shape
    copies = [
        pltpu.make_async_copy(mine_any, mine_ref, sem_ref.at[0]),
        pltpu.make_async_copy(later_any, later_ref, sem_ref.at[1]),
    ]
    for copy in copies:
        copy.start()
    spare_ref[...] = jnp.zeros_like(spare_ref)
    for copy in copies:
        copy.wait()
    chips = out_ref.shape[0]
    blocks = width // HDIM
    each = local * blocks
    for frame in range(frames):
        wide = mine_ref[0, frame].astype(jnp.float32)
        for block in range(blocks):
            rows_ref[pl.ds(frame * each + block, local, stride=blocks), :] = wide[:, block * HDIM:(block + 1) * HDIM]
    for tick in range(later_ref.shape[0]):
        for frame in range(frames):
            wide = later_ref[tick, frame].astype(jnp.float32)
            for block in range(blocks):
                chip, half = divmod(block, CORES)
                row = chip * SPARE + (tick * frames + frame) * local * CORES + half
                spare_ref[pl.ds(row, local, stride=CORES), :] = wide[:, block * HDIM:(block + 1) * HDIM]
    rows = rows_ref[...].astype(jnp.bfloat16)
    for chip in range(chips):
        out_ref[chip, :frames * each] = rows
        out_ref[chip, frames * each:] = spare_ref[chip * SPARE:(chip + 1) * SPARE].astype(jnp.bfloat16)


def unpack_first(came_ref, weight_any, hidden_ref, fresh_ref, weight_ref, wide_ref, sem_ref):
    fetch = pltpu.make_async_copy(weight_any, weight_ref, sem_ref.at[0])
    fetch.start()
    chips, rows, _ = came_ref.shape
    halves, tokens = hidden_ref.shape[1:3]
    owned = tokens // chips
    blocks = chips * halves
    for source in range(chips):
        wide_ref[source * rows:(source + 1) * rows] = came_ref[source].astype(jnp.float32)

    def over_sources(row):
        return wide_ref[pl.ds(row, chips, stride=rows), :].astype(jnp.bfloat16)

    for token in range(owned):
        span = slice(token * chips, (token + 1) * chips)
        for block in range(blocks):
            hidden_ref[block // halves, block % halves, span] = over_sources(token * blocks + block)
        for tick in range(fresh_ref.shape[0]):
            for half in range(halves):
                fresh_ref[tick, half, span] = over_sources(
                    owned * blocks + (tick * owned + token) * halves + half
                )
    fetch.wait()


def slot_of(frames_ref, tick):
    slots = frames_ref.shape[0]
    return lax.rem(tick + slots * MOST_SECTIONS - lax.axis_index("section"), slots)


def own_core():
    return lax.rem(lax.axis_index("seq"), CORES)


def live_rows(frames, frames_ref, tick, rows):
    row_ids = lax.broadcasted_iota(jnp.int32, (rows, 1), 0)
    return row_ids < frames_ref[slot_of(frames_ref, tick)] * (rows // frames)


def first_rows(tokens, slot_rows, width):
    stale = tokens + slot_rows // CORES
    return stale, stale + width // WEIGHT_PARTS


def two_heads(own_ref, other_ref, kinds, span):
    return jnp.concatenate([ref[kind, span] for ref in (own_ref, other_ref) for kind in kinds], axis=1)


def layer_keys(tick, frames, frames_ref, x_ref, gain_ref, w_own_ref, w_other_ref, *refs):
    *first_refs, xn_ref, new_ref = refs
    chips, halves, tokens, width = x_ref.shape
    pair = halves * width
    squares = jnp.zeros((tokens, width), jnp.float32)
    for chip in range(chips):
        for half in range(halves):
            wide = x_ref[chip, half].astype(jnp.float32)
            squares = squares + wide * wide
    mean_square = jnp.sum(squares, axis=1, keepdims=True) / (chips * pair)
    scale = jnp.where(live_rows(frames, frames_ref, tick, tokens), lax.rsqrt(mean_square + 1e-06), 0.0)
    total = jnp.zeros((tokens, 2 * pair), jnp.float32)
    for chip in range(chips):
        span = slice(chip * pair, (chip + 1) * pair)
        wide = jnp.concatenate([x_ref[chip, half] for half in range(halves)], axis=1).astype(jnp.float32)
        normed = (wide * scale * gain_ref[:, span].astype(jnp.float32)).astype(jnp.bfloat16)
        xn_ref[:, span] = normed
        total = total + jnp.dot(
            normed, two_heads(w_own_ref, w_other_ref, (1, 2), span), preferred_element_type=jnp.float32
        )
    new_ref[:tokens] = total.astype(jnp.bfloat16)
    if tick == 0:
        stale_ref, out_ref = first_refs
        rows, both = stale_ref.shape
        stale_end, weight_end = first_rows(tokens, rows, out_ref.shape[0])
        for part in range(CORES):
            new_ref[tokens:stale_end, part * both:(part + 1) * both] = stale_ref[
                part * rows // CORES:(part + 1) * rows // CORES
            ]
        part_rows = weight_end - stale_end
        for part in range(WEIGHT_PARTS):
            new_ref[stale_end:weight_end, part * width:(part + 1) * width] = out_ref[
                part * part_rows:(part + 1) * part_rows
            ]


def layer_queries(xn_ref, w_own_ref, w_other_ref, out_ref):
    pair = out_ref.shape[1]
    total = jnp.zeros(out_ref.shape, jnp.float32)
    for first in range(0, xn_ref.shape[1], pair):
        span = slice(first, first + pair)
        total = total + jnp.dot(
            xn_ref[:, span], two_heads(w_own_ref, w_other_ref, (0,), span), preferred_element_type=jnp.float32
        )
    out_ref[...] = total.astype(jnp.bfloat16)


def layer_attend(tick, frames, frames_ref, q_ref, own_ref, other_ref, *refs):
    out_ref, kv_out = refs[-2:]
    chips, halves, tokens, width = out_ref.shape
    slots = kv_out.shape[0]
    rows = CORES * tokens
    span = tokens // frames
    both = 2 * width
    slot = slot_of(frames_ref, tick)
    core = own_core()
    if tick == 0:
        for place_of, ref in enumerate((own_ref, other_ref)):
            columns = slice(place_of * both, (place_of + 1) * both)
            for old in range(slots):
                part, place = divmod(old, slots // CORES)
                for frame in range(frames):
                    for piece in range(CORES):
                        row = tokens + place * rows + (frame * CORES + piece) * span
                        kv_out[old, piece, frame * span:(frame + 1) * span, columns] = ref[
                            row:row + span, part * both:(part + 1) * both
                        ]
    kv_out[slot, core] = own_ref[:tokens]
    kv_out[slot, 1 - core, :, :both] = other_ref[:tokens, both:]
    kv_out[slot, 1 - core, :, both:] = other_ref[:tokens, :both]
    key_ids = lax.broadcasted_iota(jnp.int32, (1, slots * rows), 1)
    limit = jnp.zeros_like(key_ids)
    for patch in range(slots):
        limit = jnp.where(key_ids // rows == patch, frames_ref[patch] * span, limit)
    key_live = key_ids % tokens < limit
    for head, half in enumerate((core, 1 - core)):
        queries = q_ref[:, head * width:(head + 1) * width]
        first = head * both
        keys = kv_out[:, :, :, first:first + width].reshape(slots * rows, width)
        values = kv_out[:, :, :, first + width:first + both].reshape(slots * rows, width)
        scores = lax.dot_general(
            queries, keys, (((1,), (1,)), ((), ())), preferred_element_type=jnp.float32
        ) * (1.0 / math.sqrt(HDIM))
        scores = jnp.where(key_live, scores, -jnp.inf)
        exponent = jnp.exp(scores - jnp.max(scores, axis=1, keepdims=True))
        row_total = jnp.sum(exponent, axis=1, keepdims=True)
        attended = jnp.dot(exponent.astype(jnp.bfloat16), values, preferred_element_type=jnp.float32)
        attended = (attended / row_total).astype(jnp.bfloat16)
        for chip in range(chips):
            out_ref[chip, half] = attended


def spread(tick, fresh_ref, arrived_ref, out_ref):
    rows = jnp.where(lax.axis_index("section") == 0, fresh_ref[tick - 1], arrived_ref[...])
    for chip in range(out_ref.shape[0]):
        out_ref[chip] = rows


def layer_back(tick, frames, slot_rows, frames_ref, a_ref, w_own_ref, first_other_ref, x_ref, out_ref):
    chips, halves, tokens, width = a_ref.shape
    pair = halves * width
    chip = lax.div(lax.axis_index("seq"), CORES)
    core = own_core()
    live = live_rows(frames, frames_ref, tick, tokens)
    stale_end, weight_end = first_rows(tokens, slot_rows, w_own_ref.shape[0])
    branch = jnp.zeros((tokens, pair), jnp.float32)
    for source in range(chips):
        wide = jnp.concatenate([a_ref[source, half] for half in range(halves)], axis=1)
        part, row = divmod(source * pair, weight_end - stale_end)
        row += stale_end
        weights = jnp.concatenate(
            [
                w_own_ref[source * pair:(source + 1) * pair],
                first_other_ref[row:row + pair, part * width:(part + 1) * width],
            ],
            axis=1,
        )
        branch = branch + jnp.dot(wide, weights, preferred_element_type=jnp.float32)
    branch = branch.astype(jnp.bfloat16).astype(jnp.float32)
    for head, half in enumerate((core, 1 - core)):
        total = x_ref[chip, half].astype(jnp.float32) + branch[:, head * width:(head + 1) * width]
        out_ref[half] = jnp.where(live, total, 0.0).astype(jnp.bfloat16)


def pack_last(*refs):
    *result_refs, out_ref, wide_ref = refs
    chips, parts, _ = out_ref.shape
    ticks = len(result_refs)
    for tick, ref in enumerate(result_refs):
        halves, tokens, _ = ref.shape
        for half in range(halves):
            first = (half * ticks + tick) * tokens
            wide_ref[first:first + tokens] = ref[half].astype(jnp.float32)
    for chip in range(chips):
        out_ref[chip] = wide_ref[pl.ds(chip, parts, stride=chips), :].astype(jnp.bfloat16)


def unpack_last(frames_ref, came_ref, out_ref, turn_ref):
    chips, parts, width = came_ref.shape
    patches, frames, local, _ = out_ref.shape
    each = parts // CORES
    for chip in range(chips):
        wide = came_ref[chip].astype(jnp.float32)
        for half in range(CORES):
            first = (chip * CORES + half) * width
            turn_ref[:, first:first + width] = wide[half * each:(half + 1) * each]
    for tick in range(patches):
        slot = slot_of(frames_ref, tick)
        for frame in range(frames):
            row = (tick * frames + frame) * local
            out_ref[slot, frame] = turn_ref[row:row + local].astype(jnp.bfloat16)


def on_device(in_flight, entering, patch_frames, norm_gain, qkv_weight, out_weight, stale_kv):
    sections = lax.axis_size("section")
    group = lax.axis_size("seq")
    patches, frames, tokens = stale_kv.shape[1:4]
    local = in_flight.shape[2]
    width = in_flight.shape[3]
    ticks = patches
    chips = group // CORES
    halves = CORES
    owned = frames * local
    rows = owned * chips
    blocks = chips * halves
    same_core = [[CORES * chip + core for chip in range(chips)] for core in range(CORES)]
    partner = [(device, device ^ 1) for device in range(group)]

    def swap(value):
        return lax.all_to_all(
            value, "seq", split_axis=0, concat_axis=0, tiled=True, axis_index_groups=same_core
        )

    w_in = jnp.transpose(qkv_weight[0], (1, 0, 2))
    w_in_other = lax.ppermute(w_in, "seq", partner)
    stale = stale_kv[0].reshape(patches * frames * tokens, 2 * HDIM)
    sent = call(
        pack_first,
        "pack_first",
        shape(chips, owned * blocks + SPARE, HDIM),
        (),
        (in_flight, entering, stale),
        [
            pltpu.VMEM(in_flight.shape, jnp.bfloat16),
            pltpu.VMEM(entering.shape, jnp.bfloat16),
            pltpu.VMEM((owned * blocks, HDIM), jnp.float32),
            pltpu.VMEM((chips * SPARE, HDIM), jnp.float32),
            pltpu.SemaphoreType.DMA((2,)),
        ],
        in_hbm=(0, 1),
        anywhere=(2,),
    )
    came = swap(sent)
    gathered, fresh, w_out = call(
        unpack_first,
        "unpack_first",
        (shape(chips, halves, rows, HDIM), shape(ticks - 1, halves, rows, HDIM), shape(width, HDIM)),
        (),
        (came, out_weight[0]),
        [pltpu.VMEM((chips * (owned * blocks + SPARE), HDIM), jnp.float32), pltpu.SemaphoreType.DMA((1,))],
        in_hbm=(1,),
    )
    results = []
    for tick in range(ticks):
        if tick:
            arrived = lax.ppermute(
                results[-1], "section", [(source, source + 1) for source in range(sections - 1)]
            )
            gathered = call(
                functools.partial(spread, tick), "spread", shape(chips, halves, rows, HDIM), (), (fresh, arrived)
            )
            gathered = swap(gathered)
        new_rows = rows if tick else first_rows(rows, stale.shape[0], width)[1]
        normed, own = call(
            functools.partial(layer_keys, tick, frames),
            "keys",
            (shape(rows, width), shape(new_rows, 2 * halves * HDIM)),
            (patch_frames,),
            (gathered, norm_gain, w_in, w_in_other) + (() if tick else (stale, w_out)),
        )
        other = lax.ppermute(own, "seq", partner)
        queries = call(layer_queries, "queries", shape(rows, halves * HDIM), (), (normed, w_in, w_in_other))
        attended, kv = call(
            functools.partial(layer_attend, tick, frames),
            "attend",
            (shape(chips, halves, rows, HDIM), shape(patches, CORES, rows, 2 * halves * HDIM)),
            (patch_frames,),
            (queries, own, other) + ((kv,) if tick else ()),
            aliases={4: 1} if tick else {},
        )
        if tick == 0:
            first_other = other
        results.append(
            call(
                functools.partial(layer_back, tick, frames, stale.shape[0]),
                "back",
                shape(halves, rows, HDIM),
                (patch_frames,),
                (swap(attended), w_out, first_other, gathered),
            )
        )

    parts = ticks * halves * owned
    sent = call(
        pack_last,
        "pack_last",
        shape(chips, parts, HDIM),
        (),
        tuple(results),
        [pltpu.VMEM((ticks * halves * rows, HDIM), jnp.float32)],
    )
    outputs = call(
        unpack_last,
        "unpack_last",
        shape(patches, frames, local, width),
        (patch_frames,),
        (swap(sent),),
        [pltpu.VMEM((ticks * owned, width), jnp.float32)],
    )
    return outputs[None]


def solution(mesh):
    in_specs = (
        P("section", None, "seq", None),
        P(None, None, "seq", None),
        P(),
        P("section", None),
        P("section", None, None, "seq"),
        P("section", None, "seq"),
        P("section", None, None, None, None, "seq"),
    )
    out_specs = P("section", None, None, "seq", None)
    return jax.shard_map(
        on_device, mesh=mesh, in_specs=in_specs, out_specs=out_specs, check_vma=False
    )
```

time: 191 us -> 189 us (0.990)
  the two profiles are of different devices: /device:TPU:385 before, /device:TPU:128 now
where the time goes in v5:
time: 189 us; the launch traced here: 188 us
  blocking collectives  130 us (69%)
  Pallas kernels  21 us (11%)
  starting transfers between devices  18.2 us (10%)
  waiting for transfers between devices  17.5 us (9%)
    all_to_all x9, blocking collectives, swap(): lax.all_to_all(value, 'seq', split_axis=0, concat_axis=0, tiled=True, axi...  130 us
    pallas_call x23, Pallas kernels, call(): pl.pallas_call(body, out_shape=out_shape, in_specs=[in_smem] * len(scalar...  21 us
    ppermute x3, waiting for transfers between devices, on_device(): lax.ppermute(results[-1], 'section', [(source, source + 1) for source in...  12.7 us
    ppermute x3, starting transfers between devices, on_device(): lax.ppermute(results[-1], 'section', [(source, source + 1) for source in...  8.36 us
    ppermute x4, starting transfers between devices, on_device(): other = lax.ppermute(own, 'seq', partner)  7.68 us
    ppermute x4, waiting for transfers between devices, on_device(): other = lax.ppermute(own, 'seq', partner)  4.81 us
  transfers between devices with their start and end apart: 8, of which 7 were waited for; matrix products, arithmetic and copies ran while one was open for 1% of the time, Pallas kernels for 2%

profile of v5, /device:TPU:128, one launch (start us, length us, event | category | flops | bytes accessed | tf_op | source)
XLA Modules:
  0.0 187.9 jit_solution(10082402322105348176)
XLA Ops:
  0.0 2.2 %collective-permute-start = (bf16[3,4096,128]{2,1,0:T(8,128)(2,1)}, bf16[3,4096,128]{2,1,0:T(8,128)(2,1)S(1)}, u32[]{:S(2)}, u32[]{:S(2)}) collective-permute-start(bf16[3,4096,128]{2,1,0:T(8,128)(2,1)} %bitcast.10), channel_id=1, source_target_pairs={{0,1},{1,0},{2,3},{3,2},{4,5},{5,4},{6,7},{7,6},{8,9},{9,8},{10,11... | collective-permute-start | bytes 9437192 | tf_op jit(solution)/shard_map/ppermute | solution.py:296
  2.2 1.0 copy.13
  3.2 1.1 pack_first.1
  4.3 20.4 %all_to_all.45.came_ref = bf16[16,160,128]{2,1,0:T(8,128)(2,1)S(1)} all-to-all(bf16[16,160,128]{2,1,0:T(8,128)(2,1)S(1)} %pack_first.1), channel_id=1, replica_groups={{0,2,4,6,8,10,12,14,16,18,20,22,24,26,28,30},{1,3,5,7,9,11,13,15,17,19,..., dimensions={0} | all-to-all | bytes 1310720 | tf_op jit(solution)/shard_map/all_to_all | solution.py:291
  24.7 1.2 unpack_first.1
  26.0 1.6 keys.4
  27.6 1.9 %collective-permute-start.1 = (bf16[1344,512]{1,0:T(8,128)(2,1)S(1)}, bf16[1344,512]{1,0:T(8,128)(2,1)S(1)}, u32[]{:S(2)}, u32[]{:S(2)}) collective-permute-start(bf16[1344,512]{1,0:T(8,128)(2,1)S(1)} %get-tuple-element.26.own_ref), channel_id=1, source_target_pairs={{0,1},{1,0},{2,3},{3,2},{4,5},{5,4},{6,7},{7,6},{8,9},{9,8},{10,11... | collective-permute-start | bytes 4128776 | tf_op jit(solution)/shard_map/ppermute | solution.py:342
  29.5 0.5 queries.4.q_ref
  30.0 2.6 %collective-permute-done.1.other_ref.first_other_ref = bf16[1344,512]{1,0:T(8,128)(2,1)S(1)} collective-permute-done((bf16[1344,512]{1,0:T(8,128)(2,1)S(1)}, bf16[1344,512]{1,0:T(8,128)(2,1)S(1)}, u32[]{:S(2)}, u32[]{:S(2)}) %collective-permute-start.1) | collective-permute-done | bytes 1376288 | tf_op jit(solution)/shard_map/ppermute | solution.py:342
  32.6 1.2 attend.4
  33.8 14.9 %all_to_all.46.a_ref = bf16[16,2,64,128]{3,2,1,0:T(8,128)(2,1)S(1)} all-to-all(bf16[16,2,64,128]{3,2,1,0:T(8,128)(2,1)S(1)} %get-tuple-element.27), channel_id=1, replica_groups={{0,2,4,6,8,10,12,14,16,18,20,22,24,26,28,30},{1,3,5,7,9,11,13,15,17,19,..., dimensions={0} | all-to-all | bytes 1048576 | tf_op jit(solution)/shard_map/all_to_all | solution.py:291
  48.7 1.0 back.4.refs_0_
  49.8 3.8 %collective-permute-start.2 = (bf16[2,64,128]{2,1,0:T(8,128)(2,1)S(1)}, bf16[2,64,128]{2,1,0:T(8,128)(2,1)S(1)}, u32[]{:S(2)}, u32[]{:S(2)}) collective-permute-start(bf16[2,64,128]{2,1,0:T(8,128)(2,1)S(1)} %back.4.refs_0_), channel_id=1, source_target_pairs={{0,32},{32,64},{64,96},{96,128},{128,160},{160,192},{192,224},{224... | collective-permute-start | bytes 98312 | tf_op jit(solution)/shard_map/ppermute | solution.py:327
  53.6 3.2 %collective-permute-done.2.arrived_ref = bf16[2,64,128]{2,1,0:T(8,128)(2,1)S(1)} collective-permute-done((bf16[2,64,128]{2,1,0:T(8,128)(2,1)S(1)}, bf16[2,64,128]{2,1,0:T(8,128)(2,1)S(1)}, u32[]{:S(2)}, u32[]{:S(2)}) %collective-permute-start.2) | collective-permute-done | bytes 32800 | tf_op jit(solution)/shard_map/ppermute | solution.py:327
  56.8 0.1 spread.3
  56.9 13.0 %all_to_all.47.x_ref = bf16[16,2,64,128]{3,2,1,0:T(8,128)(2,1)S(1)} all-to-all(bf16[16,2,64,128]{3,2,1,0:T(8,128)(2,1)S(1)} %spread.3), channel_id=1, replica_groups={{0,2,4,6,8,10,12,14,16,18,20,22,24,26,28,30},{1,3,5,7,9,11,13,15,17,19,..., dimensions={0} | all-to-all | bytes 1048576 | tf_op jit(solution)/shard_map/all_to_all | solution.py:291
  70.0 1.5 keys.5
  71.5 1.9 %collective-permute-start.3 = (bf16[64,512]{1,0:T(8,128)(2,1)S(1)}, bf16[64,512]{1,0:T(8,128)(2,1)S(1)}, u32[]{:S(2)}, u32[]{:S(2)}) collective-permute-start(bf16[64,512]{1,0:T(8,128)(2,1)S(1)} %get-tuple-element.30.own_ref), channel_id=1, source_target_pairs={{0,1},{1,0},{2,3},{3,2},{4,5},{5,4},{6,7},{7,6},{8,9},{9,8},{10,11... | collective-permute-start | bytes 196616 | tf_op jit(solution)/shard_map/ppermute | solution.py:342
  73.4 0.5 queries.5.q_ref
  73.9 0.7 collective-permute-done.3.other_ref
  74.6 1.2 attend.5
  75.8 14.8 %all_to_all.48.a_ref = bf16[16,2,64,128]{3,2,1,0:T(8,128)(2,1)S(1)} all-to-all(bf16[16,2,64,128]{3,2,1,0:T(8,128)(2,1)S(1)} %get-tuple-element.32), channel_id=1, replica_groups={{0,2,4,6,8,10,12,14,16,18,20,22,24,26,28,30},{1,3,5,7,9,11,13,15,17,19,..., dimensions={0} | all-to-all | bytes 1048576 | tf_op jit(solution)/shard_map/all_to_all | solution.py:291
  90.7 1.0 back.5.refs_1_
  91.7 2.6 %collective-permute-start.4 = (bf16[2,64,128]{2,1,0:T(8,128)(2,1)S(1)}, bf16[2,64,128]{2,1,0:T(8,128)(2,1)S(1)}, u32[]{:S(2)}, u32[]{:S(2)}) collective-permute-start(bf16[2,64,128]{2,1,0:T(8,128)(2,1)S(1)} %back.5.refs_1_), channel_id=1, source_target_pairs={{0,32},{32,64},{64,96},{96,128},{128,160},{160,192},{192,224},{224... | collective-permute-start | bytes 98312 | tf_op jit(solution)/shard_map/ppermute | solution.py:327
  94.3 4.4 %collective-permute-done.4.arrived_ref = bf16[2,64,128]{2,1,0:T(8,128)(2,1)S(1)} collective-permute-done((bf16[2,64,128]{2,1,0:T(8,128)(2,1)S(1)}, bf16[2,64,128]{2,1,0:T(8,128)(2,1)S(1)}, u32[]{:S(2)}, u32[]{:S(2)}) %collective-permute-start.4) | collective-permute-done | bytes 32800 | tf_op jit(solution)/shard_map/ppermute | solution.py:327
  98.7 0.1 spread.4
  98.8 13.0 %all_to_all.49.x_ref = bf16[16,2,64,128]{3,2,1,0:T(8,128)(2,1)S(1)} all-to-all(bf16[16,2,64,128]{3,2,1,0:T(8,128)(2,1)S(1)} %spread.4), channel_id=1, replica_groups={{0,2,4,6,8,10,12,14,16,18,20,22,24,26,28,30},{1,3,5,7,9,11,13,15,17,19,..., dimensions={0} | all-to-all | bytes 1048576 | tf_op jit(solution)/shard_map/all_to_all | solution.py:291
  111.9 1.5 keys.6
  113.4 1.9 %collective-permute-start.5 = (bf16[64,512]{1,0:T(8,128)(2,1)S(1)}, bf16[64,512]{1,0:T(8,128)(2,1)S(1)}, u32[]{:S(2)}, u32[]{:S(2)}) collective-permute-start(bf16[64,512]{1,0:T(8,128)(2,1)S(1)} %get-tuple-element.34.own_ref), channel_id=1, source_target_pairs={{0,1},{1,0},{2,3},{3,2},{4,5},{5,4},{6,7},{7,6},{8,9},{9,8},{10,11... | collective-permute-start | bytes 196616 | tf_op jit(solution)/shard_map/ppermute | solution.py:342
  115.3 0.5 queries.6.q_ref
  115.8 0.7 collective-permute-done.5.other_ref
  116.6 1.2 attend.6
  117.8 14.8 %all_to_all.50.a_ref = bf16[16,2,64,128]{3,2,1,0:T(8,128)(2,1)S(1)} all-to-all(bf16[16,2,64,128]{3,2,1,0:T(8,128)(2,1)S(1)} %get-tuple-element.36), channel_id=1, replica_groups={{0,2,4,6,8,10,12,14,16,18,20,22,24,26,28,30},{1,3,5,7,9,11,13,15,17,19,..., dimensions={0} | all-to-all | bytes 1048576 | tf_op jit(solution)/shard_map/all_to_all | solution.py:291
  132.6 1.0 back.6.refs_2_
  133.7 1.9 %collective-permute-start.6 = (bf16[2,64,128]{2,1,0:T(8,128)(2,1)S(1)}, bf16[2,64,128]{2,1,0:T(8,128)(2,1)S(1)}, u32[]{:S(2)}, u32[]{:S(2)}) collective-permute-start(bf16[2,64,128]{2,1,0:T(8,128)(2,1)S(1)} %back.6.refs_2_), channel_id=1, source_target_pairs={{0,32},{32,64},{64,96},{96,128},{128,160},{160,192},{192,224},{224... | collective-permute-start | bytes 98312 | tf_op jit(solution)/shard_map/ppermute | solution.py:327
  135.6 5.1 %collective-permute-done.6.arrived_ref = bf16[2,64,128]{2,1,0:T(8,128)(2,1)S(1)} collective-permute-done((bf16[2,64,128]{2,1,0:T(8,128)(2,1)S(1)}, bf16[2,64,128]{2,1,0:T(8,128)(2,1)S(1)}, u32[]{:S(2)}, u32[]{:S(2)}) %collective-permute-start.6) | collective-permute-done | bytes 32800 | tf_op jit(solution)/shard_map/ppermute | solution.py:327
  140.7 0.1 spread.5
  140.8 13.0 %all_to_all.51.x_ref = bf16[16,2,64,128]{3,2,1,0:T(8,128)(2,1)S(1)} all-to-all(bf16[16,2,64,128]{3,2,1,0:T(8,128)(2,1)S(1)} %spread.5), channel_id=1, replica_groups={{0,2,4,6,8,10,12,14,16,18,20,22,24,26,28,30},{1,3,5,7,9,11,13,15,17,19,..., dimensions={0} | all-to-all | bytes 1048576 | tf_op jit(solution)/shard_map/all_to_all | solution.py:291
  153.8 1.5 keys.7
  155.3 1.9 %collective-permute-start.7 = (bf16[64,512]{1,0:T(8,128)(2,1)S(1)}, bf16[64,512]{1,0:T(8,128)(2,1)S(1)}, u32[]{:S(2)}, u32[]{:S(2)}) collective-permute-start(bf16[64,512]{1,0:T(8,128)(2,1)S(1)} %get-tuple-element.38.own_ref), channel_id=1, source_target_pairs={{0,1},{1,0},{2,3},{3,2},{4,5},{5,4},{6,7},{7,6},{8,9},{9,8},{10,11... | collective-permute-start | bytes 196616 | tf_op jit(solution)/shard_map/ppermute | solution.py:342
  157.3 0.5 queries.7.q_ref
  157.8 0.7 collective-permute-done.7.other_ref
  158.5 1.2 attend.7
  159.7 14.8 %all_to_all.52.a_ref = bf16[16,2,64,128]{3,2,1,0:T(8,128)(2,1)S(1)} all-to-all(bf16[16,2,64,128]{3,2,1,0:T(8,128)(2,1)S(1)} %get-tuple-element.40), channel_id=1, replica_groups={{0,2,4,6,8,10,12,14,16,18,20,22,24,26,28,30},{1,3,5,7,9,11,13,15,17,19,..., dimensions={0} | all-to-all | bytes 1048576 | tf_op jit(solution)/shard_map/all_to_all | solution.py:291
  174.6 1.0 back.7.refs_3_
  175.6 0.1 pack_last.1
  175.7 10.9 %all_to_all.53.came_ref = bf16[16,32,128]{2,1,0:T(8,128)(2,1)S(1)} all-to-all(bf16[16,32,128]{2,1,0:T(8,128)(2,1)S(1)} %pack_last.1), channel_id=1, replica_groups={{0,2,4,6,8,10,12,14,16,18,20,22,24,26,28,30},{1,3,5,7,9,11,13,15,17,19,..., dimensions={0} | all-to-all | bytes 262144 | tf_op jit(solution)/shard_map/all_to_all | solution.py:291
  186.6 1.3 unpack_last.1
  (7 shorter events, 0.0 us)
Async XLA Ops:
  0.0 26.0 %copy-start = (bf16[1,4096,3,128]{3,1,2,0:T(8,128)(2,1)S(1)}, bf16[1,4096,3,128]{3,1,2,0:T(8,128)(2,1)}, u32[]{:S(2)}) copy-start(bf16[1,4096,3,128]{3,1,2,0:T(8,128)(2,1)} %param.11) | copy-start | bytes 9437188
  0.0 26.0 %copy-start.2 = (s32[4]{0:T(128)S(1)}, s32[4]{0:T(128)}, u32[]{:S(2)}) copy-start(s32[4]{0:T(128)} %frames_ref.25) | copy-start | bytes 52
  0.0 26.0 %copy-start.1 = (bf16[1,4096]{1,0:T(2,128)(2,1)S(1)}, bf16[1,4096]{1,0:T(2,128)(2,1)}, u32[]{:S(2)}) copy-start(bf16[1,4096]{1,0:T(2,128)(2,1)} %gain_ref.7) | copy-start | bytes 24580
  0.0 25.9 %collective-permute-start = (bf16[3,4096,128]{2,1,0:T(8,128)(2,1)}, bf16[3,4096,128]{2,1,0:T(8,128)(2,1)S(1)}, u32[]{:S(2)}, u32[]{:S(2)}) collective-permute-start(bf16[3,4096,128]{2,1,0:T(8,128)(2,1)} %bitcast.10), channel_id=1, source_target_pairs={{0,1},{1,0},{2,3},{3,2},{4,5},{5,4},{6,7},{7,6},{8,9},{9,8},{10,11... | collective-permute-start | bytes 9437192 | tf_op jit(solution)/shard_map/ppermute | solution.py:296
  27.6 5.0 %collective-permute-start.1 = (bf16[1344,512]{1,0:T(8,128)(2,1)S(1)}, bf16[1344,512]{1,0:T(8,128)(2,1)S(1)}, u32[]{:S(2)}, u32[]{:S(2)}) collective-permute-start(bf16[1344,512]{1,0:T(8,128)(2,1)S(1)} %get-tuple-element.26.own_ref), channel_id=1, source_target_pairs={{0,1},{1,0},{2,3},{3,2},{4,5},{5,4},{6,7},{7,6},{8,9},{9,8},{10,11... | collective-permute-start | bytes 4128776 | tf_op jit(solution)/shard_map/ppermute | solution.py:342
  49.8 7.0 %collective-permute-start.2 = (bf16[2,64,128]{2,1,0:T(8,128)(2,1)S(1)}, bf16[2,64,128]{2,1,0:T(8,128)(2,1)S(1)}, u32[]{:S(2)}, u32[]{:S(2)}) collective-permute-start(bf16[2,64,128]{2,1,0:T(8,128)(2,1)S(1)} %back.4.refs_0_), channel_id=1, source_target_pairs={{0,32},{32,64},{64,96},{96,128},{128,160},{160,192},{192,224},{224... | collective-permute-start | bytes 98312 | tf_op jit(solution)/shard_map/ppermute | solution.py:327
  71.5 3.1 %collective-permute-start.3 = (bf16[64,512]{1,0:T(8,128)(2,1)S(1)}, bf16[64,512]{1,0:T(8,128)(2,1)S(1)}, u32[]{:S(2)}, u32[]{:S(2)}) collective-permute-start(bf16[64,512]{1,0:T(8,128)(2,1)S(1)} %get-tuple-element.30.own_ref), channel_id=1, source_target_pairs={{0,1},{1,0},{2,3},{3,2},{4,5},{5,4},{6,7},{7,6},{8,9},{9,8},{10,11... | collective-permute-start | bytes 196616 | tf_op jit(solution)/shard_map/ppermute | solution.py:342
  91.7 7.0 %collective-permute-start.4 = (bf16[2,64,128]{2,1,0:T(8,128)(2,1)S(1)}, bf16[2,64,128]{2,1,0:T(8,128)(2,1)S(1)}, u32[]{:S(2)}, u32[]{:S(2)}) collective-permute-start(bf16[2,64,128]{2,1,0:T(8,128)(2,1)S(1)} %back.5.refs_1_), channel_id=1, source_target_pairs={{0,32},{32,64},{64,96},{96,128},{128,160},{160,192},{192,224},{224... | collective-permute-start | bytes 98312 | tf_op jit(solution)/shard_map/ppermute | solution.py:327
  113.4 3.1 %collective-permute-start.5 = (bf16[64,512]{1,0:T(8,128)(2,1)S(1)}, bf16[64,512]{1,0:T(8,128)(2,1)S(1)}, u32[]{:S(2)}, u32[]{:S(2)}) collective-permute-start(bf16[64,512]{1,0:T(8,128)(2,1)S(1)} %get-tuple-element.34.own_ref), channel_id=1, source_target_pairs={{0,1},{1,0},{2,3},{3,2},{4,5},{5,4},{6,7},{7,6},{8,9},{9,8},{10,11... | collective-permute-start | bytes 196616 | tf_op jit(solution)/shard_map/ppermute | solution.py:342
  133.7 7.0 %collective-permute-start.6 = (bf16[2,64,128]{2,1,0:T(8,128)(2,1)S(1)}, bf16[2,64,128]{2,1,0:T(8,128)(2,1)S(1)}, u32[]{:S(2)}, u32[]{:S(2)}) collective-permute-start(bf16[2,64,128]{2,1,0:T(8,128)(2,1)S(1)} %back.6.refs_2_), channel_id=1, source_target_pairs={{0,32},{32,64},{64,96},{96,128},{128,160},{160,192},{192,224},{224... | collective-permute-start | bytes 98312 | tf_op jit(solution)/shard_map/ppermute | solution.py:327
  155.3 3.1 %collective-permute-start.7 = (bf16[64,512]{1,0:T(8,128)(2,1)S(1)}, bf16[64,512]{1,0:T(8,128)(2,1)S(1)}, u32[]{:S(2)}, u32[]{:S(2)}) collective-permute-start(bf16[64,512]{1,0:T(8,128)(2,1)S(1)} %get-tuple-element.38.own_ref), channel_id=1, source_target_pairs={{0,1},{1,0},{2,3},{3,2},{4,5},{5,4},{6,7},{7,6},{8,9},{9,8},{10,11... | collective-permute-start | bytes 196616 | tf_op jit(solution)/shard_map/ppermute | solution.py:342

commit v6 on v5

--- a/solution.py
+++ b/solution.py
@@ -12,11 +12,10 @@
 CORES = 2
 WEIGHT_PARTS = 4
 MOST_SECTIONS = 1024
-SPARE = 32
 VMEM_LIMIT = 12 * 1024 * 1024
 
 
-def call(body, name, out_shape, scalars, arrays, scratch=(), in_hbm=(), anywhere=(), aliases=()):
+def call(body, name, out_shape, scalars, arrays, scratch=(), in_hbm=(), aliases=()):
     arrays = [
         pltpu.with_memory_space_constraint(array, pltpu.HBM) if place in in_hbm else array
         for place, array in enumerate(arrays)
@@ -27,7 +26,7 @@
         body,
         out_shape=out_shape,
         in_specs=[in_smem] * len(scalars)
-        + [pl.BlockSpec(memory_space=pl.ANY) if place in (*in_hbm, *anywhere) else in_vmem for place in range(len(arrays))],
+        + [pl.BlockSpec(memory_space=pl.ANY) if place in in_hbm else in_vmem for place in range(len(arrays))],
         out_specs=jax.tree.map(lambda _: in_vmem, out_shape),
         scratch_shapes=list(scratch),
         input_output_aliases=dict(aliases),
@@ -40,60 +39,77 @@
     return jax.ShapeDtypeStruct(dims, jnp.bfloat16)
 
 
-def pack_first(mine_any, later_any, ready_any, out_ref, mine_ref, later_ref, rows_ref, spare_ref, sem_ref):
-    _, frames, local, width = mine_ref.shape
-    copies = [
-        pltpu.make_async_copy(mine_any, mine_ref, sem_ref.at[0]),
-        pltpu.make_async_copy(later_any, later_ref, sem_ref.at[1]),
+def fetch_rows(tokens_any, tokens_ref, rows_ref, sem_ref):
+    fetch = pltpu.make_async_copy(tokens_any, tokens_ref, sem_ref.at[0])
+    fetch.start()
+    fetch.wait()
+    frames, local, width = tokens_ref.shape
+    blocks = width // HDIM
+    for frame in range(frames):
+        wide = tokens_ref[frame].astype(jnp.float32)
+        for block in range(blocks):
+            rows_ref[pl.ds(frame * local * blocks + block, local, stride=blocks), :] = wide[
+                :, block * HDIM:(block + 1) * HDIM
+            ]
+
+
+def send_rows(rows_ref, out_ref):
+    chips, halves, tokens, _ = out_ref.shape
+    for half in range(halves):
+        rows = rows_ref[half * tokens:(half + 1) * tokens].astype(jnp.bfloat16)
+        for chip in range(chips):
+            out_ref[chip, half] = rows
+
+
+def pack_first(mine_any, out_ref, mine_ref, rows_ref, sem_ref):
+    fetch_rows(mine_any.at[0], mine_ref, rows_ref, sem_ref)
+    send_rows(rows_ref, out_ref)
+
+
+def to_blocks(came_ref, hidden_ref, wide_ref):
+    chips, halves, tokens, _ = came_ref.shape
+    blocks = chips * halves
+    for chip in range(chips):
+        for half in range(halves):
+            first = (chip * halves + half) * tokens
+            wide_ref[first:first + tokens] = came_ref[chip, half].astype(jnp.float32)
+    for token in range(tokens // chips):
+        for block in range(blocks):
+            hidden_ref[block // halves, block % halves, token * chips:(token + 1) * chips] = wide_ref[
+                pl.ds(token * blocks + block, chips, stride=halves * tokens), :
+            ].astype(jnp.bfloat16)
+
+
+def unpack_first(came_ref, weight_any, stale_any, hidden_ref, weight_ref, stale_ref, wide_ref, sem_ref):
+    fetches = [
+        pltpu.make_async_copy(weight_any, weight_ref, sem_ref.at[0]),
+        pltpu.make_async_copy(stale_any, stale_ref, sem_ref.at[1]),
     ]
-    for copy in copies:
-        copy.start()
-    spare_ref[...] = jnp.zeros_like(spare_ref)
-    for copy in copies:
-        copy.wait()
-    chips = out_ref.shape[0]
-    blocks = width // HDIM
-    each = local * blocks
-    for frame in range(frames):
-        wide = mine_ref[0, frame].astype(jnp.float32)
-        for block in range(blocks):
-            rows_ref[pl.ds(frame * each + block, local, stride=blocks), :] = wide[:, block * HDIM:(block + 1) * HDIM]
-    for tick in range(later_ref.shape[0]):
-        for frame in range(frames):
-            wide = later_ref[tick, frame].astype(jnp.float32)
-            for block in range(blocks):
-                chip, half = divmod(block, CORES)
-                row = chip * SPARE + (tick * frames + frame) * local * CORES + half
-                spare_ref[pl.ds(row, local, stride=CORES), :] = wide[:, block * HDIM:(block + 1) * HDIM]
-    rows = rows_ref[...].astype(jnp.bfloat16)
-    for chip in range(chips):
-        out_ref[chip, :frames * each] = rows
-        out_ref[chip, frames * each:] = spare_ref[chip * SPARE:(chip + 1) * SPARE].astype(jnp.bfloat16)
-
-
-def unpack_first(came_ref, weight_any, hidden_ref, fresh_ref, weight_ref, wide_ref, sem_ref):
-    fetch = pltpu.make_async_copy(weight_any, weight_ref, sem_ref.at[0])
-    fetch.start()
-    chips, rows, _ = came_ref.shape
-    halves, tokens = hidden_ref.shape[1:3]
-    owned = tokens // chips
-    blocks = chips * halves
-    for source in range(chips):
-        wide_ref[source * rows:(source + 1) * rows] = came_ref[source].astype(jnp.float32)
-
-    def over_sources(row):
-        return wide_ref[pl.ds(row, chips, stride=rows), :].astype(jnp.bfloat16)
-
-    for token in range(owned):
-        span = slice(token * chips, (token + 1) * chips)
-        for block in range(blocks):
-            hidden_ref[block // halves, block % halves, span] = over_sources(token * blocks + block)
-        for tick in range(fresh_ref.shape[0]):
-            for half in range(halves):
-                fresh_ref[tick, half, span] = over_sources(
-                    owned * blocks + (tick * owned + token) * halves + half
-                )
-    fetch.wait()
+    for fetch in fetches:
+        fetch.start()
+    to_blocks(came_ref, hidden_ref, wide_ref)
+    for fetch in fetches:
+        fetch.wait()
+
+
+def spread(tick, entering_any, arrived_ref, out_ref, tokens_ref, rows_ref, sem_ref):
+    section = lax.axis_index("section")
+
+    @pl.when(section == 0)
+    def _():
+        fetch_rows(entering_any.at[tick - 1], tokens_ref, rows_ref, sem_ref)
+        send_rows(rows_ref, out_ref)
+
+    @pl.when(section != 0)
+    def _():
+        for chip in range(out_ref.shape[0]):
+            out_ref[chip] = arrived_ref[...]
+
+
+def arrange(came_ref, hidden_ref, wide_ref):
+    @pl.when(lax.axis_index("section") == 0)
+    def _():
+        to_blocks(came_ref, hidden_ref, wide_ref)
 
 
 def slot_of(frames_ref, tick):
@@ -120,7 +136,7 @@
 
 
 def layer_keys(tick, frames, frames_ref, x_ref, gain_ref, w_own_ref, w_other_ref, *refs):
-    *first_refs, xn_ref, new_ref = refs
+    *first_refs, xn_ref, new_ref = refs if tick else refs[:-1]
     chips, halves, tokens, width = x_ref.shape
     pair = halves * width
     squares = jnp.zeros((tokens, width), jnp.float32)
@@ -142,12 +158,17 @@
     new_ref[:tokens] = total.astype(jnp.bfloat16)
     if tick == 0:
         stale_ref, out_ref = first_refs
-        rows, both = stale_ref.shape
+        wide_ref = refs[-1]
+        rows = stale_ref.shape[0] // 2
         stale_end, weight_end = first_rows(tokens, rows, out_ref.shape[0])
+        wide_ref[...] = stale_ref[...].astype(jnp.float32)
+        each = rows // CORES
         for part in range(CORES):
-            new_ref[tokens:stale_end, part * both:(part + 1) * both] = stale_ref[
-                part * rows // CORES:(part + 1) * rows // CORES
-            ]
+            for kind in range(2):
+                first = (part * 2 + kind) * width
+                new_ref[tokens:stale_end, first:first + width] = wide_ref[
+                    pl.ds(part * 2 * each + kind, each, stride=2), :
+                ].astype(jnp.bfloat16)
         part_rows = weight_end - stale_end
         for part in range(WEIGHT_PARTS):
             new_ref[stale_end:weight_end, part * width:(part + 1) * width] = out_ref[
@@ -211,12 +232,6 @@
             out_ref[chip, half] = attended
 
 
-def spread(tick, fresh_ref, arrived_ref, out_ref):
-    rows = jnp.where(lax.axis_index("section") == 0, fresh_ref[tick - 1], arrived_ref[...])
-    for chip in range(out_ref.shape[0]):
-        out_ref[chip] = rows
-
-
 def layer_back(tick, frames, slot_rows, frames_ref, a_ref, w_own_ref, first_other_ref, x_ref, out_ref):
     chips, halves, tokens, width = a_ref.shape
     pair = halves * width
@@ -294,32 +309,23 @@
 
     w_in = jnp.transpose(qkv_weight[0], (1, 0, 2))
     w_in_other = lax.ppermute(w_in, "seq", partner)
-    stale = stale_kv[0].reshape(patches * frames * tokens, 2 * HDIM)
-    sent = call(
-        pack_first,
-        "pack_first",
-        shape(chips, owned * blocks + SPARE, HDIM),
-        (),
-        (in_flight, entering, stale),
-        [
-            pltpu.VMEM(in_flight.shape, jnp.bfloat16),
-            pltpu.VMEM(entering.shape, jnp.bfloat16),
-            pltpu.VMEM((owned * blocks, HDIM), jnp.float32),
-            pltpu.VMEM((chips * SPARE, HDIM), jnp.float32),
-            pltpu.SemaphoreType.DMA((2,)),
-        ],
-        in_hbm=(0, 1),
-        anywhere=(2,),
-    )
-    came = swap(sent)
-    gathered, fresh, w_out = call(
+    stale = stale_kv[0].reshape(patches * frames * tokens * 2, HDIM)
+    block_dims = (chips, halves, rows, HDIM)
+    token_scratch = [
+        pltpu.VMEM((frames, local, width), jnp.bfloat16),
+        pltpu.VMEM((owned * blocks, HDIM), jnp.float32),
+        pltpu.SemaphoreType.DMA((1,)),
+    ]
+    wide = pltpu.VMEM((chips * halves * rows, HDIM), jnp.float32)
+    came = swap(call(pack_first, "pack_first", shape(*block_dims), (), (in_flight,), token_scratch, in_hbm=(0,)))
+    gathered, w_out, stale = call(
         unpack_first,
         "unpack_first",
-        (shape(chips, halves, rows, HDIM), shape(ticks - 1, halves, rows, HDIM), shape(width, HDIM)),
+        (shape(*block_dims), shape(width, HDIM), shape(*stale.shape)),
         (),
-        (came, out_weight[0]),
-        [pltpu.VMEM((chips * (owned * blocks + SPARE), HDIM), jnp.float32), pltpu.SemaphoreType.DMA((1,))],
-        in_hbm=(1,),
+        (came, out_weight[0], stale),
+        [wide, pltpu.SemaphoreType.DMA((2,))],
+        in_hbm=(1, 2),
     )
     results = []
     for tick in range(ticks):
@@ -327,17 +333,24 @@
             arrived = lax.ppermute(
                 results[-1], "section", [(source, source + 1) for source in range(sections - 1)]
             )
-            gathered = call(
-                functools.partial(spread, tick), "spread", shape(chips, halves, rows, HDIM), (), (fresh, arrived)
+            sent = call(
+                functools.partial(spread, tick),
+                "spread",
+                shape(*block_dims),
+                (),
+                (entering, arrived),
+                token_scratch,
+                in_hbm=(0,),
             )
-            gathered = swap(gathered)
-        new_rows = rows if tick else first_rows(rows, stale.shape[0], width)[1]
+            gathered = call(arrange, "arrange", shape(*block_dims), (), (swap(sent),), [wide], aliases={0: 0})
+        new_rows = rows if tick else first_rows(rows, stale.shape[0] // 2, width)[1]
         normed, own = call(
             functools.partial(layer_keys, tick, frames),
             "keys",
             (shape(rows, width), shape(new_rows, 2 * halves * HDIM)),
             (patch_frames,),
             (gathered, norm_gain, w_in, w_in_other) + (() if tick else (stale, w_out)),
+            () if tick else [pltpu.VMEM(stale.shape, jnp.float32)],
         )
         other = lax.ppermute(own, "seq", partner)
         queries = call(layer_queries, "queries", shape(rows, halves * HDIM), (), (normed, w_in, w_in_other))
@@ -353,7 +366,7 @@
             first_other = other
         results.append(
             call(
-                functools.partial(layer_back, tick, frames, stale.shape[0]),
+                functools.partial(layer_back, tick, frames, stale.shape[0] // 2),
                 "back",
                 shape(halves, rows, HDIM),
                 (patch_frames,),

time: 189 us -> 186 us (0.984)
  blocking collectives: 130 us -> 128 us
    pallas_call x23 -> x26, Pallas kernels: 21 us -> 20.9 us  [call(): pl.pallas_call(body, out_shape=out_shape, in_specs=[in_smem] * len(scalar...]
  transfers between devices with their start and end apart: 8 -> 8, of which waited for: 7 -> 7; matrix products, arithmetic and copies ran while one was open for 1% -> 0% of each run, Pallas kernels for 2% -> 2%
where the time goes in v6:
time: 186 us; the launch traced here: 185 us
  blocking collectives  128 us (69%)
  Pallas kernels  20.9 us (11%)
  starting transfers between devices  18.2 us (10%)
  waiting for transfers between devices  17.5 us (9%)
    all_to_all x9, blocking collectives, swap(): lax.all_to_all(value, 'seq', split_axis=0, concat_axis=0, tiled=True, axi...  128 us
    pallas_call x26, Pallas kernels, call(): pl.pallas_call(body, out_shape=out_shape, in_specs=[in_smem] * len(scalar...  20.9 us
    ppermute x3, waiting for transfers between devices, on_device(): lax.ppermute(results[-1], 'section', [(source, source + 1) for source in...  12.7 us
    ppermute x3, starting transfers between devices, on_device(): lax.ppermute(results[-1], 'section', [(source, source + 1) for source in...  8.35 us
    ppermute x4, starting transfers between devices, on_device(): other = lax.ppermute(own, 'seq', partner)  7.68 us
    ppermute x4, waiting for transfers between devices, on_device(): other = lax.ppermute(own, 'seq', partner)  4.81 us
  transfers between devices with their start and end apart: 8, of which 7 were waited for; matrix products, arithmetic and copies ran while one was open for 0% of the time, Pallas kernels for 2%

profile of v6, /device:TPU:128, one launch (start us, length us, event | category | flops | bytes accessed | tf_op | source)
XLA Modules:
  0.0 185.2 jit_solution(16314176870596491964)
XLA Ops:
  0.0 2.2 %collective-permute-start = (bf16[3,4096,128]{2,1,0:T(8,128)(2,1)}, bf16[3,4096,128]{2,1,0:T(8,128)(2,1)S(1)}, u32[]{:S(2)}, u32[]{:S(2)}) collective-permute-start(bf16[3,4096,128]{2,1,0:T(8,128)(2,1)} %bitcast.6), channel_id=1, source_target_pairs={{0,1},{1,0},{2,3},{3,2},{4,5},{5,4},{6,7},{7,6},{8,9},{9,8},{10,11... | collective-permute-start | bytes 9437192 | tf_op jit(solution)/shard_map/ppermute | solution.py:311
  2.2 0.8 pack_first.1
  3.1 19.0 %all_to_all.45.came_ref = bf16[16,2,64,128]{3,2,1,0:T(8,128)(2,1)S(1)} all-to-all(bf16[16,2,64,128]{3,2,1,0:T(8,128)(2,1)S(1)} %pack_first.1), channel_id=1, replica_groups={{0,2,4,6,8,10,12,14,16,18,20,22,24,26,28,30},{1,3,5,7,9,11,13,15,17,19,..., dimensions={0} | all-to-all | bytes 1048576 | tf_op jit(solution)/shard_map/all_to_all | solution.py:306
  22.1 1.3 unpack_first.1
  23.4 0.0 collective-permute-done.w_other_ref
  23.4 1.7 keys.4
  25.1 1.9 %collective-permute-start.1 = (bf16[1344,512]{1,0:T(8,128)(2,1)S(1)}, bf16[1344,512]{1,0:T(8,128)(2,1)S(1)}, u32[]{:S(2)}, u32[]{:S(2)}) collective-permute-start(bf16[1344,512]{1,0:T(8,128)(2,1)S(1)} %get-tuple-element.27.own_ref), channel_id=1, source_target_pairs={{0,1},{1,0},{2,3},{3,2},{4,5},{5,4},{6,7},{7,6},{8,9},{9,8},{10,11... | collective-permute-start | bytes 4128776 | tf_op jit(solution)/shard_map/ppermute | solution.py:355
  27.0 0.5 queries.4.q_ref
  27.5 2.6 %collective-permute-done.1.other_ref.first_other_ref = bf16[1344,512]{1,0:T(8,128)(2,1)S(1)} collective-permute-done((bf16[1344,512]{1,0:T(8,128)(2,1)S(1)}, bf16[1344,512]{1,0:T(8,128)(2,1)S(1)}, u32[]{:S(2)}, u32[]{:S(2)}) %collective-permute-start.1) | collective-permute-done | bytes 1376288 | tf_op jit(solution)/shard_map/ppermute | solution.py:355
  30.1 1.2 attend.4
  31.4 14.7 %all_to_all.46.a_ref = bf16[16,2,64,128]{3,2,1,0:T(8,128)(2,1)S(1)} all-to-all(bf16[16,2,64,128]{3,2,1,0:T(8,128)(2,1)S(1)} %get-tuple-element.28), channel_id=1, replica_groups={{0,2,4,6,8,10,12,14,16,18,20,22,24,26,28,30},{1,3,5,7,9,11,13,15,17,19,..., dimensions={0} | all-to-all | bytes 1048576 | tf_op jit(solution)/shard_map/all_to_all | solution.py:306
  46.1 1.0 back.4.refs_0_
  47.1 3.8 %collective-permute-start.2 = (bf16[2,64,128]{2,1,0:T(8,128)(2,1)S(1)}, bf16[2,64,128]{2,1,0:T(8,128)(2,1)S(1)}, u32[]{:S(2)}, u32[]{:S(2)}) collective-permute-start(bf16[2,64,128]{2,1,0:T(8,128)(2,1)S(1)} %back.4.refs_0_), channel_id=1, source_target_pairs={{0,32},{32,64},{64,96},{96,128},{128,160},{160,192},{192,224},{224... | collective-permute-start | bytes 98312 | tf_op jit(solution)/shard_map/ppermute | solution.py:333
  50.9 3.2 %collective-permute-done.2.arrived_ref = bf16[2,64,128]{2,1,0:T(8,128)(2,1)S(1)} collective-permute-done((bf16[2,64,128]{2,1,0:T(8,128)(2,1)S(1)}, bf16[2,64,128]{2,1,0:T(8,128)(2,1)S(1)}, u32[]{:S(2)}, u32[]{:S(2)}) %collective-permute-start.2) | collective-permute-done | bytes 32800 | tf_op jit(solution)/shard_map/ppermute | solution.py:333
  54.1 0.1 spread.3
  54.2 13.0 %all_to_all.47.came_ref = bf16[16,2,64,128]{3,2,1,0:T(8,128)(2,1)S(1)} all-to-all(bf16[16,2,64,128]{3,2,1,0:T(8,128)(2,1)S(1)} %spread.3), channel_id=1, replica_groups={{0,2,4,6,8,10,12,14,16,18,20,22,24,26,28,30},{1,3,5,7,9,11,13,15,17,19,..., dimensions={0} | all-to-all | bytes 1048576 | tf_op jit(solution)/shard_map/all_to_all | solution.py:306
  67.3 1.5 keys.5
  68.8 1.9 %collective-permute-start.3 = (bf16[64,512]{1,0:T(8,128)(2,1)S(1)}, bf16[64,512]{1,0:T(8,128)(2,1)S(1)}, u32[]{:S(2)}, u32[]{:S(2)}) collective-permute-start(bf16[64,512]{1,0:T(8,128)(2,1)S(1)} %get-tuple-element.30.own_ref), channel_id=1, source_target_pairs={{0,1},{1,0},{2,3},{3,2},{4,5},{5,4},{6,7},{7,6},{8,9},{9,8},{10,11... | collective-permute-start | bytes 196616 | tf_op jit(solution)/shard_map/ppermute | solution.py:355
  70.7 0.5 queries.5.q_ref
  71.2 0.7 collective-permute-done.3.other_ref
  71.9 1.2 attend.5
  73.1 14.8 %all_to_all.48.a_ref = bf16[16,2,64,128]{3,2,1,0:T(8,128)(2,1)S(1)} all-to-all(bf16[16,2,64,128]{3,2,1,0:T(8,128)(2,1)S(1)} %get-tuple-element.32), channel_id=1, replica_groups={{0,2,4,6,8,10,12,14,16,18,20,22,24,26,28,30},{1,3,5,7,9,11,13,15,17,19,..., dimensions={0} | all-to-all | bytes 1048576 | tf_op jit(solution)/shard_map/all_to_all | solution.py:306
  88.0 1.0 back.5.refs_1_
  89.0 2.6 %collective-permute-start.4 = (bf16[2,64,128]{2,1,0:T(8,128)(2,1)S(1)}, bf16[2,64,128]{2,1,0:T(8,128)(2,1)S(1)}, u32[]{:S(2)}, u32[]{:S(2)}) collective-permute-start(bf16[2,64,128]{2,1,0:T(8,128)(2,1)S(1)} %back.5.refs_1_), channel_id=1, source_target_pairs={{0,32},{32,64},{64,96},{96,128},{128,160},{160,192},{192,224},{224... | collective-permute-start | bytes 98312 | tf_op jit(solution)/shard_map/ppermute | solution.py:333
  91.7 4.4 %collective-permute-done.4.arrived_ref = bf16[2,64,128]{2,1,0:T(8,128)(2,1)S(1)} collective-permute-done((bf16[2,64,128]{2,1,0:T(8,128)(2,1)S(1)}, bf16[2,64,128]{2,1,0:T(8,128)(2,1)S(1)}, u32[]{:S(2)}, u32[]{:S(2)}) %collective-permute-start.4) | collective-permute-done | bytes 32800 | tf_op jit(solution)/shard_map/ppermute | solution.py:333
  96.1 0.1 spread.4
  96.1 13.0 %all_to_all.49.came_ref = bf16[16,2,64,128]{3,2,1,0:T(8,128)(2,1)S(1)} all-to-all(bf16[16,2,64,128]{3,2,1,0:T(8,128)(2,1)S(1)} %spread.4), channel_id=1, replica_groups={{0,2,4,6,8,10,12,14,16,18,20,22,24,26,28,30},{1,3,5,7,9,11,13,15,17,19,..., dimensions={0} | all-to-all | bytes 1048576 | tf_op jit(solution)/shard_map/all_to_all | solution.py:306
  109.2 1.5 keys.6
  110.7 1.9 %collective-permute-start.5 = (bf16[64,512]{1,0:T(8,128)(2,1)S(1)}, bf16[64,512]{1,0:T(8,128)(2,1)S(1)}, u32[]{:S(2)}, u32[]{:S(2)}) collective-permute-start(bf16[64,512]{1,0:T(8,128)(2,1)S(1)} %get-tuple-element.34.own_ref), channel_id=1, source_target_pairs={{0,1},{1,0},{2,3},{3,2},{4,5},{5,4},{6,7},{7,6},{8,9},{9,8},{10,11... | collective-permute-start | bytes 196616 | tf_op jit(solution)/shard_map/ppermute | solution.py:355
  112.6 0.5 queries.6.q_ref
  113.1 0.7 collective-permute-done.5.other_ref
  113.9 1.2 attend.6
  115.1 14.8 %all_to_all.50.a_ref = bf16[16,2,64,128]{3,2,1,0:T(8,128)(2,1)S(1)} all-to-all(bf16[16,2,64,128]{3,2,1,0:T(8,128)(2,1)S(1)} %get-tuple-element.36), channel_id=1, replica_groups={{0,2,4,6,8,10,12,14,16,18,20,22,24,26,28,30},{1,3,5,7,9,11,13,15,17,19,..., dimensions={0} | all-to-all | bytes 1048576 | tf_op jit(solution)/shard_map/all_to_all | solution.py:306
  129.9 1.0 back.6.refs_2_
  131.0 1.9 %collective-permute-start.6 = (bf16[2,64,128]{2,1,0:T(8,128)(2,1)S(1)}, bf16[2,64,128]{2,1,0:T(8,128)(2,1)S(1)}, u32[]{:S(2)}, u32[]{:S(2)}) collective-permute-start(bf16[2,64,128]{2,1,0:T(8,128)(2,1)S(1)} %back.6.refs_2_), channel_id=1, source_target_pairs={{0,32},{32,64},{64,96},{96,128},{128,160},{160,192},{192,224},{224... | collective-permute-start | bytes 98312 | tf_op jit(solution)/shard_map/ppermute | solution.py:333
  132.9 5.1 %collective-permute-done.6.arrived_ref = bf16[2,64,128]{2,1,0:T(8,128)(2,1)S(1)} collective-permute-done((bf16[2,64,128]{2,1,0:T(8,128)(2,1)S(1)}, bf16[2,64,128]{2,1,0:T(8,128)(2,1)S(1)}, u32[]{:S(2)}, u32[]{:S(2)}) %collective-permute-start.6) | collective-permute-done | bytes 32800 | tf_op jit(solution)/shard_map/ppermute | solution.py:333
  138.0 0.1 spread.5
  138.1 13.0 %all_to_all.51.came_ref = bf16[16,2,64,128]{3,2,1,0:T(8,128)(2,1)S(1)} all-to-all(bf16[16,2,64,128]{3,2,1,0:T(8,128)(2,1)S(1)} %spread.5), channel_id=1, replica_groups={{0,2,4,6,8,10,12,14,16,18,20,22,24,26,28,30},{1,3,5,7,9,11,13,15,17,19,..., dimensions={0} | all-to-all | bytes 1048576 | tf_op jit(solution)/shard_map/all_to_all | solution.py:306
  151.1 1.5 keys.7
  152.6 1.9 %collective-permute-start.7 = (bf16[64,512]{1,0:T(8,128)(2,1)S(1)}, bf16[64,512]{1,0:T(8,128)(2,1)S(1)}, u32[]{:S(2)}, u32[]{:S(2)}) collective-permute-start(bf16[64,512]{1,0:T(8,128)(2,1)S(1)} %get-tuple-element.38.own_ref), channel_id=1, source_target_pairs={{0,1},{1,0},{2,3},{3,2},{4,5},{5,4},{6,7},{7,6},{8,9},{9,8},{10,11... | collective-permute-start | bytes 196616 | tf_op jit(solution)/shard_map/ppermute | solution.py:355
  154.6 0.5 queries.7.q_ref
  155.1 0.7 collective-permute-done.7.other_ref
  155.8 1.2 attend.7
  157.0 14.8 %all_to_all.52.a_ref = bf16[16,2,64,128]{3,2,1,0:T(8,128)(2,1)S(1)} all-to-all(bf16[16,2,64,128]{3,2,1,0:T(8,128)(2,1)S(1)} %get-tuple-element.40), channel_id=1, replica_groups={{0,2,4,6,8,10,12,14,16,18,20,22,24,26,28,30},{1,3,5,7,9,11,13,15,17,19,..., dimensions={0} | all-to-all | bytes 1048576 | tf_op jit(solution)/shard_map/all_to_all | solution.py:306
  171.9 1.0 back.7.refs_3_
  172.9 0.1 pack_last.1
  173.0 10.9 %all_to_all.53.came_ref = bf16[16,32,128]{2,1,0:T(8,128)(2,1)S(1)} all-to-all(bf16[16,32,128]{2,1,0:T(8,128)(2,1)S(1)} %pack_last.1), channel_id=1, replica_groups={{0,2,4,6,8,10,12,14,16,18,20,22,24,26,28,30},{1,3,5,7,9,11,13,15,17,19,..., dimensions={0} | all-to-all | bytes 262144 | tf_op jit(solution)/shard_map/all_to_all | solution.py:306
  184.0 1.3 unpack_last.1
  (9 shorter events, 0.0 us)
Async XLA Ops:
  0.0 23.4 %copy-start = (bf16[1,4096,3,128]{3,1,2,0:T(8,128)(2,1)S(1)}, bf16[1,4096,3,128]{3,1,2,0:T(8,128)(2,1)}, u32[]{:S(2)}) copy-start(bf16[1,4096,3,128]{3,1,2,0:T(8,128)(2,1)} %param.11) | copy-start | bytes 9437188
  0.0 23.4 %copy-start.2 = (s32[4]{0:T(128)S(1)}, s32[4]{0:T(128)}, u32[]{:S(2)}) copy-start(s32[4]{0:T(128)} %frames_ref.25) | copy-start | bytes 52
  0.0 23.4 %copy-start.1 = (bf16[1,4096]{1,0:T(2,128)(2,1)S(1)}, bf16[1,4096]{1,0:T(2,128)(2,1)}, u32[]{:S(2)}) copy-start(bf16[1,4096]{1,0:T(2,128)(2,1)} %gain_ref.7) | copy-start | bytes 24580
  0.0 23.4 %collective-permute-start = (bf16[3,4096,128]{2,1,0:T(8,128)(2,1)}, bf16[3,4096,128]{2,1,0:T(8,128)(2,1)S(1)}, u32[]{:S(2)}, u32[]{:S(2)}) collective-permute-start(bf16[3,4096,128]{2,1,0:T(8,128)(2,1)} %bitcast.6), channel_id=1, source_target_pairs={{0,1},{1,0},{2,3},{3,2},{4,5},{5,4},{6,7},{7,6},{8,9},{9,8},{10,11... | collective-permute-start | bytes 9437192 | tf_op jit(solution)/shard_map/ppermute | solution.py:311
  25.1 5.0 %collective-permute-start.1 = (bf16[1344,512]{1,0:T(8,128)(2,1)S(1)}, bf16[1344,512]{1,0:T(8,128)(2,1)S(1)}, u32[]{:S(2)}, u32[]{:S(2)}) collective-permute-start(bf16[1344,512]{1,0:T(8,128)(2,1)S(1)} %get-tuple-element.27.own_ref), channel_id=1, source_target_pairs={{0,1},{1,0},{2,3},{3,2},{4,5},{5,4},{6,7},{7,6},{8,9},{9,8},{10,11... | collective-permute-start | bytes 4128776 | tf_op jit(solution)/shard_map/ppermute | solution.py:355
  47.1 7.0 %collective-permute-start.2 = (bf16[2,64,128]{2,1,0:T(8,128)(2,1)S(1)}, bf16[2,64,128]{2,1,0:T(8,128)(2,1)S(1)}, u32[]{:S(2)}, u32[]{:S(2)}) collective-permute-start(bf16[2,64,128]{2,1,0:T(8,128)(2,1)S(1)} %back.4.refs_0_), channel_id=1, source_target_pairs={{0,32},{32,64},{64,96},{96,128},{128,160},{160,192},{192,224},{224... | collective-permute-start | bytes 98312 | tf_op jit(solution)/shard_map/ppermute | solution.py:333
  68.8 3.1 %collective-permute-start.3 = (bf16[64,512]{1,0:T(8,128)(2,1)S(1)}, bf16[64,512]{1,0:T(8,128)(2,1)S(1)}, u32[]{:S(2)}, u32[]{:S(2)}) collective-permute-start(bf16[64,512]{1,0:T(8,128)(2,1)S(1)} %get-tuple-element.30.own_ref), channel_id=1, source_target_pairs={{0,1},{1,0},{2,3},{3,2},{4,5},{5,4},{6,7},{7,6},{8,9},{9,8},{10,11... | collective-permute-start | bytes 196616 | tf_op jit(solution)/shard_map/ppermute | solution.py:355
  89.0 7.0 %collective-permute-start.4 = (bf16[2,64,128]{2,1,0:T(8,128)(2,1)S(1)}, bf16[2,64,128]{2,1,0:T(8,128)(2,1)S(1)}, u32[]{:S(2)}, u32[]{:S(2)}) collective-permute-start(bf16[2,64,128]{2,1,0:T(8,128)(2,1)S(1)} %back.5.refs_1_), channel_id=1, source_target_pairs={{0,32},{32,64},{64,96},{96,128},{128,160},{160,192},{192,224},{224... | collective-permute-start | bytes 98312 | tf_op jit(solution)/shard_map/ppermute | solution.py:333
  110.7 3.1 %collective-permute-start.5 = (bf16[64,512]{1,0:T(8,128)(2,1)S(1)}, bf16[64,512]{1,0:T(8,128)(2,1)S(1)}, u32[]{:S(2)}, u32[]{:S(2)}) collective-permute-start(bf16[64,512]{1,0:T(8,128)(2,1)S(1)} %get-tuple-element.34.own_ref), channel_id=1, source_target_pairs={{0,1},{1,0},{2,3},{3,2},{4,5},{5,4},{6,7},{7,6},{8,9},{9,8},{10,11... | collective-permute-start | bytes 196616 | tf_op jit(solution)/shard_map/ppermute | solution.py:355
  131.0 7.0 %collective-permute-start.6 = (bf16[2,64,128]{2,1,0:T(8,128)(2,1)S(1)}, bf16[2,64,128]{2,1,0:T(8,128)(2,1)S(1)}, u32[]{:S(2)}, u32[]{:S(2)}) collective-permute-start(bf16[2,64,128]{2,1,0:T(8,128)(2,1)S(1)} %back.6.refs_2_), channel_id=1, source_target_pairs={{0,32},{32,64},{64,96},{96,128},{128,160},{160,192},{192,224},{224... | collective-permute-start | bytes 98312 | tf_op jit(solution)/shard_map/ppermute | solution.py:333
  152.6 3.1 %collective-permute-start.7 = (bf16[64,512]{1,0:T(8,128)(2,1)S(1)}, bf16[64,512]{1,0:T(8,128)(2,1)S(1)}, u32[]{:S(2)}, u32[]{:S(2)}) collective-permute-start(bf16[64,512]{1,0:T(8,128)(2,1)S(1)} %get-tuple-element.38.own_ref), channel_id=1, source_target_pairs={{0,1},{1,0},{2,3},{3,2},{4,5},{5,4},{6,7},{7,6},{8,9},{9,8},{10,11... | collective-permute-start | bytes 196616 | tf_op jit(solution)/shard_map/ppermute | solution.py:355

commit v7 on v6

--- a/solution.py
+++ b/solution.py
@@ -215,21 +215,28 @@
     for patch in range(slots):
         limit = jnp.where(key_ids // rows == patch, frames_ref[patch] * span, limit)
     key_live = key_ids % tokens < limit
+    scores = []
+    for head in range(halves):
+        keys = kv_out[:, :, :, head * both:head * both + width].reshape(slots * rows, width)
+        scores.append(
+            lax.dot_general(
+                q_ref[:, head * width:(head + 1) * width], keys, (((1,), (1,)), ((), ())),
+                preferred_element_type=jnp.float32,
+            )
+        )
+    scores = jnp.where(key_live, jnp.concatenate(scores, axis=0) * (1.0 / math.sqrt(HDIM)), -jnp.inf)
+    exponent = jnp.exp(scores - jnp.max(scores, axis=1, keepdims=True))
+    weights_low = exponent.astype(jnp.bfloat16)
+    share = 1.0 / jnp.sum(exponent, axis=1, keepdims=True)
+    attended = []
+    for head in range(halves):
+        span = slice(head * tokens, (head + 1) * tokens)
+        values = kv_out[:, :, :, head * both + width:(head + 1) * both].reshape(slots * rows, width)
+        weighted = jnp.dot(weights_low[span], values, preferred_element_type=jnp.float32)
+        attended.append((weighted * share[span]).astype(jnp.bfloat16))
     for head, half in enumerate((core, 1 - core)):
-        queries = q_ref[:, head * width:(head + 1) * width]
-        first = head * both
-        keys = kv_out[:, :, :, first:first + width].reshape(slots * rows, width)
-        values = kv_out[:, :, :, first + width:first + both].reshape(slots * rows, width)
-        scores = lax.dot_general(
-            queries, keys, (((1,), (1,)), ((), ())), preferred_element_type=jnp.float32
-        ) * (1.0 / math.sqrt(HDIM))
-        scores = jnp.where(key_live, scores, -jnp.inf)
-        exponent = jnp.exp(scores - jnp.max(scores, axis=1, keepdims=True))
-        row_total = jnp.sum(exponent, axis=1, keepdims=True)
-        attended = jnp.dot(exponent.astype(jnp.bfloat16), values, preferred_element_type=jnp.float32)
-        attended = (attended / row_total).astype(jnp.bfloat16)
         for chip in range(chips):
-            out_ref[chip, half] = attended
+            out_ref[chip, half] = attended[head]
 
 
 def layer_back(tick, frames, slot_rows, frames_ref, a_ref, w_own_ref, first_other_ref, x_ref, out_ref):

time: 186 us -> 185 us (level)
  the two profiles are of different devices: /device:TPU:128 before, /device:TPU:385 now
where the time goes in v7:
time: 185 us; the launch traced here: 182 us
  blocking collectives  119 us (64%)
  starting transfers between devices  28.7 us (16%)
  Pallas kernels  20 us (11%)
  waiting for transfers between devices  14.5 us (8%)
    all_to_all x9, blocking collectives, swap(): lax.all_to_all(value, 'seq', split_axis=0, concat_axis=0, tiled=True, axi...  119 us
    pallas_call x26, Pallas kernels, call(): pl.pallas_call(body, out_shape=out_shape, in_specs=[in_smem] * len(scalar...  20 us
    ppermute x4, starting transfers between devices, on_device(): other = lax.ppermute(own, 'seq', partner)  19.4 us
    ppermute x3, waiting for transfers between devices, on_device(): lax.ppermute(results[-1], 'section', [(source, source + 1) for source in...  11.1 us
    ppermute x3, starting transfers between devices, on_device(): lax.ppermute(results[-1], 'section', [(source, source + 1) for source in...  6.48 us
  transfers between devices with their start and end apart: 8, of which 7 were waited for; matrix products, arithmetic and copies ran while one was open for 0% of the time, Pallas kernels for 2%

profile of v7, /device:TPU:385, one launch (start us, length us, event | category | flops | bytes accessed | tf_op | source)
XLA Modules:
  0.0 182.5 jit_solution(16645042660833492394)
XLA Ops:
  0.0 2.8 %collective-permute-start = (bf16[3,4096,128]{2,1,0:T(8,128)(2,1)}, bf16[3,4096,128]{2,1,0:T(8,128)(2,1)S(1)}, u32[]{:S(2)}, u32[]{:S(2)}) collective-permute-start(bf16[3,4096,128]{2,1,0:T(8,128)(2,1)} %bitcast.6), channel_id=1, source_target_pairs={{0,1},{1,0},{2,3},{3,2},{4,5},{5,4},{6,7},{7,6},{8,9},{9,8},{10,11... | collective-permute-start | bytes 9437192 | tf_op jit(solution)/shard_map/ppermute | solution.py:318
  2.9 0.8 pack_first.1
  3.7 17.6 %all_to_all.45.came_ref = bf16[16,2,64,128]{3,2,1,0:T(8,128)(2,1)S(1)} all-to-all(bf16[16,2,64,128]{3,2,1,0:T(8,128)(2,1)S(1)} %pack_first.1), channel_id=1, replica_groups={{0,2,4,6,8,10,12,14,16,18,20,22,24,26,28,30},{1,3,5,7,9,11,13,15,17,19,..., dimensions={0} | all-to-all | bytes 1048576 | tf_op jit(solution)/shard_map/all_to_all | solution.py:313
  21.4 1.3 unpack_first.1
  22.6 0.0 collective-permute-done.w_other_ref
  22.7 1.7 keys.4
  24.4 3.3 %collective-permute-start.1 = (bf16[1344,512]{1,0:T(8,128)(2,1)S(1)}, bf16[1344,512]{1,0:T(8,128)(2,1)S(1)}, u32[]{:S(2)}, u32[]{:S(2)}) collective-permute-start(bf16[1344,512]{1,0:T(8,128)(2,1)S(1)} %get-tuple-element.27.own_ref), channel_id=1, source_target_pairs={{0,1},{1,0},{2,3},{3,2},{4,5},{5,4},{6,7},{7,6},{8,9},{9,8},{10,11... | collective-permute-start | bytes 4128776 | tf_op jit(solution)/shard_map/ppermute | solution.py:362
  27.7 0.5 queries.4.q_ref
  28.2 2.2 %collective-permute-done.1.other_ref.first_other_ref = bf16[1344,512]{1,0:T(8,128)(2,1)S(1)} collective-permute-done((bf16[1344,512]{1,0:T(8,128)(2,1)S(1)}, bf16[1344,512]{1,0:T(8,128)(2,1)S(1)}, u32[]{:S(2)}, u32[]{:S(2)}) %collective-permute-start.1) | collective-permute-done | bytes 1376288 | tf_op jit(solution)/shard_map/ppermute | solution.py:362
  30.4 1.0 attend.4
  31.4 13.4 %all_to_all.46.a_ref = bf16[16,2,64,128]{3,2,1,0:T(8,128)(2,1)S(1)} all-to-all(bf16[16,2,64,128]{3,2,1,0:T(8,128)(2,1)S(1)} %get-tuple-element.28), channel_id=1, replica_groups={{0,2,4,6,8,10,12,14,16,18,20,22,24,26,28,30},{1,3,5,7,9,11,13,15,17,19,..., dimensions={0} | all-to-all | bytes 1048576 | tf_op jit(solution)/shard_map/all_to_all | solution.py:313
  44.8 1.0 back.4.refs_0_
  45.8 2.6 %collective-permute-start.2 = (bf16[2,64,128]{2,1,0:T(8,128)(2,1)S(1)}, bf16[2,64,128]{2,1,0:T(8,128)(2,1)S(1)}, u32[]{:S(2)}, u32[]{:S(2)}) collective-permute-start(bf16[2,64,128]{2,1,0:T(8,128)(2,1)S(1)} %back.4.refs_0_), channel_id=1, source_target_pairs={{0,32},{32,64},{64,96},{96,128},{128,160},{160,192},{192,224},{224... | collective-permute-start | bytes 98312 | tf_op jit(solution)/shard_map/ppermute | solution.py:340
  48.5 3.2 %collective-permute-done.2.arrived_ref = bf16[2,64,128]{2,1,0:T(8,128)(2,1)S(1)} collective-permute-done((bf16[2,64,128]{2,1,0:T(8,128)(2,1)S(1)}, bf16[2,64,128]{2,1,0:T(8,128)(2,1)S(1)}, u32[]{:S(2)}, u32[]{:S(2)}) %collective-permute-start.2) | collective-permute-done | bytes 32800 | tf_op jit(solution)/shard_map/ppermute | solution.py:340
  51.7 0.1 spread.3
  51.8 12.5 %all_to_all.47.came_ref = bf16[16,2,64,128]{3,2,1,0:T(8,128)(2,1)S(1)} all-to-all(bf16[16,2,64,128]{3,2,1,0:T(8,128)(2,1)S(1)} %spread.3), channel_id=1, replica_groups={{0,2,4,6,8,10,12,14,16,18,20,22,24,26,28,30},{1,3,5,7,9,11,13,15,17,19,..., dimensions={0} | all-to-all | bytes 1048576 | tf_op jit(solution)/shard_map/all_to_all | solution.py:313
  64.3 1.5 keys.5
  65.8 5.4 %collective-permute-start.3 = (bf16[64,512]{1,0:T(8,128)(2,1)S(1)}, bf16[64,512]{1,0:T(8,128)(2,1)S(1)}, u32[]{:S(2)}, u32[]{:S(2)}) collective-permute-start(bf16[64,512]{1,0:T(8,128)(2,1)S(1)} %get-tuple-element.30.own_ref), channel_id=1, source_target_pairs={{0,1},{1,0},{2,3},{3,2},{4,5},{5,4},{6,7},{7,6},{8,9},{9,8},{10,11... | collective-permute-start | bytes 196616 | tf_op jit(solution)/shard_map/ppermute | solution.py:362
  71.2 0.5 queries.5.q_ref
  71.6 0.4 collective-permute-done.3.other_ref
  72.0 1.0 attend.5
  73.0 13.5 %all_to_all.48.a_ref = bf16[16,2,64,128]{3,2,1,0:T(8,128)(2,1)S(1)} all-to-all(bf16[16,2,64,128]{3,2,1,0:T(8,128)(2,1)S(1)} %get-tuple-element.32), channel_id=1, replica_groups={{0,2,4,6,8,10,12,14,16,18,20,22,24,26,28,30},{1,3,5,7,9,11,13,15,17,19,..., dimensions={0} | all-to-all | bytes 1048576 | tf_op jit(solution)/shard_map/all_to_all | solution.py:313
  86.5 1.0 back.5.refs_1_
  87.5 1.9 %collective-permute-start.4 = (bf16[2,64,128]{2,1,0:T(8,128)(2,1)S(1)}, bf16[2,64,128]{2,1,0:T(8,128)(2,1)S(1)}, u32[]{:S(2)}, u32[]{:S(2)}) collective-permute-start(bf16[2,64,128]{2,1,0:T(8,128)(2,1)S(1)} %back.5.refs_1_), channel_id=1, source_target_pairs={{0,32},{32,64},{64,96},{96,128},{128,160},{160,192},{192,224},{224... | collective-permute-start | bytes 98312 | tf_op jit(solution)/shard_map/ppermute | solution.py:340
  89.5 3.9 %collective-permute-done.4.arrived_ref = bf16[2,64,128]{2,1,0:T(8,128)(2,1)S(1)} collective-permute-done((bf16[2,64,128]{2,1,0:T(8,128)(2,1)S(1)}, bf16[2,64,128]{2,1,0:T(8,128)(2,1)S(1)}, u32[]{:S(2)}, u32[]{:S(2)}) %collective-permute-start.4) | collective-permute-done | bytes 32800 | tf_op jit(solution)/shard_map/ppermute | solution.py:340
  93.4 0.1 spread.4
  93.5 12.5 %all_to_all.49.came_ref = bf16[16,2,64,128]{3,2,1,0:T(8,128)(2,1)S(1)} all-to-all(bf16[16,2,64,128]{3,2,1,0:T(8,128)(2,1)S(1)} %spread.4), channel_id=1, replica_groups={{0,2,4,6,8,10,12,14,16,18,20,22,24,26,28,30},{1,3,5,7,9,11,13,15,17,19,..., dimensions={0} | all-to-all | bytes 1048576 | tf_op jit(solution)/shard_map/all_to_all | solution.py:313
  106.0 1.5 keys.6
  107.5 5.4 %collective-permute-start.5 = (bf16[64,512]{1,0:T(8,128)(2,1)S(1)}, bf16[64,512]{1,0:T(8,128)(2,1)S(1)}, u32[]{:S(2)}, u32[]{:S(2)}) collective-permute-start(bf16[64,512]{1,0:T(8,128)(2,1)S(1)} %get-tuple-element.34.own_ref), channel_id=1, source_target_pairs={{0,1},{1,0},{2,3},{3,2},{4,5},{5,4},{6,7},{7,6},{8,9},{9,8},{10,11... | collective-permute-start | bytes 196616 | tf_op jit(solution)/shard_map/ppermute | solution.py:362
  112.9 0.5 queries.6.q_ref
  113.4 0.4 collective-permute-done.5.other_ref
  113.8 1.0 attend.6
  114.8 13.5 %all_to_all.50.a_ref = bf16[16,2,64,128]{3,2,1,0:T(8,128)(2,1)S(1)} all-to-all(bf16[16,2,64,128]{3,2,1,0:T(8,128)(2,1)S(1)} %get-tuple-element.36), channel_id=1, replica_groups={{0,2,4,6,8,10,12,14,16,18,20,22,24,26,28,30},{1,3,5,7,9,11,13,15,17,19,..., dimensions={0} | all-to-all | bytes 1048576 | tf_op jit(solution)/shard_map/all_to_all | solution.py:313
  128.2 1.0 back.6.refs_2_
  129.3 1.9 %collective-permute-start.6 = (bf16[2,64,128]{2,1,0:T(8,128)(2,1)S(1)}, bf16[2,64,128]{2,1,0:T(8,128)(2,1)S(1)}, u32[]{:S(2)}, u32[]{:S(2)}) collective-permute-start(bf16[2,64,128]{2,1,0:T(8,128)(2,1)S(1)} %back.6.refs_2_), channel_id=1, source_target_pairs={{0,32},{32,64},{64,96},{96,128},{128,160},{160,192},{192,224},{224... | collective-permute-start | bytes 98312 | tf_op jit(solution)/shard_map/ppermute | solution.py:340
  131.2 3.9 %collective-permute-done.6.arrived_ref = bf16[2,64,128]{2,1,0:T(8,128)(2,1)S(1)} collective-permute-done((bf16[2,64,128]{2,1,0:T(8,128)(2,1)S(1)}, bf16[2,64,128]{2,1,0:T(8,128)(2,1)S(1)}, u32[]{:S(2)}, u32[]{:S(2)}) %collective-permute-start.6) | collective-permute-done | bytes 32800 | tf_op jit(solution)/shard_map/ppermute | solution.py:340
  135.1 0.1 spread.5
  135.2 12.5 %all_to_all.51.came_ref = bf16[16,2,64,128]{3,2,1,0:T(8,128)(2,1)S(1)} all-to-all(bf16[16,2,64,128]{3,2,1,0:T(8,128)(2,1)S(1)} %spread.5), channel_id=1, replica_groups={{0,2,4,6,8,10,12,14,16,18,20,22,24,26,28,30},{1,3,5,7,9,11,13,15,17,19,..., dimensions={0} | all-to-all | bytes 1048576 | tf_op jit(solution)/shard_map/all_to_all | solution.py:313
  147.7 1.5 keys.7
  149.2 5.4 %collective-permute-start.7 = (bf16[64,512]{1,0:T(8,128)(2,1)S(1)}, bf16[64,512]{1,0:T(8,128)(2,1)S(1)}, u32[]{:S(2)}, u32[]{:S(2)}) collective-permute-start(bf16[64,512]{1,0:T(8,128)(2,1)S(1)} %get-tuple-element.38.own_ref), channel_id=1, source_target_pairs={{0,1},{1,0},{2,3},{3,2},{4,5},{5,4},{6,7},{7,6},{8,9},{9,8},{10,11... | collective-permute-start | bytes 196616 | tf_op jit(solution)/shard_map/ppermute | solution.py:362
  154.6 0.5 queries.7.q_ref
  155.1 0.4 collective-permute-done.7.other_ref
  155.5 1.0 attend.7
  156.5 13.5 %all_to_all.52.a_ref = bf16[16,2,64,128]{3,2,1,0:T(8,128)(2,1)S(1)} all-to-all(bf16[16,2,64,128]{3,2,1,0:T(8,128)(2,1)S(1)} %get-tuple-element.40), channel_id=1, replica_groups={{0,2,4,6,8,10,12,14,16,18,20,22,24,26,28,30},{1,3,5,7,9,11,13,15,17,19,..., dimensions={0} | all-to-all | bytes 1048576 | tf_op jit(solution)/shard_map/all_to_all | solution.py:313
  169.9 1.0 back.7.refs_3_
  171.0 0.1 pack_last.1
  171.1 10.1 %all_to_all.53.came_ref = bf16[16,32,128]{2,1,0:T(8,128)(2,1)S(1)} all-to-all(bf16[16,32,128]{2,1,0:T(8,128)(2,1)S(1)} %pack_last.1), channel_id=1, replica_groups={{0,2,4,6,8,10,12,14,16,18,20,22,24,26,28,30},{1,3,5,7,9,11,13,15,17,19,..., dimensions={0} | all-to-all | bytes 262144 | tf_op jit(solution)/shard_map/all_to_all | solution.py:313
  181.2 1.3 unpack_last.1
  (9 shorter events, 0.0 us)
Async XLA Ops:
  0.0 22.7 %copy-start = (bf16[1,4096,3,128]{3,1,2,0:T(8,128)(2,1)S(1)}, bf16[1,4096,3,128]{3,1,2,0:T(8,128)(2,1)}, u32[]{:S(2)}) copy-start(bf16[1,4096,3,128]{3,1,2,0:T(8,128)(2,1)} %param.11) | copy-start | bytes 9437188
  0.0 22.7 %copy-start.2 = (s32[4]{0:T(128)S(1)}, s32[4]{0:T(128)}, u32[]{:S(2)}) copy-start(s32[4]{0:T(128)} %frames_ref.25) | copy-start | bytes 52
  0.0 22.7 %copy-start.1 = (bf16[1,4096]{1,0:T(2,128)(2,1)S(1)}, bf16[1,4096]{1,0:T(2,128)(2,1)}, u32[]{:S(2)}) copy-start(bf16[1,4096]{1,0:T(2,128)(2,1)} %gain_ref.7) | copy-start | bytes 24580
  0.0 22.6 %collective-permute-start = (bf16[3,4096,128]{2,1,0:T(8,128)(2,1)}, bf16[3,4096,128]{2,1,0:T(8,128)(2,1)S(1)}, u32[]{:S(2)}, u32[]{:S(2)}) collective-permute-start(bf16[3,4096,128]{2,1,0:T(8,128)(2,1)} %bitcast.6), channel_id=1, source_target_pairs={{0,1},{1,0},{2,3},{3,2},{4,5},{5,4},{6,7},{7,6},{8,9},{9,8},{10,11... | collective-permute-start | bytes 9437192 | tf_op jit(solution)/shard_map/ppermute | solution.py:318
  24.4 6.1 %collective-permute-start.1 = (bf16[1344,512]{1,0:T(8,128)(2,1)S(1)}, bf16[1344,512]{1,0:T(8,128)(2,1)S(1)}, u32[]{:S(2)}, u32[]{:S(2)}) collective-permute-start(bf16[1344,512]{1,0:T(8,128)(2,1)S(1)} %get-tuple-element.27.own_ref), channel_id=1, source_target_pairs={{0,1},{1,0},{2,3},{3,2},{4,5},{5,4},{6,7},{7,6},{8,9},{9,8},{10,11... | collective-permute-start | bytes 4128776 | tf_op jit(solution)/shard_map/ppermute | solution.py:362
  45.8 5.9 %collective-permute-start.2 = (bf16[2,64,128]{2,1,0:T(8,128)(2,1)S(1)}, bf16[2,64,128]{2,1,0:T(8,128)(2,1)S(1)}, u32[]{:S(2)}, u32[]{:S(2)}) collective-permute-start(bf16[2,64,128]{2,1,0:T(8,128)(2,1)S(1)} %back.4.refs_0_), channel_id=1, source_target_pairs={{0,32},{32,64},{64,96},{96,128},{128,160},{160,192},{192,224},{224... | collective-permute-start | bytes 98312 | tf_op jit(solution)/shard_map/ppermute | solution.py:340
  65.8 6.3 %collective-permute-start.3 = (bf16[64,512]{1,0:T(8,128)(2,1)S(1)}, bf16[64,512]{1,0:T(8,128)(2,1)S(1)}, u32[]{:S(2)}, u32[]{:S(2)}) collective-permute-start(bf16[64,512]{1,0:T(8,128)(2,1)S(1)} %get-tuple-element.30.own_ref), channel_id=1, source_target_pairs={{0,1},{1,0},{2,3},{3,2},{4,5},{5,4},{6,7},{7,6},{8,9},{9,8},{10,11... | collective-permute-start | bytes 196616 | tf_op jit(solution)/shard_map/ppermute | solution.py:362
  87.5 5.9 %collective-permute-start.4 = (bf16[2,64,128]{2,1,0:T(8,128)(2,1)S(1)}, bf16[2,64,128]{2,1,0:T(8,128)(2,1)S(1)}, u32[]{:S(2)}, u32[]{:S(2)}) collective-permute-start(bf16[2,64,128]{2,1,0:T(8,128)(2,1)S(1)} %back.5.refs_1_), channel_id=1, source_target_pairs={{0,32},{32,64},{64,96},{96,128},{128,160},{160,192},{192,224},{224... | collective-permute-start | bytes 98312 | tf_op jit(solution)/shard_map/ppermute | solution.py:340
  107.5 6.2 %collective-permute-start.5 = (bf16[64,512]{1,0:T(8,128)(2,1)S(1)}, bf16[64,512]{1,0:T(8,128)(2,1)S(1)}, u32[]{:S(2)}, u32[]{:S(2)}) collective-permute-start(bf16[64,512]{1,0:T(8,128)(2,1)S(1)} %get-tuple-element.34.own_ref), channel_id=1, source_target_pairs={{0,1},{1,0},{2,3},{3,2},{4,5},{5,4},{6,7},{7,6},{8,9},{9,8},{10,11... | collective-permute-start | bytes 196616 | tf_op jit(solution)/shard_map/ppermute | solution.py:362
  129.3 5.9 %collective-permute-start.6 = (bf16[2,64,128]{2,1,0:T(8,128)(2,1)S(1)}, bf16[2,64,128]{2,1,0:T(8,128)(2,1)S(1)}, u32[]{:S(2)}, u32[]{:S(2)}) collective-permute-start(bf16[2,64,128]{2,1,0:T(8,128)(2,1)S(1)} %back.6.refs_2_), channel_id=1, source_target_pairs={{0,32},{32,64},{64,96},{96,128},{128,160},{160,192},{192,224},{224... | collective-permute-start | bytes 98312 | tf_op jit(solution)/shard_map/ppermute | solution.py:340
  149.2 6.2 %collective-permute-start.7 = (bf16[64,512]{1,0:T(8,128)(2,1)S(1)}, bf16[64,512]{1,0:T(8,128)(2,1)S(1)}, u32[]{:S(2)}, u32[]{:S(2)}) collective-permute-start(bf16[64,512]{1,0:T(8,128)(2,1)S(1)} %get-tuple-element.38.own_ref), channel_id=1, source_target_pairs={{0,1},{1,0},{2,3},{3,2},{4,5},{5,4},{6,7},{7,6},{8,9},{9,8},{10,11... | collective-permute-start | bytes 196616 | tf_op jit(solution)/shard_map/ppermute | solution.py:362

commit v8 on v7

--- a/solution.py
+++ b/solution.py
@@ -11,6 +11,7 @@
 HDIM = 128
 CORES = 2
 WEIGHT_PARTS = 4
+SUBLANES = 8
 MOST_SECTIONS = 1024
 VMEM_LIMIT = 12 * 1024 * 1024
 
@@ -286,7 +287,7 @@
         wide = came_ref[chip].astype(jnp.float32)
         for half in range(CORES):
             first = (chip * CORES + half) * width
-            turn_ref[:, first:first + width] = wide[half * each:(half + 1) * each]
+            turn_ref[:each, first:first + width] = wide[half * each:(half + 1) * each]
     for tick in range(patches):
         slot = slot_of(frames_ref, tick)
         for frame in range(frames):
@@ -320,7 +321,7 @@
     block_dims = (chips, halves, rows, HDIM)
     token_scratch = [
         pltpu.VMEM((frames, local, width), jnp.bfloat16),
-        pltpu.VMEM((owned * blocks, HDIM), jnp.float32),
+        pltpu.VMEM(((owned + SUBLANES) * blocks, HDIM), jnp.float32),
         pltpu.SemaphoreType.DMA((1,)),
     ]
     wide = pltpu.VMEM((chips * halves * rows, HDIM), jnp.float32)
@@ -396,7 +397,7 @@
         shape(patches, frames, local, width),
         (patch_frames,),
         (swap(sent),),
-        [pltpu.VMEM((ticks * owned, width), jnp.float32)],
+        [pltpu.VMEM((ticks * owned + SUBLANES, width), jnp.float32)],
     )
     return outputs[None]
 

time: 185 us -> 185 us (level)
  no operation moved by 1% of the time
where the time goes in v8:
time: 185 us; the launch traced here: 182 us
  blocking collectives  119 us (64%)
  starting transfers between devices  28.7 us (16%)
  Pallas kernels  20 us (11%)
  waiting for transfers between devices  14.5 us (8%)
    all_to_all x9, blocking collectives, swap(): lax.all_to_all(value, 'seq', split_axis=0, concat_axis=0, tiled=True, axi...  119 us
    pallas_call x26, Pallas kernels, call(): pl.pallas_call(body, out_shape=out_shape, in_specs=[in_smem] * len(scalar...  20 us
    ppermute x4, starting transfers between devices, on_device(): other = lax.ppermute(own, 'seq', partner)  19.4 us
    ppermute x3, waiting for transfers between devices, on_device(): lax.ppermute(results[-1], 'section', [(source, source + 1) for source in...  11.1 us
    ppermute x3, starting transfers between devices, on_device(): lax.ppermute(results[-1], 'section', [(source, source + 1) for source in...  6.48 us
  transfers between devices with their start and end apart: 8, of which 7 were waited for; matrix products, arithmetic and copies ran while one was open for 0% of the time, Pallas kernels for 2%

profile of v8, /device:TPU:385, one launch (start us, length us, event | category | flops | bytes accessed | tf_op | source)
XLA Modules:
  0.0 182.5 jit_solution(16757636535144806666)
XLA Ops:
  0.0 2.8 %collective-permute-start = (bf16[3,4096,128]{2,1,0:T(8,128)(2,1)}, bf16[3,4096,128]{2,1,0:T(8,128)(2,1)S(1)}, u32[]{:S(2)}, u32[]{:S(2)}) collective-permute-start(bf16[3,4096,128]{2,1,0:T(8,128)(2,1)} %bitcast.6), channel_id=1, source_target_pairs={{0,1},{1,0},{2,3},{3,2},{4,5},{5,4},{6,7},{7,6},{8,9},{9,8},{10,11... | collective-permute-start | bytes 9437192 | tf_op jit(solution)/shard_map/ppermute | solution.py:319
  2.9 0.8 pack_first.1
  3.7 17.6 %all_to_all.45.came_ref = bf16[16,2,64,128]{3,2,1,0:T(8,128)(2,1)S(1)} all-to-all(bf16[16,2,64,128]{3,2,1,0:T(8,128)(2,1)S(1)} %pack_first.1), channel_id=1, replica_groups={{0,2,4,6,8,10,12,14,16,18,20,22,24,26,28,30},{1,3,5,7,9,11,13,15,17,19,..., dimensions={0} | all-to-all | bytes 1048576 | tf_op jit(solution)/shard_map/all_to_all | solution.py:314
  21.4 1.3 unpack_first.1
  22.6 0.0 collective-permute-done.w_other_ref
  22.7 1.7 keys.4
  24.4 3.3 %collective-permute-start.1 = (bf16[1344,512]{1,0:T(8,128)(2,1)S(1)}, bf16[1344,512]{1,0:T(8,128)(2,1)S(1)}, u32[]{:S(2)}, u32[]{:S(2)}) collective-permute-start(bf16[1344,512]{1,0:T(8,128)(2,1)S(1)} %get-tuple-element.27.own_ref), channel_id=1, source_target_pairs={{0,1},{1,0},{2,3},{3,2},{4,5},{5,4},{6,7},{7,6},{8,9},{9,8},{10,11... | collective-permute-start | bytes 4128776 | tf_op jit(solution)/shard_map/ppermute | solution.py:363
  27.7 0.5 queries.4.q_ref
  28.2 2.2 %collective-permute-done.1.other_ref.first_other_ref = bf16[1344,512]{1,0:T(8,128)(2,1)S(1)} collective-permute-done((bf16[1344,512]{1,0:T(8,128)(2,1)S(1)}, bf16[1344,512]{1,0:T(8,128)(2,1)S(1)}, u32[]{:S(2)}, u32[]{:S(2)}) %collective-permute-start.1) | collective-permute-done | bytes 1376288 | tf_op jit(solution)/shard_map/ppermute | solution.py:363
  30.4 1.0 attend.4
  31.4 13.4 %all_to_all.46.a_ref = bf16[16,2,64,128]{3,2,1,0:T(8,128)(2,1)S(1)} all-to-all(bf16[16,2,64,128]{3,2,1,0:T(8,128)(2,1)S(1)} %get-tuple-element.28), channel_id=1, replica_groups={{0,2,4,6,8,10,12,14,16,18,20,22,24,26,28,30},{1,3,5,7,9,11,13,15,17,19,..., dimensions={0} | all-to-all | bytes 1048576 | tf_op jit(solution)/shard_map/all_to_all | solution.py:314
  44.8 1.0 back.4.refs_0_
  45.8 2.6 %collective-permute-start.2 = (bf16[2,64,128]{2,1,0:T(8,128)(2,1)S(1)}, bf16[2,64,128]{2,1,0:T(8,128)(2,1)S(1)}, u32[]{:S(2)}, u32[]{:S(2)}) collective-permute-start(bf16[2,64,128]{2,1,0:T(8,128)(2,1)S(1)} %back.4.refs_0_), channel_id=1, source_target_pairs={{0,32},{32,64},{64,96},{96,128},{128,160},{160,192},{192,224},{224... | collective-permute-start | bytes 98312 | tf_op jit(solution)/shard_map/ppermute | solution.py:341
  48.5 3.2 %collective-permute-done.2.arrived_ref = bf16[2,64,128]{2,1,0:T(8,128)(2,1)S(1)} collective-permute-done((bf16[2,64,128]{2,1,0:T(8,128)(2,1)S(1)}, bf16[2,64,128]{2,1,0:T(8,128)(2,1)S(1)}, u32[]{:S(2)}, u32[]{:S(2)}) %collective-permute-start.2) | collective-permute-done | bytes 32800 | tf_op jit(solution)/shard_map/ppermute | solution.py:341
  51.7 0.1 spread.3
  51.8 12.5 %all_to_all.47.came_ref = bf16[16,2,64,128]{3,2,1,0:T(8,128)(2,1)S(1)} all-to-all(bf16[16,2,64,128]{3,2,1,0:T(8,128)(2,1)S(1)} %spread.3), channel_id=1, replica_groups={{0,2,4,6,8,10,12,14,16,18,20,22,24,26,28,30},{1,3,5,7,9,11,13,15,17,19,..., dimensions={0} | all-to-all | bytes 1048576 | tf_op jit(solution)/shard_map/all_to_all | solution.py:314
  64.3 1.5 keys.5
  65.8 5.4 %collective-permute-start.3 = (bf16[64,512]{1,0:T(8,128)(2,1)S(1)}, bf16[64,512]{1,0:T(8,128)(2,1)S(1)}, u32[]{:S(2)}, u32[]{:S(2)}) collective-permute-start(bf16[64,512]{1,0:T(8,128)(2,1)S(1)} %get-tuple-element.30.own_ref), channel_id=1, source_target_pairs={{0,1},{1,0},{2,3},{3,2},{4,5},{5,4},{6,7},{7,6},{8,9},{9,8},{10,11... | collective-permute-start | bytes 196616 | tf_op jit(solution)/shard_map/ppermute | solution.py:363
  71.2 0.5 queries.5.q_ref
  71.6 0.4 collective-permute-done.3.other_ref
  72.0 1.0 attend.5
  73.0 13.5 %all_to_all.48.a_ref = bf16[16,2,64,128]{3,2,1,0:T(8,128)(2,1)S(1)} all-to-all(bf16[16,2,64,128]{3,2,1,0:T(8,128)(2,1)S(1)} %get-tuple-element.32), channel_id=1, replica_groups={{0,2,4,6,8,10,12,14,16,18,20,22,24,26,28,30},{1,3,5,7,9,11,13,15,17,19,..., dimensions={0} | all-to-all | bytes 1048576 | tf_op jit(solution)/shard_map/all_to_all | solution.py:314
  86.5 1.0 back.5.refs_1_
  87.5 1.9 %collective-permute-start.4 = (bf16[2,64,128]{2,1,0:T(8,128)(2,1)S(1)}, bf16[2,64,128]{2,1,0:T(8,128)(2,1)S(1)}, u32[]{:S(2)}, u32[]{:S(2)}) collective-permute-start(bf16[2,64,128]{2,1,0:T(8,128)(2,1)S(1)} %back.5.refs_1_), channel_id=1, source_target_pairs={{0,32},{32,64},{64,96},{96,128},{128,160},{160,192},{192,224},{224... | collective-permute-start | bytes 98312 | tf_op jit(solution)/shard_map/ppermute | solution.py:341
  89.5 3.9 %collective-permute-done.4.arrived_ref = bf16[2,64,128]{2,1,0:T(8,128)(2,1)S(1)} collective-permute-done((bf16[2,64,128]{2,1,0:T(8,128)(2,1)S(1)}, bf16[2,64,128]{2,1,0:T(8,128)(2,1)S(1)}, u32[]{:S(2)}, u32[]{:S(2)}) %collective-permute-start.4) | collective-permute-done | bytes 32800 | tf_op jit(solution)/shard_map/ppermute | solution.py:341
  93.4 0.1 spread.4
  93.5 12.5 %all_to_all.49.came_ref = bf16[16,2,64,128]{3,2,1,0:T(8,128)(2,1)S(1)} all-to-all(bf16[16,2,64,128]{3,2,1,0:T(8,128)(2,1)S(1)} %spread.4), channel_id=1, replica_groups={{0,2,4,6,8,10,12,14,16,18,20,22,24,26,28,30},{1,3,5,7,9,11,13,15,17,19,..., dimensions={0} | all-to-all | bytes 1048576 | tf_op jit(solution)/shard_map/all_to_all | solution.py:314
  106.0 1.5 keys.6
  107.5 5.4 %collective-permute-start.5 = (bf16[64,512]{1,0:T(8,128)(2,1)S(1)}, bf16[64,512]{1,0:T(8,128)(2,1)S(1)}, u32[]{:S(2)}, u32[]{:S(2)}) collective-permute-start(bf16[64,512]{1,0:T(8,128)(2,1)S(1)} %get-tuple-element.34.own_ref), channel_id=1, source_target_pairs={{0,1},{1,0},{2,3},{3,2},{4,5},{5,4},{6,7},{7,6},{8,9},{9,8},{10,11... | collective-permute-start | bytes 196616 | tf_op jit(solution)/shard_map/ppermute | solution.py:363
  112.9 0.5 queries.6.q_ref
  113.4 0.4 collective-permute-done.5.other_ref
  113.8 1.0 attend.6
  114.8 13.5 %all_to_all.50.a_ref = bf16[16,2,64,128]{3,2,1,0:T(8,128)(2,1)S(1)} all-to-all(bf16[16,2,64,128]{3,2,1,0:T(8,128)(2,1)S(1)} %get-tuple-element.36), channel_id=1, replica_groups={{0,2,4,6,8,10,12,14,16,18,20,22,24,26,28,30},{1,3,5,7,9,11,13,15,17,19,..., dimensions={0} | all-to-all | bytes 1048576 | tf_op jit(solution)/shard_map/all_to_all | solution.py:314
  128.2 1.0 back.6.refs_2_
  129.3 1.9 %collective-permute-start.6 = (bf16[2,64,128]{2,1,0:T(8,128)(2,1)S(1)}, bf16[2,64,128]{2,1,0:T(8,128)(2,1)S(1)}, u32[]{:S(2)}, u32[]{:S(2)}) collective-permute-start(bf16[2,64,128]{2,1,0:T(8,128)(2,1)S(1)} %back.6.refs_2_), channel_id=1, source_target_pairs={{0,32},{32,64},{64,96},{96,128},{128,160},{160,192},{192,224},{224... | collective-permute-start | bytes 98312 | tf_op jit(solution)/shard_map/ppermute | solution.py:341
  131.2 3.9 %collective-permute-done.6.arrived_ref = bf16[2,64,128]{2,1,0:T(8,128)(2,1)S(1)} collective-permute-done((bf16[2,64,128]{2,1,0:T(8,128)(2,1)S(1)}, bf16[2,64,128]{2,1,0:T(8,128)(2,1)S(1)}, u32[]{:S(2)}, u32[]{:S(2)}) %collective-permute-start.6) | collective-permute-done | bytes 32800 | tf_op jit(solution)/shard_map/ppermute | solution.py:341
  135.1 0.1 spread.5
  135.2 12.5 %all_to_all.51.came_ref = bf16[16,2,64,128]{3,2,1,0:T(8,128)(2,1)S(1)} all-to-all(bf16[16,2,64,128]{3,2,1,0:T(8,128)(2,1)S(1)} %spread.5), channel_id=1, replica_groups={{0,2,4,6,8,10,12,14,16,18,20,22,24,26,28,30},{1,3,5,7,9,11,13,15,17,19,..., dimensions={0} | all-to-all | bytes 1048576 | tf_op jit(solution)/shard_map/all_to_all | solution.py:314
  147.7 1.5 keys.7
  149.2 5.4 %collective-permute-start.7 = (bf16[64,512]{1,0:T(8,128)(2,1)S(1)}, bf16[64,512]{1,0:T(8,128)(2,1)S(1)}, u32[]{:S(2)}, u32[]{:S(2)}) collective-permute-start(bf16[64,512]{1,0:T(8,128)(2,1)S(1)} %get-tuple-element.38.own_ref), channel_id=1, source_target_pairs={{0,1},{1,0},{2,3},{3,2},{4,5},{5,4},{6,7},{7,6},{8,9},{9,8},{10,11... | collective-permute-start | bytes 196616 | tf_op jit(solution)/shard_map/ppermute | solution.py:363
  154.6 0.5 queries.7.q_ref
  155.1 0.4 collective-permute-done.7.other_ref
  155.5 1.0 attend.7
  156.5 13.5 %all_to_all.52.a_ref = bf16[16,2,64,128]{3,2,1,0:T(8,128)(2,1)S(1)} all-to-all(bf16[16,2,64,128]{3,2,1,0:T(8,128)(2,1)S(1)} %get-tuple-element.40), channel_id=1, replica_groups={{0,2,4,6,8,10,12,14,16,18,20,22,24,26,28,30},{1,3,5,7,9,11,13,15,17,19,..., dimensions={0} | all-to-all | bytes 1048576 | tf_op jit(solution)/shard_map/all_to_all | solution.py:314
  169.9 1.0 back.7.refs_3_
  171.0 0.1 pack_last.1
  171.1 10.1 %all_to_all.53.came_ref = bf16[16,32,128]{2,1,0:T(8,128)(2,1)S(1)} all-to-all(bf16[16,32,128]{2,1,0:T(8,128)(2,1)S(1)} %pack_last.1), channel_id=1, replica_groups={{0,2,4,6,8,10,12,14,16,18,20,22,24,26,28,30},{1,3,5,7,9,11,13,15,17,19,..., dimensions={0} | all-to-all | bytes 262144 | tf_op jit(solution)/shard_map/all_to_all | solution.py:314
  181.2 1.3 unpack_last.1
  (9 shorter events, 0.0 us)
Async XLA Ops:
  0.0 22.7 %copy-start = (bf16[1,4096,3,128]{3,1,2,0:T(8,128)(2,1)S(1)}, bf16[1,4096,3,128]{3,1,2,0:T(8,128)(2,1)}, u32[]{:S(2)}) copy-start(bf16[1,4096,3,128]{3,1,2,0:T(8,128)(2,1)} %param.11) | copy-start | bytes 9437188
  0.0 22.7 %copy-start.2 = (s32[4]{0:T(128)S(1)}, s32[4]{0:T(128)}, u32[]{:S(2)}) copy-start(s32[4]{0:T(128)} %frames_ref.25) | copy-start | bytes 52
  0.0 22.7 %copy-start.1 = (bf16[1,4096]{1,0:T(2,128)(2,1)S(1)}, bf16[1,4096]{1,0:T(2,128)(2,1)}, u32[]{:S(2)}) copy-start(bf16[1,4096]{1,0:T(2,128)(2,1)} %gain_ref.7) | copy-start | bytes 24580
  0.0 22.6 %collective-permute-start = (bf16[3,4096,128]{2,1,0:T(8,128)(2,1)}, bf16[3,4096,128]{2,1,0:T(8,128)(2,1)S(1)}, u32[]{:S(2)}, u32[]{:S(2)}) collective-permute-start(bf16[3,4096,128]{2,1,0:T(8,128)(2,1)} %bitcast.6), channel_id=1, source_target_pairs={{0,1},{1,0},{2,3},{3,2},{4,5},{5,4},{6,7},{7,6},{8,9},{9,8},{10,11... | collective-permute-start | bytes 9437192 | tf_op jit(solution)/shard_map/ppermute | solution.py:319
  24.4 6.1 %collective-permute-start.1 = (bf16[1344,512]{1,0:T(8,128)(2,1)S(1)}, bf16[1344,512]{1,0:T(8,128)(2,1)S(1)}, u32[]{:S(2)}, u32[]{:S(2)}) collective-permute-start(bf16[1344,512]{1,0:T(8,128)(2,1)S(1)} %get-tuple-element.27.own_ref), channel_id=1, source_target_pairs={{0,1},{1,0},{2,3},{3,2},{4,5},{5,4},{6,7},{7,6},{8,9},{9,8},{10,11... | collective-permute-start | bytes 4128776 | tf_op jit(solution)/shard_map/ppermute | solution.py:363
  45.8 5.9 %collective-permute-start.2 = (bf16[2,64,128]{2,1,0:T(8,128)(2,1)S(1)}, bf16[2,64,128]{2,1,0:T(8,128)(2,1)S(1)}, u32[]{:S(2)}, u32[]{:S(2)}) collective-permute-start(bf16[2,64,128]{2,1,0:T(8,128)(2,1)S(1)} %back.4.refs_0_), channel_id=1, source_target_pairs={{0,32},{32,64},{64,96},{96,128},{128,160},{160,192},{192,224},{224... | collective-permute-start | bytes 98312 | tf_op jit(solution)/shard_map/ppermute | solution.py:341
  65.8 6.3 %collective-permute-start.3 = (bf16[64,512]{1,0:T(8,128)(2,1)S(1)}, bf16[64,512]{1,0:T(8,128)(2,1)S(1)}, u32[]{:S(2)}, u32[]{:S(2)}) collective-permute-start(bf16[64,512]{1,0:T(8,128)(2,1)S(1)} %get-tuple-element.30.own_ref), channel_id=1, source_target_pairs={{0,1},{1,0},{2,3},{3,2},{4,5},{5,4},{6,7},{7,6},{8,9},{9,8},{10,11... | collective-permute-start | bytes 196616 | tf_op jit(solution)/shard_map/ppermute | solution.py:363
  87.5 5.9 %collective-permute-start.4 = (bf16[2,64,128]{2,1,0:T(8,128)(2,1)S(1)}, bf16[2,64,128]{2,1,0:T(8,128)(2,1)S(1)}, u32[]{:S(2)}, u32[]{:S(2)}) collective-permute-start(bf16[2,64,128]{2,1,0:T(8,128)(2,1)S(1)} %back.5.refs_1_), channel_id=1, source_target_pairs={{0,32},{32,64},{64,96},{96,128},{128,160},{160,192},{192,224},{224... | collective-permute-start | bytes 98312 | tf_op jit(solution)/shard_map/ppermute | solution.py:341
  107.5 6.2 %collective-permute-start.5 = (bf16[64,512]{1,0:T(8,128)(2,1)S(1)}, bf16[64,512]{1,0:T(8,128)(2,1)S(1)}, u32[]{:S(2)}, u32[]{:S(2)}) collective-permute-start(bf16[64,512]{1,0:T(8,128)(2,1)S(1)} %get-tuple-element.34.own_ref), channel_id=1, source_target_pairs={{0,1},{1,0},{2,3},{3,2},{4,5},{5,4},{6,7},{7,6},{8,9},{9,8},{10,11... | collective-permute-start | bytes 196616 | tf_op jit(solution)/shard_map/ppermute | solution.py:363
  129.3 5.9 %collective-permute-start.6 = (bf16[2,64,128]{2,1,0:T(8,128)(2,1)S(1)}, bf16[2,64,128]{2,1,0:T(8,128)(2,1)S(1)}, u32[]{:S(2)}, u32[]{:S(2)}) collective-permute-start(bf16[2,64,128]{2,1,0:T(8,128)(2,1)S(1)} %back.6.refs_2_), channel_id=1, source_target_pairs={{0,32},{32,64},{64,96},{96,128},{128,160},{160,192},{192,224},{224... | collective-permute-start | bytes 98312 | tf_op jit(solution)/shard_map/ppermute | solution.py:341
  149.2 6.2 %collective-permute-start.7 = (bf16[64,512]{1,0:T(8,128)(2,1)S(1)}, bf16[64,512]{1,0:T(8,128)(2,1)S(1)}, u32[]{:S(2)}, u32[]{:S(2)}) collective-permute-start(bf16[64,512]{1,0:T(8,128)(2,1)S(1)} %get-tuple-element.38.own_ref), channel_id=1, source_target_pairs={{0,1},{1,0},{2,3},{3,2},{4,5},{5,4},{6,7},{7,6},{8,9},{9,8},{10,11... | collective-permute-start | bytes 196616 | tf_op jit(solution)/shard_map/ppermute | solution.py:363

commit v9 on v8

--- a/solution.py
+++ b/solution.py
@@ -137,7 +137,8 @@
 
 
 def layer_keys(tick, frames, frames_ref, x_ref, gain_ref, w_own_ref, w_other_ref, *refs):
-    *first_refs, xn_ref, new_ref = refs if tick else refs[:-1]
+    *first_refs, q_ref, both_ref, xn_ref = refs if tick else refs[:-1]
+    new_ref = both_ref.at[0]
     chips, halves, tokens, width = x_ref.shape
     pair = halves * width
     squares = jnp.zeros((tokens, width), jnp.float32)
@@ -175,20 +176,17 @@
             new_ref[stale_end:weight_end, part * width:(part + 1) * width] = out_ref[
                 part * part_rows:(part + 1) * part_rows
             ]
-
-
-def layer_queries(xn_ref, w_own_ref, w_other_ref, out_ref):
-    pair = out_ref.shape[1]
-    total = jnp.zeros(out_ref.shape, jnp.float32)
-    for first in range(0, xn_ref.shape[1], pair):
-        span = slice(first, first + pair)
+    both_ref[1] = both_ref[0]
+    total = jnp.zeros(q_ref.shape, jnp.float32)
+    for chip in range(chips):
+        span = slice(chip * pair, (chip + 1) * pair)
         total = total + jnp.dot(
             xn_ref[:, span], two_heads(w_own_ref, w_other_ref, (0,), span), preferred_element_type=jnp.float32
         )
-    out_ref[...] = total.astype(jnp.bfloat16)
-
-
-def layer_attend(tick, frames, frames_ref, q_ref, own_ref, other_ref, *refs):
+    q_ref[...] = total.astype(jnp.bfloat16)
+
+
+def layer_attend(tick, frames, frames_ref, q_ref, both_ref, came_ref, *refs):
     out_ref, kv_out = refs[-2:]
     chips, halves, tokens, width = out_ref.shape
     slots = kv_out.shape[0]
@@ -197,6 +195,7 @@
     both = 2 * width
     slot = slot_of(frames_ref, tick)
     core = own_core()
+    own_ref, other_ref = both_ref.at[0], came_ref.at[1 - core]
     if tick == 0:
         for place_of, ref in enumerate((own_ref, other_ref)):
             columns = slice(place_of * both, (place_of + 1) * both)
@@ -240,11 +239,12 @@
             out_ref[chip, half] = attended[head]
 
 
-def layer_back(tick, frames, slot_rows, frames_ref, a_ref, w_own_ref, first_other_ref, x_ref, out_ref):
+def layer_back(tick, frames, slot_rows, frames_ref, a_ref, w_own_ref, first_came_ref, x_ref, out_ref):
     chips, halves, tokens, width = a_ref.shape
     pair = halves * width
     chip = lax.div(lax.axis_index("seq"), CORES)
     core = own_core()
+    first_other_ref = first_came_ref.at[1 - core]
     live = live_rows(frames, frames_ref, tick, tokens)
     stale_end, weight_end = first_rows(tokens, slot_rows, w_own_ref.shape[0])
     branch = jnp.zeros((tokens, pair), jnp.float32)
@@ -308,6 +308,7 @@
     rows = owned * chips
     blocks = chips * halves
     same_core = [[CORES * chip + core for chip in range(chips)] for core in range(CORES)]
+    same_chip = [[CORES * chip + core for core in range(CORES)] for chip in range(chips)]
     partner = [(device, device ^ 1) for device in range(group)]
 
     def swap(value):
@@ -352,16 +353,15 @@
             )
             gathered = call(arrange, "arrange", shape(*block_dims), (), (swap(sent),), [wide], aliases={0: 0})
         new_rows = rows if tick else first_rows(rows, stale.shape[0] // 2, width)[1]
-        normed, own = call(
+        queries, own = call(
             functools.partial(layer_keys, tick, frames),
             "keys",
-            (shape(rows, width), shape(new_rows, 2 * halves * HDIM)),
+            (shape(rows, halves * HDIM), shape(CORES, new_rows, 2 * halves * HDIM)),
             (patch_frames,),
             (gathered, norm_gain, w_in, w_in_other) + (() if tick else (stale, w_out)),
-            () if tick else [pltpu.VMEM(stale.shape, jnp.float32)],
-        )
-        other = lax.ppermute(own, "seq", partner)
-        queries = call(layer_queries, "queries", shape(rows, halves * HDIM), (), (normed, w_in, w_in_other))
+            [pltpu.VMEM((rows, width), jnp.bfloat16)] + ([] if tick else [pltpu.VMEM(stale.shape, jnp.float32)]),
+        )
+        other = lax.all_to_all(own, "seq", split_axis=0, concat_axis=0, tiled=True, axis_index_groups=same_chip)
         attended, kv = call(
             functools.partial(layer_attend, tick, frames),
             "attend",

time: 185 us -> 190 us (1.027)
  blocking collectives: 119 us -> 147 us
  starting transfers between devices: 28.7 us -> 9.34 us
  waiting for transfers between devices: 14.5 us -> 11.1 us
    all_to_all x0 -> x4, blocking collectives: none -> 27.8 us  [on_device(): lax.all_to_all(own, 'seq', split_axis=0, concat_axis=0, tiled=True, axis_...]
    ppermute x4 -> x0, starting transfers between devices: 19.4 us -> none  [on_device(): other = lax.ppermute(own, 'seq', partner)]
    ppermute x4 -> x0, waiting for transfers between devices: 3.43 us -> none  [on_device(): other = lax.ppermute(own, 'seq', partner)]
    pallas_call x26 -> x22, Pallas kernels: 20 us -> 19.8 us  [call(): pl.pallas_call(body, out_shape=out_shape, in_specs=[in_smem] * len(scalar...]
  transfers between devices with their start and end apart: 8 -> 4, of which waited for: 7 -> 3; matrix products, arithmetic and copies ran while one was open for 0% -> 0% of each run, Pallas kernels for 2% -> 1%
where the time goes in v9:
time: 190 us; the launch traced here: 187 us
  blocking collectives  147 us (77%)
  Pallas kernels  19.8 us (10%)
  waiting for transfers between devices  11.1 us (6%)
  starting transfers between devices  9.34 us (5%)
    all_to_all x9, blocking collectives, swap(): lax.all_to_all(value, 'seq', split_axis=0, concat_axis=0, tiled=True, axi...  119 us
    all_to_all x4, blocking collectives, on_device(): lax.all_to_all(own, 'seq', split_axis=0, concat_axis=0, tiled=True, axis_...  27.8 us
    pallas_call x22, Pallas kernels, call(): pl.pallas_call(body, out_shape=out_shape, in_specs=[in_smem] * len(scalar...  19.8 us
    ppermute x3, waiting for transfers between devices, on_device(): lax.ppermute(results[-1], 'section', [(source, source + 1) for source in...  11.1 us
    ppermute x3, starting transfers between devices, on_device(): lax.ppermute(results[-1], 'section', [(source, source + 1) for source in...  6.49 us
  transfers between devices with their start and end apart: 4, of which 3 were waited for; matrix products, arithmetic and copies ran while one was open for 0% of the time, Pallas kernels for 1%

profile of v9, /device:TPU:385, one launch (start us, length us, event | category | flops | bytes accessed | tf_op | source)
XLA Modules:
  0.0 187.1 jit_solution(10947977079167323536)
XLA Ops:
  0.0 0.0 copy-start
  0.0 0.0 copy-start.2
  0.0 0.0 copy-start.1
  0.0 2.8 %collective-permute-start = (bf16[3,4096,128]{2,1,0:T(8,128)(2,1)}, bf16[3,4096,128]{2,1,0:T(8,128)(2,1)S(1)}, u32[]{:S(2)}, u32[]{:S(2)}) collective-permute-start(bf16[3,4096,128]{2,1,0:T(8,128)(2,1)} %bitcast.6), channel_id=1, source_target_pairs={{0,1},{1,0},{2,3},{3,2},{4,5},{5,4},{6,7},{7,6},{8,9},{9,8},{10,11... | collective-permute-start | bytes 9437192 | tf_op jit(solution)/shard_map/ppermute | solution.py:320
  2.9 0.8 pack_first.1
  3.7 17.6 %all_to_all.65.came_ref = bf16[16,2,64,128]{3,2,1,0:T(8,128)(2,1)S(1)} all-to-all(bf16[16,2,64,128]{3,2,1,0:T(8,128)(2,1)S(1)} %pack_first.1), channel_id=1, replica_groups={{0,2,4,6,8,10,12,14,16,18,20,22,24,26,28,30},{1,3,5,7,9,11,13,15,17,19,..., dimensions={0} | all-to-all | bytes 1048576 | tf_op jit(solution)/shard_map/all_to_all | solution.py:315
  21.4 1.3 unpack_first.1
  22.6 0.0 collective-permute-done.w_other_ref
  22.7 0.0 copy-done
  22.7 0.0 copy-done.2
  22.7 0.0 copy-done.1
  22.7 2.2 %keys.4 = (bf16[64,256]{1,0:T(8,128)(2,1)S(1)}, bf16[2,1344,512]{2,1,0:T(8,128)(2,1)S(1)}) custom-call(s32[4]{0:T(128)S(1)} %copy-done.2, bf16[16,2,64,128]{3,2,1,0:T(8,128)(2,1)S(1)} %get-tuple-element.23.x_ref, bf16[1,4096]{1,0:T(2,128)(2,1)S(1)} %copy-done.1, bf16[3,4096,128]{2,1,0:T(8,128)(2,1)S(1)} %bitcast.7, ...), custom_call_target="tpu_custom_call" | custom-call | tf_op jit(solution)/shard_map/keys/pallas_call | solution.py:26
  24.8 7.0 %all_to_all.66.came_ref.first_came_ref = bf16[2,1344,512]{2,1,0:T(8,128)(2,1)S(1)} all-to-all(bf16[2,1344,512]{2,1,0:T(8,128)(2,1)S(1)} %get-tuple-element.27.both_ref), channel_id=1, replica_groups={{0,1},{2,3},{4,5},{6,7},{8,9},{10,11},{12,13},{14,15},{16,17},{18,19},{..., dimensions={0} | all-to-all | bytes 5505024 | tf_op jit(solution)/shard_map/all_to_all | solution.py:364
  31.8 1.0 attend.4
  32.8 13.3 %all_to_all.67.a_ref = bf16[16,2,64,128]{3,2,1,0:T(8,128)(2,1)S(1)} all-to-all(bf16[16,2,64,128]{3,2,1,0:T(8,128)(2,1)S(1)} %get-tuple-element.28), channel_id=1, replica_groups={{0,2,4,6,8,10,12,14,16,18,20,22,24,26,28,30},{1,3,5,7,9,11,13,15,17,19,..., dimensions={0} | all-to-all | bytes 1048576 | tf_op jit(solution)/shard_map/all_to_all | solution.py:315
  46.2 1.0 back.4.refs_0_
  47.2 2.6 %collective-permute-start.1 = (bf16[2,64,128]{2,1,0:T(8,128)(2,1)S(1)}, bf16[2,64,128]{2,1,0:T(8,128)(2,1)S(1)}, u32[]{:S(2)}, u32[]{:S(2)}) collective-permute-start(bf16[2,64,128]{2,1,0:T(8,128)(2,1)S(1)} %back.4.refs_0_), channel_id=1, source_target_pairs={{0,32},{32,64},{64,96},{96,128},{128,160},{160,192},{192,224},{224... | collective-permute-start | bytes 98312 | tf_op jit(solution)/shard_map/ppermute | solution.py:342
  49.9 3.2 %collective-permute-done.1.arrived_ref = bf16[2,64,128]{2,1,0:T(8,128)(2,1)S(1)} collective-permute-done((bf16[2,64,128]{2,1,0:T(8,128)(2,1)S(1)}, bf16[2,64,128]{2,1,0:T(8,128)(2,1)S(1)}, u32[]{:S(2)}, u32[]{:S(2)}) %collective-permute-start.1) | collective-permute-done | bytes 32800 | tf_op jit(solution)/shard_map/ppermute | solution.py:342
  53.1 0.1 spread.3
  53.2 12.5 %all_to_all.68.came_ref = bf16[16,2,64,128]{3,2,1,0:T(8,128)(2,1)S(1)} all-to-all(bf16[16,2,64,128]{3,2,1,0:T(8,128)(2,1)S(1)} %spread.3), channel_id=1, replica_groups={{0,2,4,6,8,10,12,14,16,18,20,22,24,26,28,30},{1,3,5,7,9,11,13,15,17,19,..., dimensions={0} | all-to-all | bytes 1048576 | tf_op jit(solution)/shard_map/all_to_all | solution.py:315
  65.7 1.9 %keys.5 = (bf16[64,256]{1,0:T(8,128)(2,1)S(1)}, bf16[2,64,512]{2,1,0:T(8,128)(2,1)S(1)}) custom-call(s32[4]{0:T(128)S(1)} %copy-done.2, bf16[16,2,64,128]{3,2,1,0:T(8,128)(2,1)S(1)} %arrange.3.x_ref, bf16[1,4096]{1,0:T(2,128)(2,1)S(1)} %copy-done.1, bf16[3,4096,128]{2,1,0:T(8,128)(2,1)S(1)} %bitcast.8, bf16[3,4096,128]{2,1,0:T(8,128)(2,1)S(1)} %collective-permute-done.w_other_ref), custom_call_target="tpu_custom_call" | custom-call | tf_op jit(solution)/shard_map/keys/pallas_call | solution.py:26
  67.6 7.0 %all_to_all.69.came_ref = bf16[2,64,512]{2,1,0:T(8,128)(2,1)S(1)} all-to-all(bf16[2,64,512]{2,1,0:T(8,128)(2,1)S(1)} %get-tuple-element.30.both_ref), channel_id=1, replica_groups={{0,1},{2,3},{4,5},{6,7},{8,9},{10,11},{12,13},{14,15},{16,17},{18,19},{..., dimensions={0} | all-to-all | bytes 262144 | tf_op jit(solution)/shard_map/all_to_all | solution.py:364
  74.5 1.0 attend.5
  75.5 13.5 %all_to_all.70.a_ref = bf16[16,2,64,128]{3,2,1,0:T(8,128)(2,1)S(1)} all-to-all(bf16[16,2,64,128]{3,2,1,0:T(8,128)(2,1)S(1)} %get-tuple-element.32), channel_id=1, replica_groups={{0,2,4,6,8,10,12,14,16,18,20,22,24,26,28,30},{1,3,5,7,9,11,13,15,17,19,..., dimensions={0} | all-to-all | bytes 1048576 | tf_op jit(solution)/shard_map/all_to_all | solution.py:315
  89.0 1.0 back.5.refs_1_
  90.0 1.9 %collective-permute-start.2 = (bf16[2,64,128]{2,1,0:T(8,128)(2,1)S(1)}, bf16[2,64,128]{2,1,0:T(8,128)(2,1)S(1)}, u32[]{:S(2)}, u32[]{:S(2)}) collective-permute-start(bf16[2,64,128]{2,1,0:T(8,128)(2,1)S(1)} %back.5.refs_1_), channel_id=1, source_target_pairs={{0,32},{32,64},{64,96},{96,128},{128,160},{160,192},{192,224},{224... | collective-permute-start | bytes 98312 | tf_op jit(solution)/shard_map/ppermute | solution.py:342
  92.0 3.9 %collective-permute-done.2.arrived_ref = bf16[2,64,128]{2,1,0:T(8,128)(2,1)S(1)} collective-permute-done((bf16[2,64,128]{2,1,0:T(8,128)(2,1)S(1)}, bf16[2,64,128]{2,1,0:T(8,128)(2,1)S(1)}, u32[]{:S(2)}, u32[]{:S(2)}) %collective-permute-start.2) | collective-permute-done | bytes 32800 | tf_op jit(solution)/shard_map/ppermute | solution.py:342
  95.9 0.1 spread.4
  96.0 12.5 %all_to_all.71.came_ref = bf16[16,2,64,128]{3,2,1,0:T(8,128)(2,1)S(1)} all-to-all(bf16[16,2,64,128]{3,2,1,0:T(8,128)(2,1)S(1)} %spread.4), channel_id=1, replica_groups={{0,2,4,6,8,10,12,14,16,18,20,22,24,26,28,30},{1,3,5,7,9,11,13,15,17,19,..., dimensions={0} | all-to-all | bytes 1048576 | tf_op jit(solution)/shard_map/all_to_all | solution.py:315
  108.5 1.9 %keys.6 = (bf16[64,256]{1,0:T(8,128)(2,1)S(1)}, bf16[2,64,512]{2,1,0:T(8,128)(2,1)S(1)}) custom-call(s32[4]{0:T(128)S(1)} %copy-done.2, bf16[16,2,64,128]{3,2,1,0:T(8,128)(2,1)S(1)} %arrange.4.x_ref, bf16[1,4096]{1,0:T(2,128)(2,1)S(1)} %copy-done.1, bf16[3,4096,128]{2,1,0:T(8,128)(2,1)S(1)} %bitcast.9, bf16[3,4096,128]{2,1,0:T(8,128)(2,1)S(1)} %collective-permute-done.w_other_ref), custom_call_target="tpu_custom_call" | custom-call | tf_op jit(solution)/shard_map/keys/pallas_call | solution.py:26
  110.4 6.9 %all_to_all.72.came_ref = bf16[2,64,512]{2,1,0:T(8,128)(2,1)S(1)} all-to-all(bf16[2,64,512]{2,1,0:T(8,128)(2,1)S(1)} %get-tuple-element.34.both_ref), channel_id=1, replica_groups={{0,1},{2,3},{4,5},{6,7},{8,9},{10,11},{12,13},{14,15},{16,17},{18,19},{..., dimensions={0} | all-to-all | bytes 262144 | tf_op jit(solution)/shard_map/all_to_all | solution.py:364
  117.3 1.0 attend.6
  118.3 13.5 %all_to_all.73.a_ref = bf16[16,2,64,128]{3,2,1,0:T(8,128)(2,1)S(1)} all-to-all(bf16[16,2,64,128]{3,2,1,0:T(8,128)(2,1)S(1)} %get-tuple-element.36), channel_id=1, replica_groups={{0,2,4,6,8,10,12,14,16,18,20,22,24,26,28,30},{1,3,5,7,9,11,13,15,17,19,..., dimensions={0} | all-to-all | bytes 1048576 | tf_op jit(solution)/shard_map/all_to_all | solution.py:315
  131.8 1.0 back.6.refs_2_
  132.8 1.9 %collective-permute-start.3 = (bf16[2,64,128]{2,1,0:T(8,128)(2,1)S(1)}, bf16[2,64,128]{2,1,0:T(8,128)(2,1)S(1)}, u32[]{:S(2)}, u32[]{:S(2)}) collective-permute-start(bf16[2,64,128]{2,1,0:T(8,128)(2,1)S(1)} %back.6.refs_2_), channel_id=1, source_target_pairs={{0,32},{32,64},{64,96},{96,128},{128,160},{160,192},{192,224},{224... | collective-permute-start | bytes 98312 | tf_op jit(solution)/shard_map/ppermute | solution.py:342
  134.8 3.9 %collective-permute-done.3.arrived_ref = bf16[2,64,128]{2,1,0:T(8,128)(2,1)S(1)} collective-permute-done((bf16[2,64,128]{2,1,0:T(8,128)(2,1)S(1)}, bf16[2,64,128]{2,1,0:T(8,128)(2,1)S(1)}, u32[]{:S(2)}, u32[]{:S(2)}) %collective-permute-start.3) | collective-permute-done | bytes 32800 | tf_op jit(solution)/shard_map/ppermute | solution.py:342
  138.7 0.1 spread.5
  138.8 12.5 %all_to_all.74.came_ref = bf16[16,2,64,128]{3,2,1,0:T(8,128)(2,1)S(1)} all-to-all(bf16[16,2,64,128]{3,2,1,0:T(8,128)(2,1)S(1)} %spread.5), channel_id=1, replica_groups={{0,2,4,6,8,10,12,14,16,18,20,22,24,26,28,30},{1,3,5,7,9,11,13,15,17,19,..., dimensions={0} | all-to-all | bytes 1048576 | tf_op jit(solution)/shard_map/all_to_all | solution.py:315
  151.3 1.9 %keys.7 = (bf16[64,256]{1,0:T(8,128)(2,1)S(1)}, bf16[2,64,512]{2,1,0:T(8,128)(2,1)S(1)}) custom-call(s32[4]{0:T(128)S(1)} %copy-done.2, bf16[16,2,64,128]{3,2,1,0:T(8,128)(2,1)S(1)} %arrange.5.x_ref, bf16[1,4096]{1,0:T(2,128)(2,1)S(1)} %copy-done.1, bf16[3,4096,128]{2,1,0:T(8,128)(2,1)S(1)} %bitcast.10, ...), custom_call_target="tpu_custom_call" | custom-call | tf_op jit(solution)/shard_map/keys/pallas_call | solution.py:26
  153.2 6.9 %all_to_all.75.came_ref = bf16[2,64,512]{2,1,0:T(8,128)(2,1)S(1)} all-to-all(bf16[2,64,512]{2,1,0:T(8,128)(2,1)S(1)} %get-tuple-element.38.both_ref), channel_id=1, replica_groups={{0,1},{2,3},{4,5},{6,7},{8,9},{10,11},{12,13},{14,15},{16,17},{18,19},{..., dimensions={0} | all-to-all | bytes 262144 | tf_op jit(solution)/shard_map/all_to_all | solution.py:364
  160.1 1.0 attend.7
  161.1 13.5 %all_to_all.76.a_ref = bf16[16,2,64,128]{3,2,1,0:T(8,128)(2,1)S(1)} all-to-all(bf16[16,2,64,128]{3,2,1,0:T(8,128)(2,1)S(1)} %get-tuple-element.40), channel_id=1, replica_groups={{0,2,4,6,8,10,12,14,16,18,20,22,24,26,28,30},{1,3,5,7,9,11,13,15,17,19,..., dimensions={0} | all-to-all | bytes 1048576 | tf_op jit(solution)/shard_map/all_to_all | solution.py:315
  174.6 1.0 back.7.refs_3_
  175.6 0.1 pack_last.1
  175.7 10.1 %all_to_all.77.came_ref = bf16[16,32,128]{2,1,0:T(8,128)(2,1)S(1)} all-to-all(bf16[16,32,128]{2,1,0:T(8,128)(2,1)S(1)} %pack_last.1), channel_id=1, replica_groups={{0,2,4,6,8,10,12,14,16,18,20,22,24,26,28,30},{1,3,5,7,9,11,13,15,17,19,..., dimensions={0} | all-to-all | bytes 262144 | tf_op jit(solution)/shard_map/all_to_all | solution.py:315
  185.9 1.3 unpack_last.1
  (3 shorter events, 0.0 us)
Async XLA Ops:
  0.0 22.7 %copy-start = (bf16[1,4096,3,128]{3,1,2,0:T(8,128)(2,1)S(1)}, bf16[1,4096,3,128]{3,1,2,0:T(8,128)(2,1)}, u32[]{:S(2)}) copy-start(bf16[1,4096,3,128]{3,1,2,0:T(8,128)(2,1)} %param.11) | copy-start | bytes 9437188
  0.0 22.7 %copy-start.2 = (s32[4]{0:T(128)S(1)}, s32[4]{0:T(128)}, u32[]{:S(2)}) copy-start(s32[4]{0:T(128)} %frames_ref.25) | copy-start | bytes 52
  0.0 22.7 %copy-start.1 = (bf16[1,4096]{1,0:T(2,128)(2,1)S(1)}, bf16[1,4096]{1,0:T(2,128)(2,1)}, u32[]{:S(2)}) copy-start(bf16[1,4096]{1,0:T(2,128)(2,1)} %gain_ref.7) | copy-start | bytes 24580
  0.0 22.6 %collective-permute-start = (bf16[3,4096,128]{2,1,0:T(8,128)(2,1)}, bf16[3,4096,128]{2,1,0:T(8,128)(2,1)S(1)}, u32[]{:S(2)}, u32[]{:S(2)}) collective-permute-start(bf16[3,4096,128]{2,1,0:T(8,128)(2,1)} %bitcast.6), channel_id=1, source_target_pairs={{0,1},{1,0},{2,3},{3,2},{4,5},{5,4},{6,7},{7,6},{8,9},{9,8},{10,11... | collective-permute-start | bytes 9437192 | tf_op jit(solution)/shard_map/ppermute | solution.py:320
  47.2 5.9 %collective-permute-start.1 = (bf16[2,64,128]{2,1,0:T(8,128)(2,1)S(1)}, bf16[2,64,128]{2,1,0:T(8,128)(2,1)S(1)}, u32[]{:S(2)}, u32[]{:S(2)}) collective-permute-start(bf16[2,64,128]{2,1,0:T(8,128)(2,1)S(1)} %back.4.refs_0_), channel_id=1, source_target_pairs={{0,32},{32,64},{64,96},{96,128},{128,160},{160,192},{192,224},{224... | collective-permute-start | bytes 98312 | tf_op jit(solution)/shard_map/ppermute | solution.py:342
  90.0 5.9 %collective-permute-start.2 = (bf16[2,64,128]{2,1,0:T(8,128)(2,1)S(1)}, bf16[2,64,128]{2,1,0:T(8,128)(2,1)S(1)}, u32[]{:S(2)}, u32[]{:S(2)}) collective-permute-start(bf16[2,64,128]{2,1,0:T(8,128)(2,1)S(1)} %back.5.refs_1_), channel_id=1, source_target_pairs={{0,32},{32,64},{64,96},{96,128},{128,160},{160,192},{192,224},{224... | collective-permute-start | bytes 98312 | tf_op jit(solution)/shard_map/ppermute | solution.py:342
  132.8 5.9 %collective-permute-start.3 = (bf16[2,64,128]{2,1,0:T(8,128)(2,1)S(1)}, bf16[2,64,128]{2,1,0:T(8,128)(2,1)S(1)}, u32[]{:S(2)}, u32[]{:S(2)}) collective-permute-start(bf16[2,64,128]{2,1,0:T(8,128)(2,1)S(1)} %back.6.refs_2_), channel_id=1, source_target_pairs={{0,32},{32,64},{64,96},{96,128},{128,160},{160,192},{192,224},{224... | collective-permute-start | bytes 98312 | tf_op jit(solution)/shard_map/ppermute | solution.py:342

commit v10 on v8

--- a/solution.py
+++ b/solution.py
@@ -81,62 +81,76 @@
             ].astype(jnp.bfloat16)
 
 
-def unpack_first(came_ref, weight_any, stale_any, hidden_ref, weight_ref, stale_ref, wide_ref, sem_ref):
+def spread(tick, entering_any, arrived_ref, out_ref, tokens_ref, rows_ref, sem_ref):
+    section = lax.axis_index("section")
+
+    @pl.when(section == 0)
+    def _():
+        fetch_rows(entering_any.at[tick - 1], tokens_ref, rows_ref, sem_ref)
+        send_rows(rows_ref, out_ref)
+
+    @pl.when(section != 0)
+    def _():
+        for chip in range(out_ref.shape[0]):
+            out_ref[chip] = arrived_ref[...]
+
+
+def arrange(came_ref, hidden_ref, wide_ref):
+    @pl.when(lax.axis_index("section") == 0)
+    def _():
+        to_blocks(came_ref, hidden_ref, wide_ref)
+
+
+def slot_of(frames_ref, tick):
+    slots = frames_ref.shape[0]
+    return lax.rem(tick + slots * MOST_SECTIONS - lax.axis_index("section"), slots)
+
+
+def own_core():
+    return lax.rem(lax.axis_index("seq"), CORES)
+
+
+def live_rows(frames, frames_ref, tick, rows):
+    row_ids = lax.broadcasted_iota(jnp.int32, (rows, 1), 0)
+    return row_ids < frames_ref[slot_of(frames_ref, tick)] * (rows // frames)
+
+
+def first_rows(tokens, slot_rows, width):
+    stale = tokens + slot_rows // CORES
+    return stale, stale + width // WEIGHT_PARTS
+
+
+def two_heads(own_ref, other_ref, kinds, span):
+    return jnp.concatenate([ref[kind, span] for ref in (own_ref, other_ref) for kind in kinds], axis=1)
+
+
+def layer_keys_first(
+    frames, frames_any, came_ref, gain_any, w_own_any, w_other_ref, weight_any, stale_any,
+    x_ref, w_own_ref, weight_ref, xn_ref, new_ref, stale_ref, wide_ref, frames_ref, gain_ref, sem_ref,
+):
+    firsts = [
+        pltpu.make_async_copy(frames_any, frames_ref, sem_ref.at[2]),
+        pltpu.make_async_copy(gain_any, gain_ref, sem_ref.at[3]),
+        pltpu.make_async_copy(w_own_any, w_own_ref, sem_ref.at[4]),
+    ]
+    for first in firsts:
+        first.start()
     fetches = [
         pltpu.make_async_copy(weight_any, weight_ref, sem_ref.at[0]),
         pltpu.make_async_copy(stale_any, stale_ref, sem_ref.at[1]),
     ]
     for fetch in fetches:
         fetch.start()
-    to_blocks(came_ref, hidden_ref, wide_ref)
-    for fetch in fetches:
-        fetch.wait()
-
-
-def spread(tick, entering_any, arrived_ref, out_ref, tokens_ref, rows_ref, sem_ref):
-    section = lax.axis_index("section")
-
-    @pl.when(section == 0)
-    def _():
-        fetch_rows(entering_any.at[tick - 1], tokens_ref, rows_ref, sem_ref)
-        send_rows(rows_ref, out_ref)
-
-    @pl.when(section != 0)
-    def _():
-        for chip in range(out_ref.shape[0]):
-            out_ref[chip] = arrived_ref[...]
-
-
-def arrange(came_ref, hidden_ref, wide_ref):
-    @pl.when(lax.axis_index("section") == 0)
-    def _():
-        to_blocks(came_ref, hidden_ref, wide_ref)
-
-
-def slot_of(frames_ref, tick):
-    slots = frames_ref.shape[0]
-    return lax.rem(tick + slots * MOST_SECTIONS - lax.axis_index("section"), slots)
-
-
-def own_core():
-    return lax.rem(lax.axis_index("seq"), CORES)
-
-
-def live_rows(frames, frames_ref, tick, rows):
-    row_ids = lax.broadcasted_iota(jnp.int32, (rows, 1), 0)
-    return row_ids < frames_ref[slot_of(frames_ref, tick)] * (rows // frames)
-
-
-def first_rows(tokens, slot_rows, width):
-    stale = tokens + slot_rows // CORES
-    return stale, stale + width // WEIGHT_PARTS
-
-
-def two_heads(own_ref, other_ref, kinds, span):
-    return jnp.concatenate([ref[kind, span] for ref in (own_ref, other_ref) for kind in kinds], axis=1)
-
-
-def layer_keys(tick, frames, frames_ref, x_ref, gain_ref, w_own_ref, w_other_ref, *refs):
+    to_blocks(came_ref, x_ref, wide_ref)
+    for first in firsts:
+        first.wait()
+    layer_keys(
+        0, frames, frames_ref, x_ref, gain_ref, w_own_ref, w_other_ref,
+        stale_ref, weight_ref, xn_ref, new_ref, wide_ref, fetches=fetches,
+    )
+
+
+def layer_keys(tick, frames, frames_ref, x_ref, gain_ref, w_own_ref, w_other_ref, *refs, fetches=()):
     *first_refs, xn_ref, new_ref = refs if tick else refs[:-1]
     chips, halves, tokens, width = x_ref.shape
     pair = halves * width
@@ -159,7 +173,9 @@
     new_ref[:tokens] = total.astype(jnp.bfloat16)
     if tick == 0:
         stale_ref, out_ref = first_refs
-        wide_ref = refs[-1]
+        wide_ref = refs[-1].at[:stale_ref.shape[0]]
+        for fetch in fetches:
+            fetch.wait()
         rows = stale_ref.shape[0] // 2
         stale_end, weight_end = first_rows(tokens, rows, out_ref.shape[0])
         wide_ref[...] = stale_ref[...].astype(jnp.float32)
@@ -326,15 +342,6 @@
     ]
     wide = pltpu.VMEM((chips * halves * rows, HDIM), jnp.float32)
     came = swap(call(pack_first, "pack_first", shape(*block_dims), (), (in_flight,), token_scratch, in_hbm=(0,)))
-    gathered, w_out, stale = call(
-        unpack_first,
-        "unpack_first",
-        (shape(*block_dims), shape(width, HDIM), shape(*stale.shape)),
-        (),
-        (came, out_weight[0], stale),
-        [wide, pltpu.SemaphoreType.DMA((2,))],
-        in_hbm=(1, 2),
-    )
     results = []
     for tick in range(ticks):
         if tick:
@@ -352,14 +359,36 @@
             )
             gathered = call(arrange, "arrange", shape(*block_dims), (), (swap(sent),), [wide], aliases={0: 0})
         new_rows = rows if tick else first_rows(rows, stale.shape[0] // 2, width)[1]
-        normed, own = call(
-            functools.partial(layer_keys, tick, frames),
-            "keys",
-            (shape(rows, width), shape(new_rows, 2 * halves * HDIM)),
-            (patch_frames,),
-            (gathered, norm_gain, w_in, w_in_other) + (() if tick else (stale, w_out)),
-            () if tick else [pltpu.VMEM(stale.shape, jnp.float32)],
-        )
+        if tick == 0:
+            gathered, w_in, w_out, normed, own = call(
+                functools.partial(layer_keys_first, frames),
+                "keys_first",
+                (
+                    shape(*block_dims),
+                    shape(*w_in.shape),
+                    shape(width, HDIM),
+                    shape(rows, width),
+                    shape(new_rows, 2 * halves * HDIM),
+                ),
+                (),
+                (patch_frames, came, norm_gain, w_in, w_in_other, out_weight[0], stale),
+                [
+                    pltpu.VMEM(stale.shape, jnp.bfloat16),
+                    wide,
+                    pltpu.SMEM(patch_frames.shape, jnp.int32),
+                    pltpu.VMEM(norm_gain.shape, jnp.bfloat16),
+                    pltpu.SemaphoreType.DMA((5,)),
+                ],
+                in_hbm=(0, 2, 3, 5, 6),
+            )
+        else:
+            normed, own = call(
+                functools.partial(layer_keys, tick, frames),
+                "keys",
+                (shape(rows, width), shape(new_rows, 2 * halves * HDIM)),
+                (patch_frames,),
+                (gathered, norm_gain, w_in, w_in_other),
+            )
         other = lax.ppermute(own, "seq", partner)
         queries = call(layer_queries, "queries", shape(rows, halves * HDIM), (), (normed, w_in, w_in_other))
         attended, kv = call(

time: 185 us -> 185 us (level)
  the two profiles are of different devices: /device:TPU:385 before, /device:TPU:256 now
where the time goes in v10:
time: 185 us; the launch traced here: 184 us
  blocking collectives  128 us (69%)
  Pallas kernels  20.3 us (11%)
  waiting for transfers between devices  19 us (10%)
  starting transfers between devices  16.4 us (9%)
    all_to_all x9, blocking collectives, swap(): lax.all_to_all(value, 'seq', split_axis=0, concat_axis=0, tiled=True, axi...  128 us
    pallas_call x25, Pallas kernels, call(): pl.pallas_call(body, out_shape=out_shape, in_specs=[in_smem] * len(scalar...  20.3 us
    ppermute x3, waiting for transfers between devices, on_device(): lax.ppermute(results[-1], 'section', [(source, source + 1) for source in...  14.3 us
    ppermute x4, starting transfers between devices, on_device(): other = lax.ppermute(own, 'seq', partner)  7.68 us
    ppermute x3, starting transfers between devices, on_device(): lax.ppermute(results[-1], 'section', [(source, source + 1) for source in...  6.76 us
    ppermute x4, waiting for transfers between devices, on_device(): other = lax.ppermute(own, 'seq', partner)  4.76 us
  transfers between devices with their start and end apart: 8, of which 7 were waited for; matrix products, arithmetic and copies ran while one was open for 0% of the time, Pallas kernels for 2%

profile of v10, /device:TPU:256, one launch (start us, length us, event | category | flops | bytes accessed | tf_op | source)
XLA Modules:
  0.0 184.3 jit_solution(15494076848488984118)
XLA Ops:
  0.0 1.9 %collective-permute-start = (bf16[3,4096,128]{2,1,0:T(8,128)(2,1)}, bf16[3,4096,128]{2,1,0:T(8,128)(2,1)S(1)}, u32[]{:S(2)}, u32[]{:S(2)}) collective-permute-start(bf16[3,4096,128]{2,1,0:T(8,128)(2,1)} %bitcast.6), channel_id=1, source_target_pairs={{0,1},{1,0},{2,3},{3,2},{4,5},{5,4},{6,7},{7,6},{8,9},{9,8},{10,11... | collective-permute-start | bytes 9437192 | tf_op jit(solution)/shard_map/ppermute | solution.py:335
  1.9 0.8 pack_first.1
  2.8 19.0 %all_to_all.45.came_ref = bf16[16,2,64,128]{3,2,1,0:T(8,128)(2,1)S(1)} all-to-all(bf16[16,2,64,128]{3,2,1,0:T(8,128)(2,1)S(1)} %pack_first.1), channel_id=1, replica_groups={{0,2,4,6,8,10,12,14,16,18,20,22,24,26,28,30},{1,3,5,7,9,11,13,15,17,19,..., dimensions={0} | all-to-all | bytes 1048576 | tf_op jit(solution)/shard_map/all_to_all | solution.py:330
  21.8 0.0 collective-permute-done.w_other_ref
  21.8 3.2 %keys_first.1 = (bf16[16,2,64,128]{3,2,1,0:T(8,128)(2,1)S(1)}, bf16[3,4096,128]{2,1,0:T(8,128)(2,1)S(1)}, bf16[4096,128]{1,0:T(8,128)(2,1)S(1)}, bf16[64,4096]{1,0:T(8,128)(2,1)S(1)}, bf16[1344,512]{1,0:T(8,128)(2,1)S(1)}) custom-call(s32[4]{0:T(128)} %frames_ref.23, bf16[16,2,64,128]{3,2,1,0:T(8,128)(2,1)S(1)} %all_to_all.45.came_ref, ...), custom_call_target="tpu_custom_call" | custom-call | tf_op jit(solution)/shard_map/keys_first/pallas_call | solution.py:26
  25.0 1.9 %collective-permute-start.1 = (bf16[1344,512]{1,0:T(8,128)(2,1)S(1)}, bf16[1344,512]{1,0:T(8,128)(2,1)S(1)}, u32[]{:S(2)}, u32[]{:S(2)}) collective-permute-start(bf16[1344,512]{1,0:T(8,128)(2,1)S(1)} %get-tuple-element.25.own_ref), channel_id=1, source_target_pairs={{0,1},{1,0},{2,3},{3,2},{4,5},{5,4},{6,7},{7,6},{8,9},{9,8},{10,11... | collective-permute-start | bytes 4128776 | tf_op jit(solution)/shard_map/ppermute | solution.py:392
  26.9 0.0 copy-start.1
  27.0 0.5 queries.4.q_ref
  27.5 2.6 %collective-permute-done.1.other_ref.first_other_ref = bf16[1344,512]{1,0:T(8,128)(2,1)S(1)} collective-permute-done((bf16[1344,512]{1,0:T(8,128)(2,1)S(1)}, bf16[1344,512]{1,0:T(8,128)(2,1)S(1)}, u32[]{:S(2)}, u32[]{:S(2)}) %collective-permute-start.1) | collective-permute-done | bytes 1376288 | tf_op jit(solution)/shard_map/ppermute | solution.py:392
  30.0 1.0 attend.4
  31.1 14.7 %all_to_all.46.a_ref = bf16[16,2,64,128]{3,2,1,0:T(8,128)(2,1)S(1)} all-to-all(bf16[16,2,64,128]{3,2,1,0:T(8,128)(2,1)S(1)} %get-tuple-element.26), channel_id=1, replica_groups={{0,2,4,6,8,10,12,14,16,18,20,22,24,26,28,30},{1,3,5,7,9,11,13,15,17,19,..., dimensions={0} | all-to-all | bytes 1048576 | tf_op jit(solution)/shard_map/all_to_all | solution.py:330
  45.8 1.0 back.4.refs_0_
  46.8 2.9 %collective-permute-start.2 = (bf16[2,64,128]{2,1,0:T(8,128)(2,1)S(1)}, bf16[2,64,128]{2,1,0:T(8,128)(2,1)S(1)}, u32[]{:S(2)}, u32[]{:S(2)}) collective-permute-start(bf16[2,64,128]{2,1,0:T(8,128)(2,1)S(1)} %back.4.refs_0_), channel_id=1, source_target_pairs={{0,32},{32,64},{64,96},{96,128},{128,160},{160,192},{192,224},{224... | collective-permute-start | bytes 98312 | tf_op jit(solution)/shard_map/ppermute | solution.py:348
  49.8 4.1 %collective-permute-done.2.arrived_ref = bf16[2,64,128]{2,1,0:T(8,128)(2,1)S(1)} collective-permute-done((bf16[2,64,128]{2,1,0:T(8,128)(2,1)S(1)}, bf16[2,64,128]{2,1,0:T(8,128)(2,1)S(1)}, u32[]{:S(2)}, u32[]{:S(2)}) %collective-permute-start.2) | collective-permute-done | bytes 32800 | tf_op jit(solution)/shard_map/ppermute | solution.py:348
  53.9 0.1 spread.3
  53.9 13.0 %all_to_all.47.came_ref = bf16[16,2,64,128]{3,2,1,0:T(8,128)(2,1)S(1)} all-to-all(bf16[16,2,64,128]{3,2,1,0:T(8,128)(2,1)S(1)} %spread.3), channel_id=1, replica_groups={{0,2,4,6,8,10,12,14,16,18,20,22,24,26,28,30},{1,3,5,7,9,11,13,15,17,19,..., dimensions={0} | all-to-all | bytes 1048576 | tf_op jit(solution)/shard_map/all_to_all | solution.py:330
  67.0 1.5 keys.3
  68.5 1.9 %collective-permute-start.3 = (bf16[64,512]{1,0:T(8,128)(2,1)S(1)}, bf16[64,512]{1,0:T(8,128)(2,1)S(1)}, u32[]{:S(2)}, u32[]{:S(2)}) collective-permute-start(bf16[64,512]{1,0:T(8,128)(2,1)S(1)} %get-tuple-element.30.own_ref), channel_id=1, source_target_pairs={{0,1},{1,0},{2,3},{3,2},{4,5},{5,4},{6,7},{7,6},{8,9},{9,8},{10,11... | collective-permute-start | bytes 196616 | tf_op jit(solution)/shard_map/ppermute | solution.py:392
  70.4 0.5 queries.5.q_ref
  70.9 0.7 collective-permute-done.3.other_ref
  71.7 1.0 attend.5
  72.7 14.9 %all_to_all.48.a_ref = bf16[16,2,64,128]{3,2,1,0:T(8,128)(2,1)S(1)} all-to-all(bf16[16,2,64,128]{3,2,1,0:T(8,128)(2,1)S(1)} %get-tuple-element.32), channel_id=1, replica_groups={{0,2,4,6,8,10,12,14,16,18,20,22,24,26,28,30},{1,3,5,7,9,11,13,15,17,19,..., dimensions={0} | all-to-all | bytes 1048576 | tf_op jit(solution)/shard_map/all_to_all | solution.py:330
  87.5 1.0 back.5.refs_1_
  88.5 1.9 %collective-permute-start.4 = (bf16[2,64,128]{2,1,0:T(8,128)(2,1)S(1)}, bf16[2,64,128]{2,1,0:T(8,128)(2,1)S(1)}, u32[]{:S(2)}, u32[]{:S(2)}) collective-permute-start(bf16[2,64,128]{2,1,0:T(8,128)(2,1)S(1)} %back.5.refs_1_), channel_id=1, source_target_pairs={{0,32},{32,64},{64,96},{96,128},{128,160},{160,192},{192,224},{224... | collective-permute-start | bytes 98312 | tf_op jit(solution)/shard_map/ppermute | solution.py:348
  90.5 5.1 %collective-permute-done.4.arrived_ref = bf16[2,64,128]{2,1,0:T(8,128)(2,1)S(1)} collective-permute-done((bf16[2,64,128]{2,1,0:T(8,128)(2,1)S(1)}, bf16[2,64,128]{2,1,0:T(8,128)(2,1)S(1)}, u32[]{:S(2)}, u32[]{:S(2)}) %collective-permute-start.4) | collective-permute-done | bytes 32800 | tf_op jit(solution)/shard_map/ppermute | solution.py:348
  95.6 0.1 spread.4
  95.6 13.0 %all_to_all.49.came_ref = bf16[16,2,64,128]{3,2,1,0:T(8,128)(2,1)S(1)} all-to-all(bf16[16,2,64,128]{3,2,1,0:T(8,128)(2,1)S(1)} %spread.4), channel_id=1, replica_groups={{0,2,4,6,8,10,12,14,16,18,20,22,24,26,28,30},{1,3,5,7,9,11,13,15,17,19,..., dimensions={0} | all-to-all | bytes 1048576 | tf_op jit(solution)/shard_map/all_to_all | solution.py:330
  108.7 1.5 keys.4
  110.2 1.9 %collective-permute-start.5 = (bf16[64,512]{1,0:T(8,128)(2,1)S(1)}, bf16[64,512]{1,0:T(8,128)(2,1)S(1)}, u32[]{:S(2)}, u32[]{:S(2)}) collective-permute-start(bf16[64,512]{1,0:T(8,128)(2,1)S(1)} %get-tuple-element.34.own_ref), channel_id=1, source_target_pairs={{0,1},{1,0},{2,3},{3,2},{4,5},{5,4},{6,7},{7,6},{8,9},{9,8},{10,11... | collective-permute-start | bytes 196616 | tf_op jit(solution)/shard_map/ppermute | solution.py:392
  112.2 0.5 queries.6.q_ref
  112.6 0.7 collective-permute-done.5.other_ref
  113.4 1.0 attend.6
  114.4 14.8 %all_to_all.50.a_ref = bf16[16,2,64,128]{3,2,1,0:T(8,128)(2,1)S(1)} all-to-all(bf16[16,2,64,128]{3,2,1,0:T(8,128)(2,1)S(1)} %get-tuple-element.36), channel_id=1, replica_groups={{0,2,4,6,8,10,12,14,16,18,20,22,24,26,28,30},{1,3,5,7,9,11,13,15,17,19,..., dimensions={0} | all-to-all | bytes 1048576 | tf_op jit(solution)/shard_map/all_to_all | solution.py:330
  129.2 1.0 back.6.refs_2_
  130.3 1.9 %collective-permute-start.6 = (bf16[2,64,128]{2,1,0:T(8,128)(2,1)S(1)}, bf16[2,64,128]{2,1,0:T(8,128)(2,1)S(1)}, u32[]{:S(2)}, u32[]{:S(2)}) collective-permute-start(bf16[2,64,128]{2,1,0:T(8,128)(2,1)S(1)} %back.6.refs_2_), channel_id=1, source_target_pairs={{0,32},{32,64},{64,96},{96,128},{128,160},{160,192},{192,224},{224... | collective-permute-start | bytes 98312 | tf_op jit(solution)/shard_map/ppermute | solution.py:348
  132.2 5.1 %collective-permute-done.6.arrived_ref = bf16[2,64,128]{2,1,0:T(8,128)(2,1)S(1)} collective-permute-done((bf16[2,64,128]{2,1,0:T(8,128)(2,1)S(1)}, bf16[2,64,128]{2,1,0:T(8,128)(2,1)S(1)}, u32[]{:S(2)}, u32[]{:S(2)}) %collective-permute-start.6) | collective-permute-done | bytes 32800 | tf_op jit(solution)/shard_map/ppermute | solution.py:348
  137.3 0.1 spread.5
  137.4 13.0 %all_to_all.51.came_ref = bf16[16,2,64,128]{3,2,1,0:T(8,128)(2,1)S(1)} all-to-all(bf16[16,2,64,128]{3,2,1,0:T(8,128)(2,1)S(1)} %spread.5), channel_id=1, replica_groups={{0,2,4,6,8,10,12,14,16,18,20,22,24,26,28,30},{1,3,5,7,9,11,13,15,17,19,..., dimensions={0} | all-to-all | bytes 1048576 | tf_op jit(solution)/shard_map/all_to_all | solution.py:330
  150.4 1.5 keys.5
  151.9 1.9 %collective-permute-start.7 = (bf16[64,512]{1,0:T(8,128)(2,1)S(1)}, bf16[64,512]{1,0:T(8,128)(2,1)S(1)}, u32[]{:S(2)}, u32[]{:S(2)}) collective-permute-start(bf16[64,512]{1,0:T(8,128)(2,1)S(1)} %get-tuple-element.38.own_ref), channel_id=1, source_target_pairs={{0,1},{1,0},{2,3},{3,2},{4,5},{5,4},{6,7},{7,6},{8,9},{9,8},{10,11... | collective-permute-start | bytes 196616 | tf_op jit(solution)/shard_map/ppermute | solution.py:392
  153.9 0.5 queries.7.q_ref
  154.4 0.7 collective-permute-done.7.other_ref
  155.1 1.0 attend.7
  156.1 14.9 %all_to_all.52.a_ref = bf16[16,2,64,128]{3,2,1,0:T(8,128)(2,1)S(1)} all-to-all(bf16[16,2,64,128]{3,2,1,0:T(8,128)(2,1)S(1)} %get-tuple-element.40), channel_id=1, replica_groups={{0,2,4,6,8,10,12,14,16,18,20,22,24,26,28,30},{1,3,5,7,9,11,13,15,17,19,..., dimensions={0} | all-to-all | bytes 1048576 | tf_op jit(solution)/shard_map/all_to_all | solution.py:330
  170.9 1.0 back.7.refs_3_
  172.0 0.1 pack_last.1
  172.1 10.9 %all_to_all.53.came_ref = bf16[16,32,128]{2,1,0:T(8,128)(2,1)S(1)} all-to-all(bf16[16,32,128]{2,1,0:T(8,128)(2,1)S(1)} %pack_last.1), channel_id=1, replica_groups={{0,2,4,6,8,10,12,14,16,18,20,22,24,26,28,30},{1,3,5,7,9,11,13,15,17,19,..., dimensions={0} | all-to-all | bytes 262144 | tf_op jit(solution)/shard_map/all_to_all | solution.py:330
  183.0 1.3 unpack_last.1
  (6 shorter events, 0.0 us)
Async XLA Ops:
  0.0 21.8 %collective-permute-start = (bf16[3,4096,128]{2,1,0:T(8,128)(2,1)}, bf16[3,4096,128]{2,1,0:T(8,128)(2,1)S(1)}, u32[]{:S(2)}, u32[]{:S(2)}) collective-permute-start(bf16[3,4096,128]{2,1,0:T(8,128)(2,1)} %bitcast.6), channel_id=1, source_target_pairs={{0,1},{1,0},{2,3},{3,2},{4,5},{5,4},{6,7},{7,6},{8,9},{9,8},{10,11... | collective-permute-start | bytes 9437192 | tf_op jit(solution)/shard_map/ppermute | solution.py:335
  25.0 5.0 %collective-permute-start.1 = (bf16[1344,512]{1,0:T(8,128)(2,1)S(1)}, bf16[1344,512]{1,0:T(8,128)(2,1)S(1)}, u32[]{:S(2)}, u32[]{:S(2)}) collective-permute-start(bf16[1344,512]{1,0:T(8,128)(2,1)S(1)} %get-tuple-element.25.own_ref), channel_id=1, source_target_pairs={{0,1},{1,0},{2,3},{3,2},{4,5},{5,4},{6,7},{7,6},{8,9},{9,8},{10,11... | collective-permute-start | bytes 4128776 | tf_op jit(solution)/shard_map/ppermute | solution.py:392
  26.9 3.1 %copy-start.1 = (s32[4]{0:T(128)S(1)}, s32[4]{0:T(128)}, u32[]{:S(2)}) copy-start(s32[4]{0:T(128)} %frames_ref.23) | copy-start | bytes 52
  45.8 21.2 %copy-start = (bf16[1,4096]{1,0:T(2,128)(2,1)S(1)}, bf16[1,4096]{1,0:T(2,128)(2,1)}, u32[]{:S(2)}) copy-start(bf16[1,4096]{1,0:T(2,128)(2,1)} %gain_ref.5) | copy-start | bytes 24580
  46.8 7.0 %collective-permute-start.2 = (bf16[2,64,128]{2,1,0:T(8,128)(2,1)S(1)}, bf16[2,64,128]{2,1,0:T(8,128)(2,1)S(1)}, u32[]{:S(2)}, u32[]{:S(2)}) collective-permute-start(bf16[2,64,128]{2,1,0:T(8,128)(2,1)S(1)} %back.4.refs_0_), channel_id=1, source_target_pairs={{0,32},{32,64},{64,96},{96,128},{128,160},{160,192},{192,224},{224... | collective-permute-start | bytes 98312 | tf_op jit(solution)/shard_map/ppermute | solution.py:348
  68.5 3.1 %collective-permute-start.3 = (bf16[64,512]{1,0:T(8,128)(2,1)S(1)}, bf16[64,512]{1,0:T(8,128)(2,1)S(1)}, u32[]{:S(2)}, u32[]{:S(2)}) collective-permute-start(bf16[64,512]{1,0:T(8,128)(2,1)S(1)} %get-tuple-element.30.own_ref), channel_id=1, source_target_pairs={{0,1},{1,0},{2,3},{3,2},{4,5},{5,4},{6,7},{7,6},{8,9},{9,8},{10,11... | collective-permute-start | bytes 196616 | tf_op jit(solution)/shard_map/ppermute | solution.py:392
  88.5 7.0 %collective-permute-start.4 = (bf16[2,64,128]{2,1,0:T(8,128)(2,1)S(1)}, bf16[2,64,128]{2,1,0:T(8,128)(2,1)S(1)}, u32[]{:S(2)}, u32[]{:S(2)}) collective-permute-start(bf16[2,64,128]{2,1,0:T(8,128)(2,1)S(1)} %back.5.refs_1_), channel_id=1, source_target_pairs={{0,32},{32,64},{64,96},{96,128},{128,160},{160,192},{192,224},{224... | collective-permute-start | bytes 98312 | tf_op jit(solution)/shard_map/ppermute | solution.py:348
  110.2 3.1 %collective-permute-start.5 = (bf16[64,512]{1,0:T(8,128)(2,1)S(1)}, bf16[64,512]{1,0:T(8,128)(2,1)S(1)}, u32[]{:S(2)}, u32[]{:S(2)}) collective-permute-start(bf16[64,512]{1,0:T(8,128)(2,1)S(1)} %get-tuple-element.34.own_ref), channel_id=1, source_target_pairs={{0,1},{1,0},{2,3},{3,2},{4,5},{5,4},{6,7},{7,6},{8,9},{9,8},{10,11... | collective-permute-start | bytes 196616 | tf_op jit(solution)/shard_map/ppermute | solution.py:392
  130.3 7.0 %collective-permute-start.6 = (bf16[2,64,128]{2,1,0:T(8,128)(2,1)S(1)}, bf16[2,64,128]{2,1,0:T(8,128)(2,1)S(1)}, u32[]{:S(2)}, u32[]{:S(2)}) collective-permute-start(bf16[2,64,128]{2,1,0:T(8,128)(2,1)S(1)} %back.6.refs_2_), channel_id=1, source_target_pairs={{0,32},{32,64},{64,96},{96,128},{128,160},{160,192},{192,224},{224... | collective-permute-start | bytes 98312 | tf_op jit(solution)/shard_map/ppermute | solution.py:348
  151.9 3.1 %collective-permute-start.7 = (bf16[64,512]{1,0:T(8,128)(2,1)S(1)}, bf16[64,512]{1,0:T(8,128)(2,1)S(1)}, u32[]{:S(2)}, u32[]{:S(2)}) collective-permute-start(bf16[64,512]{1,0:T(8,128)(2,1)S(1)} %get-tuple-element.38.own_ref), channel_id=1, source_target_pairs={{0,1},{1,0},{2,3},{3,2},{4,5},{5,4},{6,7},{7,6},{8,9},{9,8},{10,11... | collective-permute-start | bytes 196616 | tf_op jit(solution)/shard_map/ppermute | solution.py:392
